TPU v7x, 128 devices: a whole 4x4x4 slice. The times are simulated.
128 devices in a mesh: expert: 32 (over y, z, core), shard: 4 (over x).
Axes of the slice: x: 4, y: 4, z: 4, core: 2. Of those that a mesh axis runs over, the one named last changes fastest.
Arguments:
- tokens: bfloat16 [16384, 768], P(('expert', 'shard')), may hold values from -6 to 6
- seq_lengths: int32 [128, 4], P(('expert', 'shard')), may hold values from 1 to 96, 128 in all within a row
- routes: int32 [16384, 2], P(('expert', 'shard')), may hold values from 0 to 63, all different within a row; in each aligned block of 128 rows (0 to 127, 128 to 255, ...) at most 6 rows name the same one
- gain_attn: bfloat16 [768], P('shard'), may hold values from 0.25 to 1.75
- w_query: bfloat16 [768, 768], P('shard'), may hold values from -0.21875 to 0.21875
- w_key: bfloat16 [768, 768], P('shard'), may hold values from -0.21875 to 0.21875
- w_value: bfloat16 [768, 768], P('shard'), may hold values from -0.21875 to 0.21875
- w_output: bfloat16 [768, 768], P('shard'), may hold values from -0.875 to 0.875
- rel_bias: bfloat16 [12, 32], P('shard'), may hold values from -3 to 3
- gain_moe: bfloat16 [768], P('shard'), may hold values from 0.25 to 1.75
- w_router: bfloat16 [768, 64], P('shard'), may hold values from -0.21875 to 0.21875
- w_in: bfloat16 [64, 768, 3072], P('expert', None, 'shard'), may hold values from -0.21875 to 0.21875
- w_out: bfloat16 [64, 3072, 768], P('expert', 'shard'), may hold values from -0.109375 to 0.109375
- cotangent: bfloat16 [16384, 768], P(('expert', 'shard')), may hold values from -6 to 6
Outputs:
- result: bfloat16 [16384, 768], P(('expert', 'shard'))
- grad_tokens: float32 [16384, 768], P(('expert', 'shard'))
- grad_gain_attn: float32 [768], P('shard')
- grad_w_query: float32 [768, 768], P('shard')
- grad_w_key: float32 [768, 768], P('shard')
- grad_w_value: float32 [768, 768], P('shard')
- grad_w_output: float32 [768, 768], P('shard')
- grad_rel_bias: float32 [12, 32], P('shard')
- grad_gain_moe: float32 [768], P('shard')
- grad_w_router: float32 [768, 64], P('shard')
- grad_w_in: float32 [64, 768, 3072], P('expert', None, 'shard')
- grad_w_out: float32 [64, 3072, 768], P('expert', 'shard')
Inputs may be any that keep to these rules, and one draw needn't show every extreme that they name: `seq_lengths`: each rank's 4 lengths sum to 128; its sequences lie one after another in its rows; the largest length is exactly 96. `routes`: each row names two different experts. Among the rows of one rank no expert is named more than 6 times, a bound that some block reaches.
All inputs are finite; a program needn't handle non-finite values.
Results may differ from a plain program's by a relative error of at most 0.025.
Values may be sent and summed in bfloat16 or wider, within the bound.
No kernel may reach another device: no remote copies, remote signals or barrier semaphores. Data moves between devices by JAX's collectives and lax.ppermute only.
A program may use at most 128 MiB of HBM per device.

v0:
```python
import functools
import math

import jax
import jax.numpy as jnp
from jax import lax
from jax.experimental import pallas as pl
from jax.experimental.pallas import tpu as pltpu
from jax.sharding import Mesh, PartitionSpec as P

epsilon = 1e-06
bucket_edges = list(range(1, 17)) + [
    int(math.ceil(16.0 * 8.0 ** ((bucket_level - 16) / 16.0))) for bucket_level in range(17, 32)
]


def row_segments(lengths, row_count):
    sequence_ends = jnp.cumsum(lengths)
    positions = jnp.arange(row_count, dtype=jnp.int32)
    return jnp.sum((positions[:, None] >= sequence_ends[None, :]).astype(jnp.int32), axis=1)


def position_tables(row_count, bucket_count):
    positions = jnp.arange(row_count, dtype=jnp.int32)
    distance = positions[:, None] - positions[None, :]
    edge_values = jnp.array(bucket_edges, dtype=jnp.int32)
    bucket = jnp.sum((distance[:, :, None] >= edge_values).astype(jnp.int32), axis=2)
    onehot = (bucket[:, :, None] == jnp.arange(bucket_count, dtype=jnp.int32)).astype(jnp.bfloat16)
    return (distance, onehot)


def shift_x(block, step):
    ranks = lax.axis_size("x")
    return lax.ppermute(block, "x", [(i, (i + step) % ranks) for i in range(ranks)])


def swap_core(block):
    return lax.ppermute(block, "c", [(0, 1), (1, 0)])


def along_x(block):
    return [block, shift_x(block, 1), shift_x(block, 2), shift_x(block, 3)]


def head_kernel(core_ref, routes_ref, one_ref, two_ref, bias_ref, router_ref, cotangent_ref, *refs):
    mats, line_ref, qkv_ref, out_ref, held, sems = refs[:4], *refs[4:9]
    f32 = jnp.float32
    tokens = cotangent_ref.shape[0]
    half = mats[0].shape[0] // 2
    start = pl.multiple_of(core_ref[0] * half, half)
    spots = [qkv_ref.at[pl.ds(k * half, half)] for k in range(3)] + [out_ref]
    copies = start_copies(
        [(cotangent_ref, line_ref.at[pl.ds(0, tokens)])]
        + [(m.at[pl.ds(start, half)], spot) for m, spot in zip(mats, spots)],
        sems,
    )
    held[...] = jnp.zeros_like(held)
    held[0:1, : one_ref.shape[1]] = one_ref[...].astype(f32)
    held[1:2, : two_ref.shape[1]] = two_ref[...].astype(f32)
    held[2:5, : bias_ref.shape[1]] = bias_ref[...].astype(f32)
    held[5:7, :tokens] = routes_ref[...].astype(f32)
    experts_all = router_ref.shape[1]
    for b in range(router_ref.shape[0] // 16):
        part = router_ref[16 * b : 16 * b + 16, :].astype(f32)
        held[16:32, experts_all * b : experts_all * (b + 1)] = part
    line_ref[tokens:, :] = held[...].astype(jnp.bfloat16)
    for c in copies:
        c.wait()


def start_copies(pairs, sems):
    copies = [pltpu.make_async_copy(s, d, sems.at[i]) for i, (s, d) in enumerate(pairs)]
    for c in copies:
        c.start()
    return copies


def block_copies(shard, core, mats, near, far, outs):
    rows = mats[0].shape[0]
    half = rows // 2
    pairs = []
    for k, (mat, out) in enumerate(zip(mats, outs)):
        begin = pl.multiple_of(shard * rows, rows)
        pairs.append((mat, out.at[pl.ds(begin, rows)]))
        part = pl.ds(k * half, half)
        for r in range(1, 4):
            begin = lax.rem(shard + (4 - r), 4) * rows
            mine = pl.multiple_of(begin + core * half, half)
            other = pl.multiple_of(begin + (1 - core) * half, half)
            pairs.append((near[r - 1].at[part], out.at[pl.ds(mine, half)]))
            pairs.append((far[r - 1].at[part], out.at[pl.ds(other, half)]))
    return pairs


def norm_scale(x):
    return lax.rsqrt(jnp.mean(x * x, axis=1, keepdims=True) + epsilon)


def head_half(block, side):
    lanes = lax.broadcasted_iota(jnp.int32, block.shape, 1)
    keep = (lanes < 64) if side == 0 else (lanes >= 64)
    return jnp.where(keep, block, jnp.zeros_like(block))


def to_column(row):
    n = row.shape[1]
    down = lax.broadcasted_iota(jnp.int32, (n, n), 0)
    across = lax.broadcasted_iota(jnp.int32, (n, n), 1)
    return jnp.sum(jnp.where(down == across, row, jnp.zeros_like(row)), axis=1, keepdims=True)


LAST = (((1,), (1,)), ((), ()))
FIRST = (((0,), (0,)), ((), ()))


def attend_kernel(place_ref, tokens_ref, gain_ref, bias_ref, *refs):
    f32, bf16 = jnp.float32, jnp.bfloat16
    mats, near, far = refs[:3], refs[3:6], refs[6:9]
    weights = refs[10:13]
    hidden_ref, q_ref, k_ref, v_ref, probs_ref, attended_ref, sems = refs[13:20]
    copies = start_copies(
        block_copies(place_ref[0], place_ref[1], mats, near, far, weights), sems
    )
    x = tokens_ref[...].astype(f32)
    hidden = (x * norm_scale(x) * gain_ref[...].astype(f32)).astype(bf16)
    hidden_ref[...] = hidden
    for n, (w, out) in enumerate(zip(weights, (q_ref, k_ref, v_ref))):
        for c in copies[7 * n : 7 * n + 7]:
            c.wait()
        out[...] = jnp.dot(hidden, w[...], preferred_element_type=f32).astype(bf16)
    heads = bias_ref.shape[0]
    for pair in range(heads // 2):
        lanes = slice(pair * 128, pair * 128 + 128)
        q, k, v = q_ref[:, lanes], k_ref[:, lanes], v_ref[:, lanes]
        total = jnp.zeros(q.shape, f32)
        for side in range(2):
            h = 2 * pair + side
            scores = lax.dot_general(q, head_half(k, side), LAST, preferred_element_type=f32)
            scores = scores * 0.125 + bias_ref[h]
            top = jnp.max(scores, axis=1, keepdims=True)
            grown = jnp.exp(scores - top)
            probs = grown / jnp.sum(grown, axis=1, keepdims=True)
            probs_ref[h] = probs
            total = total + jnp.dot(
                probs.astype(bf16), head_half(v, side), preferred_element_type=f32
            )
        attended_ref[:, lanes] = total.astype(bf16)


def middle_kernel(place_ref, tokens_ref, gain_ref, attended_ref, *refs):
    f32 = jnp.float32
    mats, near, far = refs[:1], refs[1:4], refs[4:7]
    weight, middle_ref, moe_ref, sems = refs[8:12]
    copies = start_copies(
        block_copies(place_ref[0], place_ref[1], mats, near, far, [weight]), sems
    )
    for c in copies:
        c.wait()
    middle = tokens_ref[...].astype(f32) + jnp.dot(
        attended_ref[...], weight[...], preferred_element_type=f32
    )
    middle_ref[...] = middle
    moe_ref[...] = (middle * norm_scale(middle) * gain_ref[...].astype(f32)).astype(jnp.bfloat16)


def backward_kernel(
    core_ref,
    tokens_ref,
    cotangent_ref,
    gain_one_ref,
    gain_two_ref,
    ids_ref,
    router_ref,
    middle_ref,
    moe_ref,
    attended_ref,
    hidden_ref,
    q_ref,
    k_ref,
    v_ref,
    probs_ref,
    spots_ref,
    rows_ref,
    *refs,
):
    f32, bf16 = jnp.float32, jnp.bfloat16
    homes, weights = refs[:4], refs[4:8]
    result_ref, tokens_out, kept_ref, given_ref, scores_ref, router_out, gains_out = refs[8:15]
    held, grads_ref, sems = refs[15:18]
    copies = start_copies([(w, held.at[i]) for i, w in enumerate(weights)], sems)
    features = tokens_ref.shape[1]
    core = core_ref[0]

    def leave(mat, left, right):
        grad = lax.dot_general(left, right, FIRST, preferred_element_type=f32).astype(bf16)
        grads_ref[...] = grad
        for x in range(4):
            low = grads_ref[x * 192 : x * 192 + 96, :]
            high = grads_ref[x * 192 + 96 : x * 192 + 192, :]
            at = (mat * 4 + x) * 96
            kept_ref[at : at + 96, :features] = jnp.where(core == 0, low, high)
            given_ref[at : at + 96, :features] = jnp.where(core == 0, high, low)

    home = homes[0][...].astype(f32)
    for piece in homes[1:]:
        home = home + piece[...].astype(f32)
    middle = middle_ref[...]
    result_ref[...] = (middle + home[:, :features]).astype(bf16)
    tail = home[:, features:]
    lane = lax.broadcasted_iota(jnp.int32, tail.shape, 1)
    grad_gates = [
        jnp.sum(jnp.where((lane == k) | (lane == 2 + k), tail, 0.0), axis=1, keepdims=True)
        for k in range(2)
    ]
    moe = moe_ref[...]
    logits = jnp.dot(moe, router_ref[...], preferred_element_type=f32)
    ids = [to_column(ids_ref[k : k + 1, : tail.shape[0]]) for k in range(2)]
    gates = gate_pair(chosen_logit(logits, ids[0]), chosen_logit(logits, ids[1]))
    mix = gates[0] * grad_gates[0] + gates[1] * grad_gates[1]
    spots = lax.broadcasted_iota(jnp.int32, logits.shape, 1)
    grad_logits = jnp.zeros(logits.shape, f32)
    for k in range(2):
        grad_logits = jnp.where(spots == ids[k], gates[k] * (grad_gates[k] - mix), grad_logits)
    grad_logits = grad_logits.astype(bf16)
    slot = lax.broadcasted_iota(jnp.int32, (rows_ref.shape[0], tail.shape[0]), 0)
    pick = ((slot == spots_ref[0:1]) | (slot == spots_ref[1:2])).astype(f32).astype(bf16)
    grad_moe = lax.dot_general(pick, rows_ref[...], FIRST, preferred_element_type=f32)
    grad_moe = grad_moe + lax.dot_general(
        grad_logits, router_ref[...], LAST, preferred_element_type=f32
    )
    router_out[...] = lax.dot_general(moe, grad_logits, FIRST, preferred_element_type=f32)
    scale = norm_scale(middle)
    normed = middle * scale
    gains_out[1:2, :] = jnp.sum(grad_moe * normed, axis=0, keepdims=True)
    inner = grad_moe * gain_two_ref[...].astype(f32)
    grad_middle = cotangent_ref[...].astype(f32) + scale * (
        inner - normed * jnp.mean(inner * normed, axis=1, keepdims=True)
    )
    branch = grad_middle.astype(bf16)
    leave(3, attended_ref[...], branch)
    copies[3].wait()
    grad_attended = lax.dot_general(branch, held[3], LAST, preferred_element_type=f32).astype(bf16)
    grad_q, grad_k, grad_v = [], [], []
    for pair in range(probs_ref.shape[0] // 2):
        lanes = slice(pair * 128, pair * 128 + 128)
        q, k, v = q_ref[:, lanes], k_ref[:, lanes], v_ref[:, lanes]
        grad = grad_attended[:, lanes]
        parts = [jnp.zeros(q.shape, f32) for _ in range(3)]
        for side in range(2):
            h = 2 * pair + side
            probs = probs_ref[h]
            grad_half = head_half(grad, side)
            parts[2] = parts[2] + lax.dot_general(
                probs.astype(bf16), grad_half, FIRST, preferred_element_type=f32
            )
            grad_probs = lax.dot_general(grad_half, v, LAST, preferred_element_type=f32)
            grad_scores = (
                probs * (grad_probs - jnp.sum(probs * grad_probs, axis=1, keepdims=True))
            ).astype(bf16)
            scores_ref[h] = grad_scores
            parts[0] = parts[0] + jnp.dot(
                grad_scores, head_half(k, side), preferred_element_type=f32
            )
            parts[1] = parts[1] + lax.dot_general(
                grad_scores, head_half(q, side), FIRST, preferred_element_type=f32
            )
        grad_q.append((parts[0] * 0.125).astype(bf16))
        grad_k.append((parts[1] * 0.125).astype(bf16))
        grad_v.append(parts[2].astype(bf16))
    hidden = hidden_ref[...]
    grad_hidden = jnp.zeros(hidden.shape, f32)
    for n, parts in enumerate((grad_q, grad_k, grad_v)):
        grad = jnp.concatenate(parts, axis=1)
        leave(n, hidden, grad)
        copies[n].wait()
        grad_hidden = grad_hidden + lax.dot_general(
            grad, held[n], LAST, preferred_element_type=f32
        )
    x = tokens_ref[...].astype(f32)
    scale = norm_scale(x)
    normed = x * scale
    gains_out[0:1, :] = jnp.sum(grad_hidden * normed, axis=0, keepdims=True)
    inner = grad_hidden * gain_one_ref[...].astype(f32)
    tokens_out[...] = grad_middle + scale * (
        inner - normed * jnp.mean(inner * normed, axis=1, keepdims=True)
    )


ANYWHERE = pl.BlockSpec(memory_space=pl.ANY)
SCALARS = pl.BlockSpec(memory_space=pltpu.SMEM)
WHOLE = pl.BlockSpec(memory_space=pltpu.VMEM)
ROOM = pltpu.CompilerParams(vmem_limit_bytes=56 * 1024 * 1024)


def head(core, routes, gain_one, gain_two, bias, router, cotangent, mats):
    bf16 = jnp.bfloat16
    rows, cols = mats[0].shape
    half = rows // 2
    tokens = cotangent.shape[0]
    return pl.pallas_call(
        head_kernel,
        out_shape=[
            jax.ShapeDtypeStruct((tokens + 32, cols), bf16),
            jax.ShapeDtypeStruct((3 * half, cols), bf16),
            jax.ShapeDtypeStruct((half, cols), bf16),
        ],
        in_specs=[SCALARS] + [WHOLE] * 5 + [ANYWHERE] * 5,
        out_specs=[WHOLE] * 3,
        scratch_shapes=[pltpu.VMEM((32, cols), jnp.float32), pltpu.SemaphoreType.DMA((5,))],
        compiler_params=ROOM,
        name="head",
    )(core[None], routes, gain_one, gain_two, bias, router, cotangent, *mats)


def attend(where, tokens, gain, bias, mats, near, far, after):
    rows, cols = mats[0].shape
    full = jax.ShapeDtypeStruct((4 * rows, cols), jnp.bfloat16)
    state = jax.ShapeDtypeStruct(tokens.shape, jnp.bfloat16)
    return pl.pallas_call(
        attend_kernel,
        out_shape=[full] * 3 + [state] * 4 + [jax.ShapeDtypeStruct(bias.shape, jnp.float32), state],
        in_specs=[SCALARS] + [WHOLE] * 3 + [ANYWHERE] * 10,
        out_specs=[WHOLE] * 9,
        scratch_shapes=[pltpu.SemaphoreType.DMA((21,))],
        compiler_params=ROOM,
        name="attend",
    )(where, tokens, gain, bias, *mats, *near, *far, after)


def to_middle(where, tokens, gain, attended, mat, near, far, after):
    rows, cols = mat.shape
    return pl.pallas_call(
        middle_kernel,
        out_shape=[
            jax.ShapeDtypeStruct((4 * rows, cols), jnp.bfloat16),
            jax.ShapeDtypeStruct(tokens.shape, jnp.float32),
            jax.ShapeDtypeStruct(tokens.shape, jnp.bfloat16),
        ],
        in_specs=[SCALARS] + [WHOLE] * 3 + [ANYWHERE] * 8,
        out_specs=[WHOLE] * 3,
        scratch_shapes=[pltpu.SemaphoreType.DMA((7,))],
        compiler_params=ROOM,
        name="middle",
    )(where, tokens, gain, attended, mat, *near, *far, after)


def backward(core, *arrays):
    tokens, router_w, probs = arrays[0], arrays[5], arrays[13]
    count, features = tokens.shape
    bf16, f32 = jnp.bfloat16, jnp.float32
    shape = jax.ShapeDtypeStruct
    return pl.pallas_call(
        backward_kernel,
        out_shape=[
            shape((count, features), bf16),
            shape((count, features), f32),
            shape((2 * features, features), bf16),
            shape((2 * features, features), bf16),
            shape(probs.shape, bf16),
            shape(router_w.shape, f32),
            shape((2, features), f32),
        ],
        in_specs=[SCALARS] + [WHOLE] * 20 + [ANYWHERE] * 4,
        out_specs=[WHOLE] * 7,
        scratch_shapes=[
            pltpu.VMEM((4, features, features), bf16),
            pltpu.VMEM((features, features), bf16),
            pltpu.SemaphoreType.DMA((4,)),
        ],
        compiler_params=ROOM,
        name="backward",
    )(core, *arrays)


def picks_of(places, e, rows):
    row = lax.broadcasted_iota(jnp.int32, (rows, places.shape[1]), 0) + e * rows
    return ((row == places[0:1]) | (row == places[1:2])).astype(jnp.float32).astype(jnp.bfloat16)


def dispatch_grads_kernel(capacity, *refs):
    pieces, (out_ref, places_ref, ids_ref, spots_ref) = refs[:4], refs[4:]
    f32, bf16, i32 = jnp.float32, jnp.bfloat16, jnp.int32
    rows = out_ref.shape[0]
    tokens = spots_ref.shape[1]
    features = pieces[0].shape[1]
    experts_all = 2 * rows // (4 * capacity)
    expert = lax.broadcasted_iota(i32, (experts_all, tokens), 0)
    down = lax.broadcasted_iota(i32, (tokens, tokens), 0)
    across = lax.broadcasted_iota(i32, (tokens, tokens), 1)
    earlier = (down < across).astype(f32).astype(bf16)
    sums = []
    for r in range(4):
        both = pieces[r][tokens : tokens + 16, :tokens].astype(f32)
        ids = [both[5 + k : 6 + k].astype(i32) for k in range(2)]
        match = [expert == i for i in ids]
        named = (match[0] | match[1]).astype(f32).astype(bf16)
        counts = jnp.dot(named, earlier, preferred_element_type=f32)
        here = slice(r * tokens, (r + 1) * tokens)
        for k in range(2):
            slot = jnp.sum(jnp.where(match[k], counts, 0.0), axis=0, keepdims=True).astype(i32)
            owner, local = ids[k] >> 1, ids[k] & 1
            places_ref[k : k + 1, here] = (
                local * rows + owner * (4 * capacity) + r * capacity + slot
            )
            ids_ref[k : k + 1, here] = ids[k]
            if r == 0:
                spots_ref[k : k + 1, :] = owner * 16 + local * capacity + slot
        sums.append(to_column(both[5:6] + both[6:7]))
    sums = jnp.concatenate(sums, axis=0)
    lanes = lax.broadcasted_iota(i32, (4 * tokens, 128), 1)
    line = jnp.concatenate([p[:tokens, :] for p in pieces], axis=0)
    places = places_ref[...]
    extra = jnp.zeros((rows, 128), f32)
    for e in range(2):
        pick = picks_of(places, e, rows)
        out_ref[:, e * features : (e + 1) * features] = jnp.dot(
            pick, line, preferred_element_type=f32
        ).astype(bf16)
        column = jnp.where(lanes == e, sums, 0.0).astype(bf16)
        extra = extra + jnp.dot(pick, column, preferred_element_type=f32)
    out_ref[:, 2 * features :] = extra.astype(bf16)


def dispatch_grads(pieces, rows, capacity, tokens):
    features = pieces[0].shape[1]
    shape = jax.ShapeDtypeStruct
    return pl.pallas_call(
        functools.partial(dispatch_grads_kernel, capacity),
        out_shape=[
            shape((rows, 2 * features + 128), jnp.bfloat16),
            shape((2, 4 * tokens), jnp.int32),
            shape((2, 4 * tokens), jnp.int32),
            shape((2, tokens), jnp.int32),
        ],
        in_specs=[WHOLE] * 4,
        out_specs=[WHOLE] * 4,
        compiler_params=ROOM,
        name="dispatch_grads",
    )(*pieces)


def dispatch_kernel(places_ref, *refs):
    pieces, out_ref = refs[:4], refs[4]
    rows = out_ref.shape[0]
    features = pieces[0].shape[1]
    line = jnp.concatenate([p[...] for p in pieces], axis=0)
    for e in range(2):
        out_ref[:, e * features : (e + 1) * features] = jnp.dot(
            picks_of(places_ref[...], e, rows), line, preferred_element_type=jnp.float32
        ).astype(jnp.bfloat16)


def dispatch(places, pieces, rows):
    return pl.pallas_call(
        dispatch_kernel,
        out_shape=jax.ShapeDtypeStruct((rows, 2 * pieces[0].shape[1]), jnp.bfloat16),
        in_specs=[WHOLE] * 5,
        out_specs=WHOLE,
        compiler_params=ROOM,
        name="dispatch",
    )(places, *pieces)


def chosen_logit(logits, ids):
    lanes = lax.broadcasted_iota(jnp.int32, logits.shape, 1)
    return jnp.sum(jnp.where(lanes == ids, logits, 0.0), axis=1, keepdims=True)


def gate_pair(first, second):
    top = jnp.maximum(first, second)
    one, two = jnp.exp(first - top), jnp.exp(second - top)
    total = one + two
    return one / total, two / total


def expert_kernel(x_ref, in_ref, out_ref, ret_ref, act_ref, rise_ref):
    f32, bf16 = jnp.float32, jnp.bfloat16
    step = 256
    slope = math.sqrt(2.0 / math.pi)

    def chunk(i, carry):
        at = pl.ds(pl.multiple_of(i * step, step), step)
        pre = jnp.dot(x_ref[at, :], in_ref[0], preferred_element_type=f32)
        tanh = jnp.tanh(slope * (pre + 0.044715 * (pre * pre * pre)))
        active = (0.5 * pre * (1.0 + tanh)).astype(bf16)
        act_ref[0, at, :] = active
        ret_ref[at, :] = jnp.dot(active, out_ref[0], preferred_element_type=f32).astype(bf16)
        rise_ref[0, at, :] = 0.5 * (1.0 + tanh) + 0.5 * pre * (1.0 - tanh * tanh) * (
            slope * (1.0 + 3.0 * 0.044715 * (pre * pre))
        )
        return carry

    lax.fori_loop(0, x_ref.shape[0] // step, chunk, 0)


def lanes_of(rows, n):
    return pl.BlockSpec((rows, n), lambda e: (0, e))


def one_of(a, b):
    return pl.BlockSpec((1, a, b), lambda e: (e, 0, 0))


def experts(arrived, w_in, w_out):
    rows = arrived.shape[0]
    features, hidden = w_in.shape[1:]
    return pl.pallas_call(
        expert_kernel,
        grid=(2,),
        out_shape=[
            jax.ShapeDtypeStruct((rows, 2 * features), jnp.bfloat16),
            jax.ShapeDtypeStruct((2, rows, hidden), jnp.bfloat16),
            jax.ShapeDtypeStruct((2, rows, hidden), jnp.float32),
        ],
        in_specs=[lanes_of(rows, features), one_of(features, hidden), one_of(hidden, features)],
        out_specs=[lanes_of(rows, features), one_of(rows, hidden), one_of(rows, hidden)],
        compiler_params=ROOM,
        name="experts",
    )(arrived, w_in, w_out)


def expert_back_kernel(
    capacity, own_ref, x_ref, g_ref, ids_ref, in_ref, out_ref, router_ref, rise_ref, *refs
):
    pre_ref, arr_ref, outs, held = refs[0], refs[1], refs[2:6], refs[6]
    f32, bf16, i32 = jnp.float32, jnp.bfloat16, jnp.int32
    e = pl.program_id(0)
    own = own_ref[0] + e
    rows = x_ref.shape[0]
    step = 256

    def chunk(i, carry):
        at = pl.ds(pl.multiple_of(i * step, step), step)
        ids = ids_ref[at, :].astype(f32)
        lanes = lax.broadcasted_iota(i32, ids.shape, 1)
        other = jnp.sum(jnp.where(lanes == e, ids, 0.0), axis=1, keepdims=True).astype(i32) - own
        logits = jnp.dot(x_ref[at, :], router_ref[...], preferred_element_type=f32)
        gate, _ = gate_pair(chosen_logit(logits, own), chosen_logit(logits, other))
        grown = (gate * g_ref[at, :].astype(f32)).astype(bf16)
        arr_ref[0, at, :] = grown
        back = lax.dot_general(grown, out_ref[0], LAST, preferred_element_type=f32)
        grad = (back * rise_ref[0, at, :]).astype(bf16)
        pre_ref[0, at, :] = grad
        held[at, :] = lax.dot_general(grad, in_ref[0], LAST, preferred_element_type=f32).astype(
            bf16
        )
        return carry

    lax.fori_loop(0, rows // step, chunk, 0)
    part = rows // 4
    here = lax.broadcasted_iota(i32, (part, rows), 0)
    there = lax.broadcasted_iota(i32, (part, rows), 1)
    block = (here * (65536 // capacity + 1)) >> 16
    for r, out in enumerate(outs):
        source = here + block * (3 * capacity) + r * capacity
        pick = (there == source).astype(f32).astype(bf16)
        out[...] = jnp.dot(pick, held[...], preferred_element_type=f32).astype(bf16)


def experts_back(own, arrived, grad_wide, w_in, w_out, router_w, rise, capacity):
    rows = arrived.shape[0]
    features, hidden = w_in.shape[1:]
    bf16 = jnp.bfloat16
    shape = jax.ShapeDtypeStruct
    part = rows // 4
    return pl.pallas_call(
        functools.partial(expert_back_kernel, capacity),
        grid=(2,),
        out_shape=[shape((2, rows, hidden), bf16), shape((2, rows, features), bf16)]
        + [shape((2 * part, features), bf16)] * 4,
        in_specs=[
            SCALARS,
            lanes_of(rows, features),
            lanes_of(rows, features),
            pl.BlockSpec((rows, 128), lambda e: (0, 2 * features // 128)),
            one_of(features, hidden),
            one_of(hidden, features),
            pl.BlockSpec(router_w.shape, lambda e: (0, 0)),
            one_of(rows, hidden),
        ],
        out_specs=[one_of(rows, hidden), one_of(rows, features)]
        + [pl.BlockSpec((part, features), lambda e: (e, 0))] * 4,
        scratch_shapes=[pltpu.VMEM((rows, features), bf16)],
        compiler_params=ROOM,
        name="experts_back",
    )(own[None], arrived, grad_wide, grad_wide, w_in, w_out, router_w, rise)


def weight_grads_kernel(x_ref, pre_ref, act_ref, arr_ref, in_ref, out_ref):
    in_ref[0] = lax.dot_general(x_ref[...], pre_ref[0], FIRST, preferred_element_type=jnp.float32)
    out_ref[0] = lax.dot_general(act_ref[0], arr_ref[0], FIRST, preferred_element_type=jnp.float32)


def weight_grads(arrived, grad_pre, active, grad_arrived):
    rows = arrived.shape[0]
    hidden, features = grad_pre.shape[2], grad_arrived.shape[2]
    step = 256
    cuts = features // step
    whole = lambda n: pl.BlockSpec((1, rows, n), lambda e, j: (e, 0, 0))
    out = lambda n: pl.BlockSpec((1, step, n), lambda e, j: (e, j, 0))
    return pl.pallas_call(
        weight_grads_kernel,
        grid=(2, cuts),
        out_shape=[
            jax.ShapeDtypeStruct((2, features, hidden), jnp.float32),
            jax.ShapeDtypeStruct((2, hidden, features), jnp.float32),
        ],
        in_specs=[
            pl.BlockSpec((rows, step), lambda e, j: (0, e * cuts + j)),
            whole(hidden),
            pl.BlockSpec((1, rows, step), lambda e, j: (e, 0, j)),
            whole(features),
        ],
        out_specs=[out(hidden), out(features)],
        compiler_params=ROOM,
        cost_estimate=pl.CostEstimate(
            flops=8 * rows * features * hidden, bytes_accessed=20_000_000, transcendentals=0
        ),
        name="weight_grads",
    )(arrived, grad_pre, active, grad_arrived)


def sum_rows_kernel(capacity, *refs):
    pieces, out_ref = refs[:4], refs[-1]
    f32, bf16, i32 = jnp.float32, jnp.bfloat16, jnp.int32
    total = pieces[0][...].astype(f32)
    for piece in pieces[1:]:
        total = total + piece[...].astype(f32)
    rows = out_ref.shape[0]
    part = total.shape[0] // 2
    here = lax.broadcasted_iota(i32, (rows, 2 * part), 0)
    there = lax.broadcasted_iota(i32, (rows, 2 * part), 1)
    owner, q = here >> 4, here & 15
    second = q >= capacity
    source = owner * capacity + jnp.where(second, part + q - capacity, q)
    pick = ((there == source) & (q < 2 * capacity)).astype(f32).astype(bf16)
    out_ref[...] = jnp.dot(pick, total.astype(bf16), preferred_element_type=f32).astype(bf16)


def sum_rows(pieces, capacity, after):
    rows, features = pieces[0].shape
    return pl.pallas_call(
        functools.partial(sum_rows_kernel, capacity),
        out_shape=jax.ShapeDtypeStruct((rows // (2 * capacity) * 16, features), jnp.bfloat16),
        in_specs=[WHOLE] * 4 + [ANYWHERE] * len(after),
        out_specs=WHOLE,
        compiler_params=ROOM,
        name="sum_rows",
    )(*pieces, *after)


def combine_kernel(places_ref, ids_ref, router_ref, ret_ref, *refs):
    f32, bf16 = jnp.float32, jnp.bfloat16
    grads, moes, outs = refs[:4], refs[4:8], refs[9:13]
    tokens, features = moes[0].shape
    rows = ret_ref.shape[0]
    row = lax.broadcasted_iota(jnp.int32, (rows, tokens), 0)
    tail_lane = lax.broadcasted_iota(jnp.int32, (tokens, 128), 1)
    for r in range(4):
        here = slice(r * tokens, (r + 1) * tokens)
        logits = jnp.dot(moes[r][...], router_ref[...], preferred_element_type=f32)
        ids = [to_column(ids_ref[k : k + 1, here]) for k in range(2)]
        gates = gate_pair(chosen_logit(logits, ids[0]), chosen_logit(logits, ids[1]))
        total = jnp.zeros((tokens, features), f32)
        tail = jnp.zeros((tokens, 128), f32)
        grad = grads[r][:tokens, :].astype(f32)
        for k in range(2):
            got = jnp.zeros((tokens, features), f32)
            for e in range(2):
                pick = (row + e * rows == places_ref[k : k + 1, here]).astype(f32).astype(bf16)
                got = got + lax.dot_general(
                    pick,
                    ret_ref[:, e * features : (e + 1) * features],
                    FIRST,
                    preferred_element_type=f32,
                )
            total = total + gates[k] * got
            dots = jnp.sum(grad * got, axis=1, keepdims=True)
            high = dots.astype(bf16).astype(f32)
            tail = jnp.where(tail_lane == k, high, tail)
            tail = jnp.where(tail_lane == 2 + k, dots - high, tail)
        outs[r][:, :features] = total.astype(bf16)
        outs[r][:, features:] = tail.astype(bf16)


def combine(places, ids, router_w, returned, grads, moes, after):
    tokens, features = moes[0].shape
    return pl.pallas_call(
        combine_kernel,
        out_shape=[jax.ShapeDtypeStruct((tokens, features + 128), jnp.bfloat16)] * 4,
        in_specs=[WHOLE] * 12 + [ANYWHERE],
        out_specs=[WHOLE] * 4,
        compiler_params=ROOM,
        name="combine",
    )(places, ids, router_w, returned, *grads, *moes, after)


def layer(
    tokens,
    seq_lengths,
    routes,
    gain_attn,
    w_query,
    w_key,
    w_value,
    w_output,
    rel_bias,
    gain_moe,
    w_router,
    w_in,
    w_out,
    cotangent,
):
    row_count, features = tokens.shape
    shard_rows = w_query.shape[0]
    expert_count = w_router.shape[1]
    bucket_count = rel_bias.shape[1]
    head_count = 4 * rel_bias.shape[0]
    capacity = 3 * row_count // expert_count
    bias_size = rel_bias.size
    f32 = jnp.float32
    bf16 = jnp.bfloat16

    shard = lax.axis_index("x").astype(jnp.int32)
    core = lax.axis_index("c").astype(jnp.int32)
    where = jnp.stack([shard, core])
    owners = expert_count // 2
    slot_rows = owners * 4 * capacity

    line, sent_qkv, sent_out = head(
        core,
        routes.T,
        gain_attn[None],
        gain_moe[None],
        rel_bias,
        w_router,
        cotangent,
        (w_query, w_key, w_value, w_output),
    )
    line_grads = along_x(line)
    near_qkv = along_x(sent_qkv)[1:]
    near_out = along_x(sent_out)[1:]
    order = (shard - jnp.arange(4)) % 4
    small = jnp.take(jnp.stack([p[row_count:] for p in line_grads]), order, axis=0)
    gain_one = small[:, 0, :shard_rows].reshape(1, features)
    gain_two = small[:, 1, :shard_rows].reshape(1, features)
    bias_table = small[:, 2:5, :bucket_count].reshape(head_count, bucket_count)
    router_w = (
        small[:, 16:]
        .reshape(4, 16, shard_rows // 16, expert_count)
        .transpose(0, 2, 1, 3)
        .reshape(features, expert_count)
    )

    def to_owners(outgoing):
        return lax.all_to_all(outgoing, ("y", "z", "c"), 0, 0, tiled=True)

    outgoing_grads, places, ids, spots = dispatch_grads(
        line_grads, slot_rows, capacity, row_count
    )
    grad_wide = to_owners(outgoing_grads)
    first_expert = 2 * lax.axis_index(("y", "z", "c")).astype(jnp.int32)

    segments = row_segments(seq_lengths[0], row_count)
    distance, onehot = position_tables(row_count, bucket_count)
    allowed = (segments[:, None] == segments[None, :]) & (distance >= 0)
    position_bias = jnp.einsum("ijb,hb->hij", onehot, bias_table, preferred_element_type=f32)
    masked_bias = jnp.where(allowed[None], position_bias, -1000000000.0)
    far_qkv = [swap_core(part) for part in near_qkv]
    far_out = [swap_core(part) for part in near_out]
    query_w, key_w, value_w, hidden_one, queries, key_rows, value_rows, probs, attended = attend(
        where,
        tokens,
        gain_one,
        masked_bias,
        (w_query, w_key, w_value),
        near_qkv,
        far_qkv,
        outgoing_grads,
    )
    output_w, middle, moe_in = to_middle(
        where, tokens, gain_two, attended, w_output, near_out, far_out, outgoing_grads
    )

    line_moe = along_x(moe_in)
    arrived = to_owners(dispatch(places, line_moe, slot_rows))
    ret, active, rise = experts(arrived, w_in, w_out)
    returned = to_owners(ret)
    grad_pre, grad_arrived, *blocks = experts_back(
        first_expert, arrived, grad_wide, w_in, w_out, router_w, rise, capacity
    )
    summed = [blocks[0]] + [shift_x(blocks[r], -r) for r in range(1, 4)]
    grad_w_in, grad_w_out = weight_grads(arrived, grad_pre, active, grad_arrived)
    rows_home = sum_rows(summed, capacity, (grad_w_in, grad_w_out))
    back_rows = to_owners(rows_home)
    bundle = combine(places, ids, router_w, returned, line_grads, line_moe, rows_home)
    homes = [bundle[0]] + [shift_x(bundle[r], -r) for r in range(1, 4)]
    result, grad_tokens, kept, given, grad_scores, grad_router, grad_gains = backward(
        core[None],
        tokens,
        cotangent,
        gain_one,
        gain_two,
        ids,
        router_w,
        middle,
        moe_in,
        attended,
        hidden_one,
        queries,
        key_rows,
        value_rows,
        probs,
        spots,
        back_rows,
        *homes,
        query_w,
        key_w,
        value_w,
        output_w,
    )
    grad_bias = jnp.einsum("hij,ijb->hb", grad_scores, onehot, preferred_element_type=f32)

    piece = shard_rows // 8
    wide = features + 128
    bias_column = jnp.pad(grad_bias.reshape(4, bias_size), ((0, 0), (0, shard_rows - bias_size)))
    small_grads = jnp.concatenate(
        [grad_router, grad_gains.T, bias_column.reshape(-1, 1)], axis=1
    ).astype(bf16)
    small_grads = jnp.pad(small_grads, ((0, 0), (0, 128 - small_grads.shape[1])))
    small_grads = small_grads.reshape(4, 2, shard_rows // 2, 128)

    def small_half(side):
        part = lax.dynamic_index_in_dim(small_grads, side, 1, keepdims=False).reshape(-1, 128)
        return jnp.pad(part, ((0, kept.shape[0] - part.shape[0]), (0, 0)))

    pairs = ((kept, swap_core(given)), (small_half(core), swap_core(small_half(1 - core))))
    paired = jnp.concatenate(
        [(a.astype(f32) + b.astype(f32)).astype(bf16) for a, b in pairs], axis=1
    )
    spread = lax.all_to_all(paired, ("y", "x", "z"), 0, 0, tiled=True)
    mine = jnp.sum(spread.reshape(64, piece, wide).astype(f32), axis=0).astype(bf16)
    totals = lax.all_to_all(
        jnp.broadcast_to(mine[None], (32, piece, wide)).reshape(32 * piece, wide),
        ("y", "c", "z"),
        0,
        0,
        tiled=True,
    ).reshape(4, shard_rows, wide)
    small_totals = totals[0, :, features:].astype(f32)
    totals = totals[:, :, :features].astype(f32)
    router_total = small_totals[:, :expert_count]
    gain_one_total = small_totals[:, expert_count]
    gain_two_total = small_totals[:, expert_count + 1]
    bias_total = small_totals[:bias_size, expert_count + 2].reshape(rel_bias.shape)
    return (
        result,
        grad_tokens,
        gain_one_total,
        totals[0],
        totals[1],
        totals[2],
        totals[3],
        bias_total,
        gain_two_total,
        router_total,
        grad_w_in,
        grad_w_out,
    )


def solution(mesh):
    cube = Mesh(mesh.devices.reshape(4, 4, 2, 4), ("y", "z", "c", "x"))
    expert = ("y", "z", "c")
    everyone = ("y", "z", "c", "x")
    placed = (
        P(everyone, None),
        P(everyone, None),
        P(everyone, None),
        P("x"),
        P("x", None),
        P("x", None),
        P("x", None),
        P("x", None),
        P("x", None),
        P("x"),
        P("x", None),
        P(expert, None, "x"),
        P(expert, "x", None),
        P(everyone, None),
    )
    return jax.shard_map(
        layer,
        mesh=cube,
        in_specs=placed,
        out_specs=(
            P(everyone, None),
            P(everyone, None),
            P("x"),
            P("x", None),
            P("x", None),
            P("x", None),
            P("x", None),
            P("x", None),
            P("x"),
            P("x", None),
            P(expert, None, "x"),
            P(expert, "x", None),
        ),
        check_vma=False,
    )
```

profile of v0, /device:TPU:1, one launch (start us, length us, event | category | flops | bytes accessed | tf_op | source)
XLA Modules:
  0.0 345.0 jit_solution(5392781749779131043)
XLA Ops:
  0.6 1.2 broadcast_in_dim.54.one_ref
  1.9 1.2 broadcast_in_dim.55.two_ref
  3.1 1.5 copy.46.router_ref
  4.6 3.0 head.1
  7.6 3.4 collective-permute-start.2
  12.1 1.5 collective-permute-start.3
  13.6 1.7 collective-permute-start.4
  18.8 14.2 %collective-permute-start.5 = (bf16[288,768]{1,0:T(8,128)(2,1)}, bf16[288,768]{1,0:T(8,128)(2,1)S(1)}, u32[]{:S(2)}, u32[]{:S(2)}) collective-permute-start(bf16[288,768]{1,0:T(8,128)(2,1)} %get-tuple-element.55), channel_id=1, source_target_pairs={{0,3},{1,0},{2,1},{3,2},{4,7},{5,4},{6,5},{7,6},{8,11},{9,8},{10,9... | collective-permute-start | bytes 1327112 | tf_op jit(solution)/shard_map/ppermute | solution.py:34
  33.1 1.2 collective-permute-start.10
  35.0 1.7 collective-permute-done.3.refs_3_
  36.6 1.5 collective-permute-start.6
  39.7 4.7 %dispatch_grads.1 = (bf16[768,1664]{1,0:T(8,128)(2,1)}, s32[2,512]{1,0:T(2,128)}, s32[2,512]{1,0:T(2,128)}, s32[2,128]{1,0:T(2,128)}) custom-call(bf16[160,768]{1,0:T(8,128)(2,1)} %get-tuple-element.53.refs_0_, bf16[160,768]{1,0:T(8,128)(2,1)} %copy-done.5, bf16[160,768]{1,0:T(8,128)(2,1)} %copy-done.4, bf16[160,768]{1,0:T(8,128)(2,1)} %copy-done.3), custom_call_target="tpu_custom_call" | custom-call | tf_op jit(solution)/shard_map/dispatch_grads/pallas_call | solution.py:427
  44.4 4.9 %collective-permute-done.9.refs_1_ = bf16[96,768]{1,0:T(8,128)(2,1)S(1)} collective-permute-done((bf16[96,768]{1,0:T(8,128)(2,1)}, bf16[96,768]{1,0:T(8,128)(2,1)S(1)}, u32[]{:S(2)}, u32[]{:S(2)}) %collective-permute-start.9) | collective-permute-done | bytes 147488 | tf_op jit(solution)/shard_map/ppermute | solution.py:34
  49.4 1.2 collective-permute-start.7
  51.7 2.4 collective-permute-done.11.refs_3_
  54.1 1.5 collective-permute-start.13
  55.7 1.2 copy_select_fusion.bias_ref
  57.8 6.8 %attend.1 = (bf16[768,768]{1,0:T(8,128)(2,1)}, bf16[768,768]{1,0:T(8,128)(2,1)}, bf16[768,768]{1,0:T(8,128)(2,1)}, bf16[128,768]{1,0:T(8,128)(2,1)}, bf16[128,76...) custom-call(s32[2]{0:T(128)} %pad_add_fusion.place_ref, ...), custom_call_target="tpu_custom_call" | custom-call | tf_op jit(solution)/shard_map/attend/pallas_call | solution.py:319
  65.4 3.6 %middle.1 = (bf16[768,768]{1,0:T(8,128)(2,1)}, f32[128,768]{1,0:T(8,128)}, bf16[128,768]{1,0:T(8,128)(2,1)}) custom-call(s32[2]{0:T(128)} %pad_add_fusion.place_ref, bf16[128,768]{1,0:T(8,128)(2,1)} %tokens_ref.5, bf16[1,768]{1,0:T(2,128)(2,1)} %reshape_squeeze.10.gain_ref.gain_two_ref, bf16[128,768]{1,0:T(8,128)(2,1)} %get-tuple-element.57.attended_ref, ...), custom_call_target="tpu_custom_call" | custom-call | tf_op jit(solution)/shard_map/middle/pallas_call | solution.py:332
  69.1 2.4 collective-permute-start.16
  71.8 5.1 %collective-permute-done.15.refs_1_.refs_5_ = bf16[128,768]{1,0:T(8,128)(2,1)S(1)} collective-permute-done((bf16[128,768]{1,0:T(8,128)(2,1)}, bf16[128,768]{1,0:T(8,128)(2,1)S(1)}, u32[]{:S(2)}, u32[]{:S(2)}) %collective-permute-start.15) | collective-permute-done | bytes 196640 | tf_op jit(solution)/shard_map/ppermute | solution.py:34
  76.9 3.7 %collective-permute-done.16.refs_2_.refs_6_ = bf16[128,768]{1,0:T(8,128)(2,1)S(1)} collective-permute-done((bf16[128,768]{1,0:T(8,128)(2,1)}, bf16[128,768]{1,0:T(8,128)(2,1)S(1)}, u32[]{:S(2)}, u32[]{:S(2)}) %collective-permute-start.16) | collective-permute-done | bytes 196640 | tf_op jit(solution)/shard_map/ppermute | solution.py:34
  81.8 4.0 %dispatch.1 = bf16[768,1536]{1,0:T(8,128)(2,1)} custom-call(s32[2,512]{1,0:T(2,128)} %get-tuple-element.67.places_ref, bf16[128,768]{1,0:T(8,128)(2,1)} %get-tuple-element.60.refs_0_.refs_4_.moe_ref, bf16[128,768]{1,0:T(8,128)(2,1)} %copy-done.6, bf16[128,768]{1,0:T(8,128)(2,1)} %copy-done.7, bf16[128,768]{1,0:T(8,128)(2,1)} %copy-done.8), custom_call_target="tpu_custom_call" | custom-call | tf_op jit(solution)/shard_map/dispatch/pallas_call | solution.py:454
  85.9 41.2 %all_to_all.59 = bf16[32,24,1536]{2,1,0:T(8,128)(2,1)} all-to-all(bf16[32,24,1536]{2,1,0:T(8,128)(2,1)} %bitcast.59), channel_id=1, replica_groups=mesh['y'=4,'z'=4,'c'=2,'x'=4] {'y','z','c'}, dimensions={0} | all-to-all | bytes 4718592 | tf_op jit(solution)/shard_map/all_to_all | solution.py:756
  127.1 3.9 %all-to-all-start.1 = ((bf16[32,24,1664]{2,1,0:T(8,128)(2,1)}), bf16[32,24,1664]{2,1,0:T(8,128)(2,1)S(1)}, u32[]{:S(2)}, u32[]{:S(2)}) async-start(bf16[32,24,1664]{2,1,0:T(8,128)(2,1)} %bitcast.54), calls=%async_computation.1 | async-start | bytes 5111808 | tf_op jit(solution)/shard_map/all_to_all | solution.py:756
  131.0 11.3 %experts.1 = (bf16[768,1536]{1,0:T(8,128)(2,1)}, bf16[2,768,768]{2,1,0:T(8,128)(2,1)}, f32[2,768,768]{2,1,0:T(8,128)}) custom-call(bf16[768,1536]{1,0:T(8,128)(2,1)} %bitcast.55, bf16[2,768,768]{2,1,0:T(8,128)(2,1)} %in_ref.3, bf16[2,768,768]{2,1,0:T(8,128)(2,1)} %out_ref.3), custom_call_target="tpu_custom_call" | custom-call | tf_op jit(solution)/shard_map/experts/pallas_call | solution.py:507
  142.3 22.0 %all-to-all-done.1 = bf16[32,24,1664]{2,1,0:T(8,128)(2,1)S(1)} async-done(((bf16[32,24,1664]{2,1,0:T(8,128)(2,1)}), bf16[32,24,1664]{2,1,0:T(8,128)(2,1)S(1)}, u32[]{:S(2)}, u32[]{:S(2)}) %all-to-all-start.1) | async-done | bytes 2555936 | tf_op jit(solution)/shard_map/all_to_all | solution.py:756
  164.3 1.5 copy-done
  165.7 5.4 %all-to-all-start.3 = ((bf16[32,24,1536]{2,1,0:T(8,128)(2,1)}), bf16[32,24,1536]{2,1,0:T(8,128)(2,1)}, u32[]{:S(2)}, u32[]{:S(2)}) async-start(bf16[32,24,1536]{2,1,0:T(8,128)(2,1)} %bitcast.67), calls=%async_computation.3 | async-start | bytes 4718592 | tf_op jit(solution)/shard_map/all_to_all | solution.py:756
  172.0 13.3 %experts_back.1 = (bf16[2,768,768]{2,1,0:T(8,128)(2,1)}, bf16[2,768,768]{2,1,0:T(8,128)(2,1)}, bf16[384,768]{1,0:T(8,128)(2,1)}, bf16[384,768]{1,0:T(8,128)(2,1)...) custom-call(s32[1]{0:T(128)} %bitcast.12.own_ref, bf16[768,1536]{1,0:T(8,128)(2,1)} %bitcast.56, ...), custom_call_target="tpu_custom_call" | custom-call | tf_op jit(solution)/shard_map/experts_back/pallas_call | solution.py:566
  185.3 2.1 collective-permute-start.18
  188.1 10.0 %weight_grads.1 = (f32[2,768,768]{2,1,0:T(8,128)}, f32[2,768,768]{2,1,0:T(8,128)}) custom-call(bf16[768,1536]{1,0:T(8,128)(2,1)} %bitcast.57, bf16[2,768,768]{2,1,0:T(8,128)(2,1)} %get-tuple-element.73.pre_ref, bf16[2,768,768]{2,1,0:T(8,128)(2,1)} %get-tuple-element.74.act_ref, bf16[2,768,768]{2,1,0:T(8,128)(2,1)} %get-tuple-element.75.arr_ref), custom_call_target="tpu_custom_call" | custom-call | flops 3623878656 | bytes 20000000 | tf_op jit(solution)/shard_map/weight_grads/pallas_call | solution.py:601
  198.2 2.3 collective-permute-done.18.refs_1_
  200.4 3.0 collective-permute-done.19.refs_2_
  203.4 13.0 %collective-permute-done.20.refs_3_ = bf16[384,768]{1,0:T(8,128)(2,1)S(1)} collective-permute-done((bf16[384,768]{1,0:T(8,128)(2,1)}, bf16[384,768]{1,0:T(8,128)(2,1)S(1)}, u32[]{:S(2)}, u32[]{:S(2)}) %collective-permute-start.20) | collective-permute-done | bytes 589856 | tf_op jit(solution)/shard_map/ppermute | solution.py:34
  217.3 3.3 sum_rows.1.refs_8_
  220.6 7.9 %all-to-all-start.2 = ((bf16[32,16,768]{2,1,0:T(8,128)(2,1)}), bf16[32,16,768]{2,1,0:T(8,128)(2,1)S(1)}, u32[]{:S(2)}, u32[]{:S(2)}) async-start(bf16[32,16,768]{2,1,0:T(8,128)(2,1)} %bitcast.60), calls=%async_computation.2 | async-start | bytes 1572864 | tf_op jit(solution)/shard_map/all_to_all | solution.py:756
  228.5 5.9 %combine.1 = (bf16[128,896]{1,0:T(8,128)(2,1)}, bf16[128,896]{1,0:T(8,128)(2,1)}, bf16[128,896]{1,0:T(8,128)(2,1)}, bf16[128,896]{1,0:T(8,128)(2,1)}) custom-call(s32[2,512]{1,0:T(2,128)} %get-tuple-element.67.places_ref, s32[2,512]{1,0:T(2,128)} %get-tuple-element.54.ids_ref, bf16[768,64]{1,0:T(8,128)(2,1)} %bitcast.64, bf16[768,1536]{1,0:T(8,128)(2,1)} %bitcast.20.ret_ref, ...), custom_call_target="tpu_custom_call" | custom-call | tf_op jit(solution)/shard_map/combine/pallas_call | solution.py:688
  236.0 6.8 %all-to-all-done.2 = bf16[32,16,768]{2,1,0:T(8,128)(2,1)S(1)} async-done(((bf16[32,16,768]{2,1,0:T(8,128)(2,1)}), bf16[32,16,768]{2,1,0:T(8,128)(2,1)S(1)}, u32[]{:S(2)}, u32[]{:S(2)}) %all-to-all-start.2) | async-done | bytes 786464 | tf_op jit(solution)/shard_map/all_to_all | solution.py:756
  243.5 5.8 %collective-permute-done.23.refs_3_ = bf16[128,896]{1,0:T(8,128)(2,1)S(1)} collective-permute-done((bf16[128,896]{1,0:T(8,128)(2,1)}, bf16[128,896]{1,0:T(8,128)(2,1)S(1)}, u32[]{:S(2)}, u32[]{:S(2)}) %collective-permute-start.23) | collective-permute-done | bytes 229408 | tf_op jit(solution)/shard_map/ppermute | solution.py:34
  250.0 12.1 %backward.1 = (bf16[128,768]{1,0:T(8,128)(2,1)}, f32[128,768]{1,0:T(8,128)}, bf16[1536,768]{1,0:T(8,128)(2,1)}, bf16[1536,768]{1,0:T(8,128)(2,1)}, bf16[12,128,1...) custom-call(s32[1]{0:T(128)} %bitcast.core_ref, bf16[128,768]{1,0:T(8,128)(2,1)} %tokens_ref.5, ...), custom_call_target="tpu_custom_call" | custom-call | tf_op jit(solution)/shard_map/backward/pallas_call | solution.py:352
  262.6 1.7 fusion.3
  265.6 1.0 convert.16
  267.1 1.7 collective-permute-done.25
  268.8 2.3 add_convert_fusion
  271.3 43.7 %all_to_all.60 = bf16[64,24,896]{2,1,0:T(8,128)(2,1)S(1)} all-to-all(bf16[64,24,896]{2,1,0:T(8,128)(2,1)S(1)} %bitcast.58), channel_id=1, replica_groups=mesh['y'=4,'z'=4,'c'=2,'x'=4] {'y','x','z'}, dimensions={0} | all-to-all | bytes 5505024 | tf_op jit(solution)/shard_map/all_to_all | solution.py:841
  315.6 25.4 %all_to_all.61 = bf16[32,24,896]{2,1,0:T(8,128)(2,1)S(1)} all-to-all(bf16[32,24,896]{2,1,0:T(8,128)(2,1)S(1)} %broadcast_in_dim.60), channel_id=1, replica_groups=mesh['y'=4,'z'=4,'c'=2,'x'=4] {'y','c','z'}, dimensions={0} | all-to-all | bytes 2752512 | tf_op jit(solution)/shard_map/all_to_all | solution.py:843
  342.2 1.4 slice_bitcast_fusion
  (131 shorter events, 22.0 us)
Async XLA Ops:
  7.6 41.7 %copy-start.27 = (bf16[96,768]{1,0:T(8,128)(2,1)S(1)}, bf16[96,768]{1,0:T(8,128)(2,1)}, u32[]{:S(2)}) copy-start(bf16[96,768]{1,0:T(8,128)(2,1)} %get-tuple-element.58) | copy-start | bytes 442372
  7.6 11.2 %collective-permute-start.2 = (bf16[160,768]{1,0:T(8,128)(2,1)}, bf16[160,768]{1,0:T(8,128)(2,1)S(1)}, u32[]{:S(2)}, u32[]{:S(2)}) collective-permute-start(bf16[160,768]{1,0:T(8,128)(2,1)} %get-tuple-element.53.refs_0_), channel_id=1, source_target_pairs={{0,3},{1,0},{2,1},{3,2},{4,7},{5,4},{6,5},{7,6},{8,11},{9,8},{10,9... | collective-permute-start | bytes 737288 | tf_op jit(solution)/shard_map/ppermute | solution.py:34
  11.0 22.0 %collective-permute-start.1 = (bf16[160,768]{1,0:T(8,128)(2,1)}, bf16[160,768]{1,0:T(8,128)(2,1)S(1)}, u32[]{:S(2)}, u32[]{:S(2)}) collective-permute-start(bf16[160,768]{1,0:T(8,128)(2,1)} %get-tuple-element.53.refs_0_), channel_id=1, source_target_pairs={{0,2},{1,3},{2,0},{3,1},{4,6},{5,7},{6,4},{7,5},{8,10},{9,11},{10,... | collective-permute-start | bytes 737288 | tf_op jit(solution)/shard_map/ppermute | solution.py:34
  11.5 21.6 %collective-permute-start = (bf16[160,768]{1,0:T(8,128)(2,1)}, bf16[160,768]{1,0:T(8,128)(2,1)S(1)}, u32[]{:S(2)}, u32[]{:S(2)}) collective-permute-start(bf16[160,768]{1,0:T(8,128)(2,1)} %get-tuple-element.53.refs_0_), channel_id=1, source_target_pairs={{0,1},{1,2},{2,3},{3,0},{4,5},{5,6},{6,7},{7,4},{8,9},{9,10},{10,1... | collective-permute-start | bytes 737288 | tf_op jit(solution)/shard_map/ppermute | solution.py:34
  12.1 24.5 %collective-permute-start.3 = (bf16[288,768]{1,0:T(8,128)(2,1)}, bf16[288,768]{1,0:T(8,128)(2,1)S(1)}, u32[]{:S(2)}, u32[]{:S(2)}) collective-permute-start(bf16[288,768]{1,0:T(8,128)(2,1)} %get-tuple-element.55), channel_id=1, source_target_pairs={{0,1},{1,2},{2,3},{3,0},{4,5},{5,6},{6,7},{7,4},{8,9},{9,10},{10,1... | collective-permute-start | bytes 1327112 | tf_op jit(solution)/shard_map/ppermute | solution.py:34
  13.6 35.7 %collective-permute-start.4 = (bf16[288,768]{1,0:T(8,128)(2,1)}, bf16[288,768]{1,0:T(8,128)(2,1)S(1)}, u32[]{:S(2)}, u32[]{:S(2)}) collective-permute-start(bf16[288,768]{1,0:T(8,128)(2,1)} %get-tuple-element.55), channel_id=1, source_target_pairs={{0,2},{1,3},{2,0},{3,1},{4,6},{5,7},{6,4},{7,5},{8,10},{9,11},{10,... | collective-permute-start | bytes 1327112 | tf_op jit(solution)/shard_map/ppermute | solution.py:34
  18.8 20.9 %copy-start.3 = (bf16[160,768]{1,0:T(8,128)(2,1)}, bf16[160,768]{1,0:T(8,128)(2,1)S(1)}, u32[]{:S(2)}) copy-start(bf16[160,768]{1,0:T(8,128)(2,1)S(1)} %collective-permute-done.2.refs_3_) | copy-start | bytes 737284
  18.8 31.8 %collective-permute-start.5 = (bf16[288,768]{1,0:T(8,128)(2,1)}, bf16[288,768]{1,0:T(8,128)(2,1)S(1)}, u32[]{:S(2)}, u32[]{:S(2)}) collective-permute-start(bf16[288,768]{1,0:T(8,128)(2,1)} %get-tuple-element.55), channel_id=1, source_target_pairs={{0,3},{1,0},{2,1},{3,2},{4,7},{5,4},{6,5},{7,6},{8,11},{9,8},{10,9... | collective-permute-start | bytes 1327112 | tf_op jit(solution)/shard_map/ppermute | solution.py:34
  33.0 6.7 %copy-start.4 = (bf16[160,768]{1,0:T(8,128)(2,1)}, bf16[160,768]{1,0:T(8,128)(2,1)S(1)}, u32[]{:S(2)}) copy-start(bf16[160,768]{1,0:T(8,128)(2,1)S(1)} %collective-permute-done.1.refs_2_) | copy-start | bytes 737284
  33.0 16.3 %collective-permute-start.9 = (bf16[96,768]{1,0:T(8,128)(2,1)}, bf16[96,768]{1,0:T(8,128)(2,1)S(1)}, u32[]{:S(2)}, u32[]{:S(2)}) collective-permute-start(bf16[96,768]{1,0:T(8,128)(2,1)} %get-tuple-element.58), channel_id=1, source_target_pairs={{0,1},{1,2},{2,3},{3,0},{4,5},{5,6},{6,7},{7,4},{8,9},{9,10},{10,1... | collective-permute-start | bytes 442376 | tf_op jit(solution)/shard_map/ppermute | solution.py:34
  33.1 6.6 %copy-start.5 = (bf16[160,768]{1,0:T(8,128)(2,1)}, bf16[160,768]{1,0:T(8,128)(2,1)S(1)}, u32[]{:S(2)}) copy-start(bf16[160,768]{1,0:T(8,128)(2,1)S(1)} %collective-permute-done.refs_1_) | copy-start | bytes 737284
  33.1 18.0 %collective-permute-start.10 = (bf16[96,768]{1,0:T(8,128)(2,1)}, bf16[96,768]{1,0:T(8,128)(2,1)S(1)}, u32[]{:S(2)}, u32[]{:S(2)}) collective-permute-start(bf16[96,768]{1,0:T(8,128)(2,1)} %get-tuple-element.58), channel_id=1, source_target_pairs={{0,2},{1,3},{2,0},{3,1},{4,6},{5,7},{6,4},{7,5},{8,10},{9,11},{10,... | collective-permute-start | bytes 442376 | tf_op jit(solution)/shard_map/ppermute | solution.py:34
  36.6 20.3 %copy-start.12 = (bf16[288,768]{1,0:T(8,128)(2,1)}, bf16[288,768]{1,0:T(8,128)(2,1)S(1)}, u32[]{:S(2)}) copy-start(bf16[288,768]{1,0:T(8,128)(2,1)S(1)} %collective-permute-done.3.refs_3_) | copy-start | bytes 1327108
  36.6 19.0 %collective-permute-start.6 = (bf16[288,768]{1,0:T(8,128)(2,1)S(1)}, bf16[288,768]{1,0:T(8,128)(2,1)S(1)}, u32[]{:S(2)}, u32[]{:S(2)}) collective-permute-start(bf16[288,768]{1,0:T(8,128)(2,1)S(1)} %collective-permute-done.3.refs_3_), channel_id=1, source_target_pairs={{0,4},{4,0},{1,5},{5,1},{2,6},{6,2},{3,7},{7,3},{8,12},{12,8},{9,1... | collective-permute-start | bytes 1327112 | tf_op jit(solution)/shard_map/ppermute | solution.py:38
  49.3 15.4 %copy-start.21 = (bf16[96,768]{1,0:T(8,128)(2,1)}, bf16[96,768]{1,0:T(8,128)(2,1)S(1)}, u32[]{:S(2)}) copy-start(bf16[96,768]{1,0:T(8,128)(2,1)S(1)} %collective-permute-done.9.refs_1_) | copy-start | bytes 442372
  49.3 4.8 %collective-permute-start.11 = (bf16[96,768]{1,0:T(8,128)(2,1)S(1)}, bf16[96,768]{1,0:T(8,128)(2,1)S(1)}, u32[]{:S(2)}, u32[]{:S(2)}) collective-permute-start(bf16[96,768]{1,0:T(8,128)(2,1)S(1)} %copy-done.27), channel_id=1, source_target_pairs={{0,3},{1,0},{2,1},{3,2},{4,7},{5,4},{6,5},{7,6},{8,11},{9,8},{10,9... | collective-permute-start | bytes 442376 | tf_op jit(solution)/shard_map/ppermute | solution.py:34
  49.4 7.6 %copy-start.13 = (bf16[288,768]{1,0:T(8,128)(2,1)}, bf16[288,768]{1,0:T(8,128)(2,1)S(1)}, u32[]{:S(2)}) copy-start(bf16[288,768]{1,0:T(8,128)(2,1)S(1)} %collective-permute-done.4.refs_4_) | copy-start | bytes 1327108
  49.4 7.5 %collective-permute-start.7 = (bf16[288,768]{1,0:T(8,128)(2,1)S(1)}, bf16[288,768]{1,0:T(8,128)(2,1)S(1)}, u32[]{:S(2)}, u32[]{:S(2)}) collective-permute-start(bf16[288,768]{1,0:T(8,128)(2,1)S(1)} %collective-permute-done.4.refs_4_), channel_id=1, source_target_pairs={{0,4},{4,0},{1,5},{5,1},{2,6},{6,2},{3,7},{7,3},{8,12},{12,8},{9,1... | collective-permute-start | bytes 1327112 | tf_op jit(solution)/shard_map/ppermute | solution.py:38
  50.6 6.3 %copy-start.14 = (bf16[288,768]{1,0:T(8,128)(2,1)}, bf16[288,768]{1,0:T(8,128)(2,1)S(1)}, u32[]{:S(2)}) copy-start(bf16[288,768]{1,0:T(8,128)(2,1)S(1)} %collective-permute-done.5.refs_5_) | copy-start | bytes 1327108
  50.6 6.3 %collective-permute-start.8 = (bf16[288,768]{1,0:T(8,128)(2,1)S(1)}, bf16[288,768]{1,0:T(8,128)(2,1)S(1)}, u32[]{:S(2)}, u32[]{:S(2)}) collective-permute-start(bf16[288,768]{1,0:T(8,128)(2,1)S(1)} %collective-permute-done.5.refs_5_), channel_id=1, source_target_pairs={{0,4},{4,0},{1,5},{5,1},{2,6},{6,2},{3,7},{7,3},{8,12},{12,8},{9,1... | collective-permute-start | bytes 1327112 | tf_op jit(solution)/shard_map/ppermute | solution.py:38
  51.1 13.5 %copy-start.22 = (bf16[96,768]{1,0:T(8,128)(2,1)}, bf16[96,768]{1,0:T(8,128)(2,1)S(1)}, u32[]{:S(2)}) copy-start(bf16[96,768]{1,0:T(8,128)(2,1)S(1)} %collective-permute-done.10.refs_2_) | copy-start | bytes 442372
  51.1 13.5 %collective-permute-start.12 = (bf16[96,768]{1,0:T(8,128)(2,1)S(1)}, bf16[96,768]{1,0:T(8,128)(2,1)S(1)}, u32[]{:S(2)}, u32[]{:S(2)}) collective-permute-start(bf16[96,768]{1,0:T(8,128)(2,1)S(1)} %collective-permute-done.9.refs_1_), channel_id=1, source_target_pairs={{0,4},{4,0},{1,5},{5,1},{2,6},{6,2},{3,7},{7,3},{8,12},{12,8},{9,1... | collective-permute-start | bytes 442376 | tf_op jit(solution)/shard_map/ppermute | solution.py:38
  54.1 10.5 %copy-start.23 = (bf16[96,768]{1,0:T(8,128)(2,1)}, bf16[96,768]{1,0:T(8,128)(2,1)S(1)}, u32[]{:S(2)}) copy-start(bf16[96,768]{1,0:T(8,128)(2,1)S(1)} %collective-permute-done.11.refs_3_) | copy-start | bytes 442372
  54.1 10.5 %collective-permute-start.13 = (bf16[96,768]{1,0:T(8,128)(2,1)S(1)}, bf16[96,768]{1,0:T(8,128)(2,1)S(1)}, u32[]{:S(2)}, u32[]{:S(2)}) collective-permute-start(bf16[96,768]{1,0:T(8,128)(2,1)S(1)} %collective-permute-done.10.refs_2_), channel_id=1, source_target_pairs={{0,4},{4,0},{1,5},{5,1},{2,6},{6,2},{3,7},{7,3},{8,12},{12,8},{9,1... | collective-permute-start | bytes 442376 | tf_op jit(solution)/shard_map/ppermute | solution.py:38
  55.6 1.3 copy-start.15
  55.6 9.1 %collective-permute-start.14 = (bf16[96,768]{1,0:T(8,128)(2,1)S(1)}, bf16[96,768]{1,0:T(8,128)(2,1)S(1)}, u32[]{:S(2)}, u32[]{:S(2)}) collective-permute-start(bf16[96,768]{1,0:T(8,128)(2,1)S(1)} %collective-permute-done.11.refs_3_), channel_id=1, source_target_pairs={{0,4},{4,0},{1,5},{5,1},{2,6},{6,2},{3,7},{7,3},{8,12},{12,8},{9,1... | collective-permute-start | bytes 442376 | tf_op jit(solution)/shard_map/ppermute | solution.py:38
  69.0 7.8 %collective-permute-start.15 = (bf16[128,768]{1,0:T(8,128)(2,1)}, bf16[128,768]{1,0:T(8,128)(2,1)S(1)}, u32[]{:S(2)}, u32[]{:S(2)}) collective-permute-start(bf16[128,768]{1,0:T(8,128)(2,1)} %get-tuple-element.60.refs_0_.refs_4_.moe_ref), channel_id=1, source_target_pairs={{0,1},{1,2},{2,3},{3,0},{4,5},{5,6},{6,7},{7,4},{8,9},{9,10},{10,1... | collective-permute-start | bytes 589832 | tf_op jit(solution)/shard_map/ppermute | solution.py:34
  69.1 11.5 %collective-permute-start.16 = (bf16[128,768]{1,0:T(8,128)(2,1)}, bf16[128,768]{1,0:T(8,128)(2,1)S(1)}, u32[]{:S(2)}, u32[]{:S(2)}) collective-permute-start(bf16[128,768]{1,0:T(8,128)(2,1)} %get-tuple-element.60.refs_0_.refs_4_.moe_ref), channel_id=1, source_target_pairs={{0,2},{1,3},{2,0},{3,1},{4,6},{5,7},{6,4},{7,5},{8,10},{9,11},{10,... | collective-permute-start | bytes 589832 | tf_op jit(solution)/shard_map/ppermute | solution.py:34
  71.5 9.7 %collective-permute-start.17 = (bf16[128,768]{1,0:T(8,128)(2,1)}, bf16[128,768]{1,0:T(8,128)(2,1)S(1)}, u32[]{:S(2)}, u32[]{:S(2)}) collective-permute-start(bf16[128,768]{1,0:T(8,128)(2,1)} %get-tuple-element.60.refs_0_.refs_4_.moe_ref), channel_id=1, source_target_pairs={{0,3},{1,0},{2,1},{3,2},{4,7},{5,4},{6,5},{7,6},{8,11},{9,8},{10,9... | collective-permute-start | bytes 589832 | tf_op jit(solution)/shard_map/ppermute | solution.py:34
  76.9 4.3 %copy-start.6 = (bf16[128,768]{1,0:T(8,128)(2,1)}, bf16[128,768]{1,0:T(8,128)(2,1)S(1)}, u32[]{:S(2)}) copy-start(bf16[128,768]{1,0:T(8,128)(2,1)S(1)} %collective-permute-done.15.refs_1_.refs_5_) | copy-start | bytes 589828
  127.1 37.2 %all-to-all-start.1 = ((bf16[32,24,1664]{2,1,0:T(8,128)(2,1)}), bf16[32,24,1664]{2,1,0:T(8,128)(2,1)S(1)}, u32[]{:S(2)}, u32[]{:S(2)}) async-start(bf16[32,24,1664]{2,1,0:T(8,128)(2,1)} %bitcast.54), calls=%async_computation.1 | async-start | bytes 5111808 | tf_op jit(solution)/shard_map/all_to_all | solution.py:756
  164.3 1.5 copy-start
  165.7 54.9 %all-to-all-start.3 = ((bf16[32,24,1536]{2,1,0:T(8,128)(2,1)}), bf16[32,24,1536]{2,1,0:T(8,128)(2,1)}, u32[]{:S(2)}, u32[]{:S(2)}) async-start(bf16[32,24,1536]{2,1,0:T(8,128)(2,1)} %bitcast.67), calls=%async_computation.3 | async-start | bytes 4718592 | tf_op jit(solution)/shard_map/all_to_all | solution.py:756
  185.3 15.1 %collective-permute-start.18 = (bf16[384,768]{1,0:T(8,128)(2,1)}, bf16[384,768]{1,0:T(8,128)(2,1)S(1)}, u32[]{:S(2)}, u32[]{:S(2)}) collective-permute-start(bf16[384,768]{1,0:T(8,128)(2,1)} %get-tuple-element.70), channel_id=1, source_target_pairs={{0,3},{1,0},{2,1},{3,2},{4,7},{5,4},{6,5},{7,6},{8,11},{9,8},{10,9... | collective-permute-start | bytes 1769480 | tf_op jit(solution)/shard_map/ppermute | solution.py:34
  187.5 16.0 %collective-permute-start.19 = (bf16[384,768]{1,0:T(8,128)(2,1)}, bf16[384,768]{1,0:T(8,128)(2,1)S(1)}, u32[]{:S(2)}, u32[]{:S(2)}) collective-permute-start(bf16[384,768]{1,0:T(8,128)(2,1)} %get-tuple-element.71), channel_id=1, source_target_pairs={{0,2},{1,3},{2,0},{3,1},{4,6},{5,7},{6,4},{7,5},{8,10},{9,11},{10,... | collective-permute-start | bytes 1769480 | tf_op jit(solution)/shard_map/ppermute | solution.py:34
  187.5 29.0 %collective-permute-start.20 = (bf16[384,768]{1,0:T(8,128)(2,1)}, bf16[384,768]{1,0:T(8,128)(2,1)S(1)}, u32[]{:S(2)}, u32[]{:S(2)}) collective-permute-start(bf16[384,768]{1,0:T(8,128)(2,1)} %get-tuple-element.72), channel_id=1, source_target_pairs={{0,1},{1,2},{2,3},{3,0},{4,5},{5,6},{6,7},{7,4},{8,9},{9,10},{10,1... | collective-permute-start | bytes 1769480 | tf_op jit(solution)/shard_map/ppermute | solution.py:34
  200.4 16.0 %copy-start.9 = (bf16[384,768]{1,0:T(8,128)(2,1)}, bf16[384,768]{1,0:T(8,128)(2,1)S(1)}, u32[]{:S(2)}) copy-start(bf16[384,768]{1,0:T(8,128)(2,1)S(1)} %collective-permute-done.18.refs_1_) | copy-start | bytes 1769476
  203.4 13.0 %copy-start.10 = (bf16[384,768]{1,0:T(8,128)(2,1)}, bf16[384,768]{1,0:T(8,128)(2,1)S(1)}, u32[]{:S(2)}) copy-start(bf16[384,768]{1,0:T(8,128)(2,1)S(1)} %collective-permute-done.19.refs_2_) | copy-start | bytes 1769476
  220.6 22.2 %all-to-all-start.2 = ((bf16[32,16,768]{2,1,0:T(8,128)(2,1)}), bf16[32,16,768]{2,1,0:T(8,128)(2,1)S(1)}, u32[]{:S(2)}, u32[]{:S(2)}) async-start(bf16[32,16,768]{2,1,0:T(8,128)(2,1)} %bitcast.60), calls=%async_computation.2 | async-start | bytes 1572864 | tf_op jit(solution)/shard_map/all_to_all | solution.py:756
  234.5 8.3 %collective-permute-start.21 = (bf16[128,896]{1,0:T(8,128)(2,1)}, bf16[128,896]{1,0:T(8,128)(2,1)S(1)}, u32[]{:S(2)}, u32[]{:S(2)}) collective-permute-start(bf16[128,896]{1,0:T(8,128)(2,1)} %get-tuple-element.80), channel_id=1, source_target_pairs={{0,3},{1,0},{2,1},{3,2},{4,7},{5,4},{6,5},{7,6},{8,11},{9,8},{10,9... | collective-permute-start | bytes 688136 | tf_op jit(solution)/shard_map/ppermute | solution.py:34
  235.1 8.4 %collective-permute-start.22 = (bf16[128,896]{1,0:T(8,128)(2,1)}, bf16[128,896]{1,0:T(8,128)(2,1)S(1)}, u32[]{:S(2)}, u32[]{:S(2)}) collective-permute-start(bf16[128,896]{1,0:T(8,128)(2,1)} %get-tuple-element.81), channel_id=1, source_target_pairs={{0,2},{1,3},{2,0},{3,1},{4,6},{5,7},{6,4},{7,5},{8,10},{9,11},{10,... | collective-permute-start | bytes 688136 | tf_op jit(solution)/shard_map/ppermute | solution.py:34
  235.1 14.2 %collective-permute-start.23 = (bf16[128,896]{1,0:T(8,128)(2,1)}, bf16[128,896]{1,0:T(8,128)(2,1)S(1)}, u32[]{:S(2)}, u32[]{:S(2)}) collective-permute-start(bf16[128,896]{1,0:T(8,128)(2,1)} %get-tuple-element.82), channel_id=1, source_target_pairs={{0,1},{1,2},{2,3},{3,0},{4,5},{5,6},{6,7},{7,4},{8,9},{9,10},{10,1... | collective-permute-start | bytes 688136 | tf_op jit(solution)/shard_map/ppermute | solution.py:34
  242.8 6.5 %copy-start.1 = (bf16[32,16,768]{2,1,0:T(8,128)(2,1)}, bf16[32,16,768]{2,1,0:T(8,128)(2,1)S(1)}, u32[]{:S(2)}) copy-start(bf16[32,16,768]{2,1,0:T(8,128)(2,1)S(1)} %all-to-all-done.2) | copy-start | bytes 2359300
  242.8 6.5 %copy-start.18 = (bf16[128,896]{1,0:T(8,128)(2,1)}, bf16[128,896]{1,0:T(8,128)(2,1)S(1)}, u32[]{:S(2)}) copy-start(bf16[128,896]{1,0:T(8,128)(2,1)S(1)} %collective-permute-done.21.refs_1_) | copy-start | bytes 688132
  243.5 5.8 %copy-start.19 = (bf16[128,896]{1,0:T(8,128)(2,1)}, bf16[128,896]{1,0:T(8,128)(2,1)S(1)}, u32[]{:S(2)}) copy-start(bf16[128,896]{1,0:T(8,128)(2,1)S(1)} %collective-permute-done.22.refs_2_) | copy-start | bytes 688132
  262.0 6.8 %collective-permute-start.24 = (bf16[1536,768]{1,0:T(8,128)(2,1)}, bf16[1536,768]{1,0:T(8,128)(2,1)}, u32[]{:S(2)}, u32[]{:S(2)}) collective-permute-start(bf16[1536,768]{1,0:T(8,128)(2,1)} %get-tuple-element.90), channel_id=1, source_target_pairs={{0,4},{4,0},{1,5},{5,1},{2,6},{6,2},{3,7},{7,3},{8,12},{12,8},{9,1... | collective-permute-start | bytes 7077896 | tf_op jit(solution)/shard_map/ppermute | solution.py:38
  262.6 6.3 %copy-start.2 = (bf16[1536,768]{1,0:T(8,128)(2,1)S(1)}, bf16[1536,768]{1,0:T(8,128)(2,1)}, u32[]{:S(2)}) copy-start(bf16[1536,768]{1,0:T(8,128)(2,1)} %get-tuple-element.89) | copy-start | bytes 7077892
  267.0 1.8 collective-permute-start.25
  (9 other events, 6.6 us)
where the time goes:
time: 346 us; the launch traced here: 345 us
  blocking collectives  110 us (32%)
  Pallas kernels  78.2 us (23%)
  waiting for transfers between devices  73.7 us (21%)
  starting transfers between devices  53.1 us (15%)
  local copies, waits for them, and re-layouts  17.5 us (5%)
  other arithmetic  8.9 us (3%)
    all_to_all x1, blocking collectives, layer(): spread = lax.all_to_all(paired, ('y', 'x', 'z'), 0, 0, tiled=True)  43.7 us
    ppermute x18, waiting for transfers between devices, shift_x(): lax.ppermute(block, 'x', [(i, (i + step) % ranks) for i in range(ranks)])  43.2 us
    all_to_all x1, blocking collectives, to_owners(): return lax.all_to_all(outgoing, ('y', 'z', 'c'), 0, 0, tiled=True)  41.2 us
    ppermute x18, starting transfers between devices, shift_x(): lax.ppermute(block, 'x', [(i, (i + step) % ranks) for i in range(ranks)])  30.3 us
    all_to_all x3, waiting for transfers between devices, to_owners(): return lax.all_to_all(outgoing, ('y', 'z', 'c'), 0, 0, tiled=True)  28.8 us
    all_to_all x1, blocking collectives, layer(): lax.all_to_all(jnp.broadcast_to(mine[None], (32, piece, wide)).reshape(32...  25.4 us
    all_to_all x3, starting transfers between devices, to_owners(): return lax.all_to_all(outgoing, ('y', 'z', 'c'), 0, 0, tiled=True)  17.2 us
    pallas_call x1, Pallas kernels, experts_back(): pl.pallas_call(functools.partial(expert_back_kernel, capacity), grid=(2,)...  13.3 us
  transfers between devices with their start and end apart: 29, of which 14 were waited for; matrix products, arithmetic and copies ran while one was open for 4% of the time, Pallas kernels for 16%

commit v1 on v0

--- a/solution.py
+++ b/solution.py
@@ -42,28 +42,34 @@
     return [block, shift_x(block, 1), shift_x(block, 2), shift_x(block, 3)]
 
 
-def head_kernel(core_ref, routes_ref, one_ref, two_ref, bias_ref, router_ref, cotangent_ref, *refs):
-    mats, line_ref, qkv_ref, out_ref, held, sems = refs[:4], *refs[4:9]
+def line_kernel(routes_ref, gains_ref, bias_ref, router_ref, cotangent_ref, line_ref, held, sem):
     f32 = jnp.float32
     tokens = cotangent_ref.shape[0]
+    copy = pltpu.make_async_copy(cotangent_ref, line_ref.at[pl.ds(0, tokens)], sem)
+    copy.start()
+    held[...] = jnp.zeros_like(held)
+    held[0:2, : gains_ref.shape[1]] = gains_ref[...].astype(f32)
+    held[2:5, : bias_ref.shape[1]] = bias_ref[...].astype(f32)
+    held[5:7, :tokens] = routes_ref[...].astype(f32)
+    width = router_ref.shape[1]
+    for b in range(router_ref.shape[0] // 16):
+        part = router_ref[16 * b : 16 * b + 16, :].astype(f32)
+        held[16:32, width * b : width * (b + 1)] = part
+    line_ref[tokens:, :] = held[...].astype(jnp.bfloat16)
+    copy.wait()
+
+
+def pack_kernel(count, core_ref, *refs):
+    mats, out_ref, sems = refs[:count], refs[count + 1], refs[count + 2]
     half = mats[0].shape[0] // 2
     start = pl.multiple_of(core_ref[0] * half, half)
-    spots = [qkv_ref.at[pl.ds(k * half, half)] for k in range(3)] + [out_ref]
     copies = start_copies(
-        [(cotangent_ref, line_ref.at[pl.ds(0, tokens)])]
-        + [(m.at[pl.ds(start, half)], spot) for m, spot in zip(mats, spots)],
+        [
+            (m.at[pl.ds(start, half)], out_ref.at[pl.ds(k * half, half)])
+            for k, m in enumerate(mats)
+        ],
         sems,
     )
-    held[...] = jnp.zeros_like(held)
-    held[0:1, : one_ref.shape[1]] = one_ref[...].astype(f32)
-    held[1:2, : two_ref.shape[1]] = two_ref[...].astype(f32)
-    held[2:5, : bias_ref.shape[1]] = bias_ref[...].astype(f32)
-    held[5:7, :tokens] = routes_ref[...].astype(f32)
-    experts_all = router_ref.shape[1]
-    for b in range(router_ref.shape[0] // 16):
-        part = router_ref[16 * b : 16 * b + 16, :].astype(f32)
-        held[16:32, experts_all * b : experts_all * (b + 1)] = part
-    line_ref[tokens:, :] = held[...].astype(jnp.bfloat16)
     for c in copies:
         c.wait()
 
@@ -107,6 +113,27 @@
     down = lax.broadcasted_iota(jnp.int32, (n, n), 0)
     across = lax.broadcasted_iota(jnp.int32, (n, n), 1)
     return jnp.sum(jnp.where(down == across, row, jnp.zeros_like(row)), axis=1, keepdims=True)
+
+
+def diagonal_sums(scores):
+    n = scores.shape[0]
+    down = lax.broadcasted_iota(jnp.int32, (n, n), 0)
+    step = 1
+    while step < n:
+        turned = pltpu.roll(scores, n - step, axis=1)
+        scores = jnp.where((down & step) != 0, turned, scores)
+        step *= 2
+    return jnp.sum(scores, axis=0, keepdims=True)
+
+
+def bucket_marks():
+    shape = (128, 128)
+    distance = (128 - lax.broadcasted_iota(jnp.int32, shape, 0)) & 127
+    bucket = jnp.zeros(shape, jnp.int32)
+    for edge in bucket_edges:
+        bucket = bucket + (distance >= edge).astype(jnp.int32)
+    mark = bucket == lax.broadcasted_iota(jnp.int32, shape, 1)
+    return mark.astype(jnp.float32).astype(jnp.bfloat16)
 
 
 LAST = (((1,), (1,)), ((), ()))
@@ -185,11 +212,12 @@
 ):
     f32, bf16 = jnp.float32, jnp.bfloat16
     homes, weights = refs[:4], refs[4:8]
-    result_ref, tokens_out, kept_ref, given_ref, scores_ref, router_out, gains_out = refs[8:15]
-    held, grads_ref, sems = refs[15:18]
+    result_ref, tokens_out, kept_ref, given_ref = refs[8:12]
+    held, grads_ref, small_ref, sems = refs[12:16]
     copies = start_copies([(w, held.at[i]) for i, w in enumerate(weights)], sems)
     features = tokens_ref.shape[1]
     core = core_ref[0]
+    small_ref[...] = jnp.zeros_like(small_ref)
 
     def leave(mat, left, right):
         grad = lax.dot_general(left, right, FIRST, preferred_element_type=f32).astype(bf16)
@@ -200,6 +228,12 @@
             at = (mat * 4 + x) * 96
             kept_ref[at : at + 96, :features] = jnp.where(core == 0, low, high)
             given_ref[at : at + 96, :features] = jnp.where(core == 0, high, low)
+
+    def leave_gain(row, gain):
+        for x in range(4):
+            at = (4 + x) * 96 + row
+            small_ref[0, at : at + 1, :] = gain[:, x * 192 : x * 192 + 128]
+            small_ref[0, at + 1 : at + 2, :64] = gain[:, x * 192 + 128 : x * 192 + 192]
 
     home = homes[0][...].astype(f32)
     for piece in homes[1:]:
@@ -213,7 +247,7 @@
         for k in range(2)
     ]
     moe = moe_ref[...]
-    logits = jnp.dot(moe, router_ref[...], preferred_element_type=f32)
+    logits = lax.dot_general(moe, router_ref[...], LAST, preferred_element_type=f32)
     ids = [to_column(ids_ref[k : k + 1, : tail.shape[0]]) for k in range(2)]
     gates = gate_pair(chosen_logit(logits, ids[0]), chosen_logit(logits, ids[1]))
     mix = gates[0] * grad_gates[0] + gates[1] * grad_gates[1]
@@ -225,13 +259,17 @@
     slot = lax.broadcasted_iota(jnp.int32, (rows_ref.shape[0], tail.shape[0]), 0)
     pick = ((slot == spots_ref[0:1]) | (slot == spots_ref[1:2])).astype(f32).astype(bf16)
     grad_moe = lax.dot_general(pick, rows_ref[...], FIRST, preferred_element_type=f32)
-    grad_moe = grad_moe + lax.dot_general(
-        grad_logits, router_ref[...], LAST, preferred_element_type=f32
-    )
-    router_out[...] = lax.dot_general(moe, grad_logits, FIRST, preferred_element_type=f32)
+    grad_moe = grad_moe + jnp.dot(grad_logits, router_ref[...], preferred_element_type=f32)
+    grad_router = lax.dot_general(moe, grad_logits, FIRST, preferred_element_type=f32)
+    for x in range(4):
+        for side in range(2):
+            begin = x * 192 + side * 96
+            small_ref[side, x * 96 : x * 96 + 96, : logits.shape[1]] = grad_router[
+                begin : begin + 96, :
+            ]
     scale = norm_scale(middle)
     normed = middle * scale
-    gains_out[1:2, :] = jnp.sum(grad_moe * normed, axis=0, keepdims=True)
+    leave_gain(2, jnp.sum(grad_moe * normed, axis=0, keepdims=True))
     inner = grad_moe * gain_two_ref[...].astype(f32)
     grad_middle = cotangent_ref[...].astype(f32) + scale * (
         inner - normed * jnp.mean(inner * normed, axis=1, keepdims=True)
@@ -240,7 +278,7 @@
     leave(3, attended_ref[...], branch)
     copies[3].wait()
     grad_attended = lax.dot_general(branch, held[3], LAST, preferred_element_type=f32).astype(bf16)
-    grad_q, grad_k, grad_v = [], [], []
+    grad_q, grad_k, grad_v, diagonals = [], [], [], []
     for pair in range(probs_ref.shape[0] // 2):
         lanes = slice(pair * 128, pair * 128 + 128)
         q, k, v = q_ref[:, lanes], k_ref[:, lanes], v_ref[:, lanes]
@@ -257,7 +295,7 @@
             grad_scores = (
                 probs * (grad_probs - jnp.sum(probs * grad_probs, axis=1, keepdims=True))
             ).astype(bf16)
-            scores_ref[h] = grad_scores
+            diagonals.append(diagonal_sums(grad_scores.astype(f32)))
             parts[0] = parts[0] + jnp.dot(
                 grad_scores, head_half(k, side), preferred_element_type=f32
             )
@@ -267,6 +305,16 @@
         grad_q.append((parts[0] * 0.125).astype(bf16))
         grad_k.append((parts[1] * 0.125).astype(bf16))
         grad_v.append(parts[2].astype(bf16))
+    left = jnp.concatenate(diagonals, axis=0)
+    grad_bias = jnp.zeros((left.shape[0], 128), f32)
+    for _ in range(3):
+        part = left.astype(bf16)
+        left = left - part.astype(f32)
+        grad_bias = grad_bias + jnp.dot(part, bucket_marks(), preferred_element_type=f32)
+    per = left.shape[0] // 4
+    for x in range(4):
+        at = (4 + x) * 96 + 4
+        small_ref[0, at : at + per, :] = grad_bias[x * per : x * per + per, :]
     hidden = hidden_ref[...]
     grad_hidden = jnp.zeros(hidden.shape, f32)
     for n, parts in enumerate((grad_q, grad_k, grad_v)):
@@ -279,11 +327,14 @@
     x = tokens_ref[...].astype(f32)
     scale = norm_scale(x)
     normed = x * scale
-    gains_out[0:1, :] = jnp.sum(grad_hidden * normed, axis=0, keepdims=True)
+    leave_gain(0, jnp.sum(grad_hidden * normed, axis=0, keepdims=True))
     inner = grad_hidden * gain_one_ref[...].astype(f32)
     tokens_out[...] = grad_middle + scale * (
         inner - normed * jnp.mean(inner * normed, axis=1, keepdims=True)
     )
+    low, high = small_ref[0], small_ref[1]
+    kept_ref[:, features:] = jnp.where(core == 0, low, high).astype(bf16)
+    given_ref[:, features:] = jnp.where(core == 0, high, low).astype(bf16)
 
 
 ANYWHERE = pl.BlockSpec(memory_space=pl.ANY)
@@ -292,24 +343,31 @@
 ROOM = pltpu.CompilerParams(vmem_limit_bytes=56 * 1024 * 1024)
 
 
-def head(core, routes, gain_one, gain_two, bias, router, cotangent, mats):
-    bf16 = jnp.bfloat16
+def make_line(routes, gains, bias, router, cotangent):
+    tokens, cols = cotangent.shape
+    return pl.pallas_call(
+        line_kernel,
+        out_shape=jax.ShapeDtypeStruct((tokens + 32, cols), jnp.bfloat16),
+        in_specs=[WHOLE] * 4 + [ANYWHERE],
+        out_specs=WHOLE,
+        scratch_shapes=[pltpu.VMEM((32, cols), jnp.float32), pltpu.SemaphoreType.DMA],
+        compiler_params=ROOM,
+        name="line",
+    )(routes, gains, bias, router, cotangent)
+
+
+def pack(core, mats, after):
     rows, cols = mats[0].shape
-    half = rows // 2
-    tokens = cotangent.shape[0]
-    return pl.pallas_call(
-        head_kernel,
-        out_shape=[
-            jax.ShapeDtypeStruct((tokens + 32, cols), bf16),
-            jax.ShapeDtypeStruct((3 * half, cols), bf16),
-            jax.ShapeDtypeStruct((half, cols), bf16),
-        ],
-        in_specs=[SCALARS] + [WHOLE] * 5 + [ANYWHERE] * 5,
-        out_specs=[WHOLE] * 3,
-        scratch_shapes=[pltpu.VMEM((32, cols), jnp.float32), pltpu.SemaphoreType.DMA((5,))],
-        compiler_params=ROOM,
-        name="head",
-    )(core[None], routes, gain_one, gain_two, bias, router, cotangent, *mats)
+    count = len(mats)
+    return pl.pallas_call(
+        functools.partial(pack_kernel, count),
+        out_shape=jax.ShapeDtypeStruct((count * rows // 2, cols), jnp.bfloat16),
+        in_specs=[SCALARS] + [ANYWHERE] * (count + 1),
+        out_specs=WHOLE,
+        scratch_shapes=[pltpu.SemaphoreType.DMA((count,))],
+        compiler_params=ROOM,
+        name="pack",
+    )(core[None], *mats, after)
 
 
 def attend(where, tokens, gain, bias, mats, near, far, after):
@@ -345,7 +403,7 @@
 
 
 def backward(core, *arrays):
-    tokens, router_w, probs = arrays[0], arrays[5], arrays[13]
+    tokens = arrays[0]
     count, features = tokens.shape
     bf16, f32 = jnp.bfloat16, jnp.float32
     shape = jax.ShapeDtypeStruct
@@ -354,22 +412,56 @@
         out_shape=[
             shape((count, features), bf16),
             shape((count, features), f32),
-            shape((2 * features, features), bf16),
-            shape((2 * features, features), bf16),
-            shape(probs.shape, bf16),
-            shape(router_w.shape, f32),
-            shape((2, features), f32),
+            shape((2 * features, features + 128), bf16),
+            shape((2 * features, features + 128), bf16),
         ],
         in_specs=[SCALARS] + [WHOLE] * 20 + [ANYWHERE] * 4,
-        out_specs=[WHOLE] * 7,
+        out_specs=[WHOLE] * 4,
         scratch_shapes=[
             pltpu.VMEM((4, features, features), bf16),
             pltpu.VMEM((features, features), bf16),
+            pltpu.VMEM((2, 2 * features, 128), f32),
             pltpu.SemaphoreType.DMA((4,)),
         ],
         compiler_params=ROOM,
         name="backward",
     )(core, *arrays)
+
+
+def finish_kernel(core_ref, own_ref, other_ref, *refs):
+    mats, (router_out, gains_out, bias_out) = refs[:4], refs[4:]
+    f32 = jnp.float32
+    core = core_ref[0]
+    half = own_ref.shape[0] // 4
+    features = mats[0].shape[1]
+    own, other = own_ref[...].astype(f32), other_ref[...].astype(f32)
+    low, high = jnp.where(core == 0, own, other), jnp.where(core == 0, other, own)
+    for k, out in enumerate(mats):
+        here = slice(k * half, (k + 1) * half)
+        out[:half, :] = low[here, :features]
+        out[half:, :] = high[here, :features]
+    wide = router_out.shape[1]
+    router_out[:half, :] = low[:half, features : features + wide]
+    router_out[half:, :] = high[:half, features : features + wide]
+    small = low[half : 2 * half, features:]
+    for k in range(2):
+        gains_out[k : k + 1, :128] = small[2 * k : 2 * k + 1, :]
+        gains_out[k : k + 1, 128:] = small[2 * k + 1 : 2 * k + 2, :64]
+    bias_out[...] = small[4 : 4 + bias_out.shape[0], : bias_out.shape[1]]
+
+
+def finish(core, own, other, shard_rows, experts_all, bias_shape):
+    features = own.shape[1] - 128
+    shape = lambda *s: jax.ShapeDtypeStruct(s, jnp.float32)
+    return pl.pallas_call(
+        finish_kernel,
+        out_shape=[shape(shard_rows, features)] * 4
+        + [shape(shard_rows, experts_all), shape(2, shard_rows), shape(*bias_shape)],
+        in_specs=[SCALARS] + [WHOLE] * 2,
+        out_specs=[WHOLE] * 7,
+        compiler_params=ROOM,
+        name="finish",
+    )(core, own, other)
 
 
 def picks_of(places, e, rows):
@@ -440,7 +532,7 @@
 
 
 def dispatch_kernel(places_ref, *refs):
-    pieces, out_ref = refs[:4], refs[4]
+    pieces, out_ref = refs[:4], refs[5]
     rows = out_ref.shape[0]
     features = pieces[0].shape[1]
     line = jnp.concatenate([p[...] for p in pieces], axis=0)
@@ -450,15 +542,15 @@
         ).astype(jnp.bfloat16)
 
 
-def dispatch(places, pieces, rows):
+def dispatch(places, pieces, rows, after):
     return pl.pallas_call(
         dispatch_kernel,
         out_shape=jax.ShapeDtypeStruct((rows, 2 * pieces[0].shape[1]), jnp.bfloat16),
-        in_specs=[WHOLE] * 5,
+        in_specs=[WHOLE] * 5 + [ANYWHERE],
         out_specs=WHOLE,
         compiler_params=ROOM,
         name="dispatch",
-    )(places, *pieces)
+    )(places, *pieces, after)
 
 
 def chosen_logit(logits, ids):
@@ -534,7 +626,9 @@
         ids = ids_ref[at, :].astype(f32)
         lanes = lax.broadcasted_iota(i32, ids.shape, 1)
         other = jnp.sum(jnp.where(lanes == e, ids, 0.0), axis=1, keepdims=True).astype(i32) - own
-        logits = jnp.dot(x_ref[at, :], router_ref[...], preferred_element_type=f32)
+        logits = lax.dot_general(
+            x_ref[at, :], router_ref[...], LAST, preferred_element_type=f32
+        )
         gate, _ = gate_pair(chosen_logit(logits, own), chosen_logit(logits, other))
         grown = (gate * g_ref[at, :].astype(f32)).astype(bf16)
         arr_ref[0, at, :] = grown
@@ -658,7 +752,9 @@
     tail_lane = lax.broadcasted_iota(jnp.int32, (tokens, 128), 1)
     for r in range(4):
         here = slice(r * tokens, (r + 1) * tokens)
-        logits = jnp.dot(moes[r][...], router_ref[...], preferred_element_type=f32)
+        logits = lax.dot_general(
+            moes[r][...], router_ref[...], LAST, preferred_element_type=f32
+        )
         ids = [to_column(ids_ref[k : k + 1, here]) for k in range(2)]
         gates = gate_pair(chosen_logit(logits, ids[0]), chosen_logit(logits, ids[1]))
         total = jnp.zeros((tokens, features), f32)
@@ -717,7 +813,6 @@
     bucket_count = rel_bias.shape[1]
     head_count = 4 * rel_bias.shape[0]
     capacity = 3 * row_count // expert_count
-    bias_size = rel_bias.size
     f32 = jnp.float32
     bf16 = jnp.bfloat16
 
@@ -727,19 +822,11 @@
     owners = expert_count // 2
     slot_rows = owners * 4 * capacity
 
-    line, sent_qkv, sent_out = head(
-        core,
-        routes.T,
-        gain_attn[None],
-        gain_moe[None],
-        rel_bias,
-        w_router,
-        cotangent,
-        (w_query, w_key, w_value, w_output),
+    line = make_line(
+        routes.T, jnp.stack([gain_attn, gain_moe]), rel_bias, w_router.T, cotangent
     )
     line_grads = along_x(line)
-    near_qkv = along_x(sent_qkv)[1:]
-    near_out = along_x(sent_out)[1:]
+    near_qkv = along_x(pack(core, (w_query, w_key, w_value), line))[1:]
     order = (shard - jnp.arange(4)) % 4
     small = jnp.take(jnp.stack([p[row_count:] for p in line_grads]), order, axis=0)
     gain_one = small[:, 0, :shard_rows].reshape(1, features)
@@ -747,9 +834,9 @@
     bias_table = small[:, 2:5, :bucket_count].reshape(head_count, bucket_count)
     router_w = (
         small[:, 16:]
-        .reshape(4, 16, shard_rows // 16, expert_count)
-        .transpose(0, 2, 1, 3)
-        .reshape(features, expert_count)
+        .reshape(4, 16, expert_count // 16, shard_rows)
+        .transpose(2, 1, 0, 3)
+        .reshape(expert_count, features)
     )
 
     def to_owners(outgoing):
@@ -759,6 +846,7 @@
         line_grads, slot_rows, capacity, row_count
     )
     grad_wide = to_owners(outgoing_grads)
+    near_out = along_x(pack(core, (w_output,), outgoing_grads))[1:]
     first_expert = 2 * lax.axis_index(("y", "z", "c")).astype(jnp.int32)
 
     segments = row_segments(seq_lengths[0], row_count)
@@ -783,7 +871,7 @@
     )
 
     line_moe = along_x(moe_in)
-    arrived = to_owners(dispatch(places, line_moe, slot_rows))
+    arrived = to_owners(dispatch(places, line_moe, slot_rows, grad_wide))
     ret, active, rise = experts(arrived, w_in, w_out)
     returned = to_owners(ret)
     grad_pre, grad_arrived, *blocks = experts_back(
@@ -795,7 +883,7 @@
     back_rows = to_owners(rows_home)
     bundle = combine(places, ids, router_w, returned, line_grads, line_moe, rows_home)
     homes = [bundle[0]] + [shift_x(bundle[r], -r) for r in range(1, 4)]
-    result, grad_tokens, kept, given, grad_scores, grad_router, grad_gains = backward(
+    result, grad_tokens, kept, given = backward(
         core[None],
         tokens,
         cotangent,
@@ -819,40 +907,22 @@
         value_w,
         output_w,
     )
-    grad_bias = jnp.einsum("hij,ijb->hb", grad_scores, onehot, preferred_element_type=f32)
-
     piece = shard_rows // 8
     wide = features + 128
-    bias_column = jnp.pad(grad_bias.reshape(4, bias_size), ((0, 0), (0, shard_rows - bias_size)))
-    small_grads = jnp.concatenate(
-        [grad_router, grad_gains.T, bias_column.reshape(-1, 1)], axis=1
-    ).astype(bf16)
-    small_grads = jnp.pad(small_grads, ((0, 0), (0, 128 - small_grads.shape[1])))
-    small_grads = small_grads.reshape(4, 2, shard_rows // 2, 128)
-
-    def small_half(side):
-        part = lax.dynamic_index_in_dim(small_grads, side, 1, keepdims=False).reshape(-1, 128)
-        return jnp.pad(part, ((0, kept.shape[0] - part.shape[0]), (0, 0)))
-
-    pairs = ((kept, swap_core(given)), (small_half(core), swap_core(small_half(1 - core))))
-    paired = jnp.concatenate(
-        [(a.astype(f32) + b.astype(f32)).astype(bf16) for a, b in pairs], axis=1
-    )
+    paired = (kept.astype(f32) + swap_core(given).astype(f32)).astype(bf16)
     spread = lax.all_to_all(paired, ("y", "x", "z"), 0, 0, tiled=True)
     mine = jnp.sum(spread.reshape(64, piece, wide).astype(f32), axis=0).astype(bf16)
-    totals = lax.all_to_all(
-        jnp.broadcast_to(mine[None], (32, piece, wide)).reshape(32 * piece, wide),
-        ("y", "c", "z"),
+    half = lax.all_to_all(
+        jnp.broadcast_to(mine[None], (16, piece, wide)).reshape(16 * piece, wide),
+        ("y", "z"),
         0,
         0,
         tiled=True,
-    ).reshape(4, shard_rows, wide)
-    small_totals = totals[0, :, features:].astype(f32)
-    totals = totals[:, :, :features].astype(f32)
-    router_total = small_totals[:, :expert_count]
-    gain_one_total = small_totals[:, expert_count]
-    gain_two_total = small_totals[:, expert_count + 1]
-    bias_total = small_totals[:bias_size, expert_count + 2].reshape(rel_bias.shape)
+    )
+    *totals, router_total, gain_totals, bias_total = finish(
+        core[None], half, swap_core(half), shard_rows, expert_count, rel_bias.shape
+    )
+    gain_one_total, gain_two_total = gain_totals[0], gain_totals[1]
     return (
         result,
         grad_tokens,

time: 346 us -> 315 us (0.910)
  blocking collectives: 110 us -> 95.9 us
  waiting for transfers between devices: 73.7 us -> 63 us
  starting transfers between devices: 53.1 us -> 43.4 us
  Pallas kernels: 78.2 us -> 86.5 us
    all_to_all x3, waiting for transfers between devices: 28.8 us -> 6.77 us  [to_owners(): return lax.all_to_all(outgoing, ('y', 'z', 'c'), 0, 0, tiled=True)]
    ppermute x18, starting transfers between devices: 30.3 us -> 15.8 us  [shift_x(): lax.ppermute(block, 'x', [(i, (i + step) % ranks) for i in range(ranks)])]
    all_to_all x1, blocking collectives: 25.4 us -> 13.1 us  [layer(): lax.all_to_all(jnp.broadcast_to(mine[None], (16, piece, wide)).reshape(16...]
    ppermute x18, waiting for transfers between devices: 43.2 us -> 49.6 us  [shift_x(): lax.ppermute(block, 'x', [(i, (i + step) % ranks) for i in range(ranks)])]
    pallas_call x1 -> x4, Pallas kernels: 3.02 us -> 8.63 us  [the longest x2 3.41 us: pack(): pl.pallas_call(functools.partial(pack_kernel, count), out_shape=jax.Shape...]
    ppermute x8, waiting for transfers between devices: 1.71 us -> 6.72 us  [swap_core(): return lax.ppermute(block, 'c', [(0, 1), (1, 0)])]
    unnamed x58 -> x51, local copies, waits for them, and re-layouts: 7.46 us -> 8.43 us
  transfers between devices with their start and end apart: 29 -> 29, of which waited for: 14 -> 14; matrix products, arithmetic and copies ran while one was open for 4% -> 3% of each run, Pallas kernels for 16% -> 16%
where the time goes in v1:
time: 315 us; the launch traced here: 314 us
  blocking collectives  95.9 us (30%)
  Pallas kernels  86.5 us (27%)
  waiting for transfers between devices  63 us (20%)
  starting transfers between devices  43.4 us (14%)
  local copies, waits for them, and re-layouts  17.3 us (5%)
  other arithmetic  6.69 us (2%)
    ppermute x18, waiting for transfers between devices, shift_x(): lax.ppermute(block, 'x', [(i, (i + step) % ranks) for i in range(ranks)])  49.6 us
    all_to_all x1, blocking collectives, layer(): spread = lax.all_to_all(paired, ('y', 'x', 'z'), 0, 0, tiled=True)  43.5 us
    all_to_all x1, blocking collectives, to_owners(): return lax.all_to_all(outgoing, ('y', 'z', 'c'), 0, 0, tiled=True)  39.3 us
    all_to_all x3, starting transfers between devices, to_owners(): return lax.all_to_all(outgoing, ('y', 'z', 'c'), 0, 0, tiled=True)  20.5 us
    ppermute x18, starting transfers between devices, shift_x(): lax.ppermute(block, 'x', [(i, (i + step) % ranks) for i in range(ranks)])  15.8 us
    pallas_call x1, Pallas kernels, backward(): pl.pallas_call(backward_kernel, out_shape=[shape((count, features), bf16)...  14.9 us
    pallas_call x1, Pallas kernels, experts_back(): pl.pallas_call(functools.partial(expert_back_kernel, capacity), grid=(2,)...  13.3 us
    all_to_all x1, blocking collectives, layer(): lax.all_to_all(jnp.broadcast_to(mine[None], (16, piece, wide)).reshape(16...  13.1 us
  transfers between devices with their start and end apart: 29, of which 14 were waited for; matrix products, arithmetic and copies ran while one was open for 3% of the time, Pallas kernels for 16%

profile of v1, /device:TPU:1, one launch (start us, length us, event | category | flops | bytes accessed | tf_op | source)
XLA Modules:
  0.0 314.2 jit_solution(15763202275715516961)
XLA Ops:
  2.5 2.4 line.1.refs_0_.refs_3_
  5.0 3.4 %collective-permute-start.2 = (bf16[160,768]{1,0:T(8,128)(2,1)}, bf16[160,768]{1,0:T(8,128)(2,1)S(1)}, u32[]{:S(2)}, u32[]{:S(2)}) collective-permute-start(bf16[160,768]{1,0:T(8,128)(2,1)} %line.1.refs_0_.refs_3_), channel_id=1, source_target_pairs={{0,3},{1,0},{2,1},{3,2},{4,7},{5,4},{6,5},{7,6},{8,11},{9,8},{10,9... | collective-permute-start | bytes 737288 | tf_op jit(solution)/shard_map/ppermute | solution.py:34
  9.5 1.8 pack.2
  11.3 2.1 collective-permute-start.5
  13.5 1.2 collective-permute-start.4
  16.6 7.9 %collective-permute-done.refs_1_ = bf16[160,768]{1,0:T(8,128)(2,1)S(1)} collective-permute-done((bf16[160,768]{1,0:T(8,128)(2,1)}, bf16[160,768]{1,0:T(8,128)(2,1)S(1)}, u32[]{:S(2)}, u32[]{:S(2)}) %collective-permute-start) | collective-permute-done | bytes 245792 | tf_op jit(solution)/shard_map/ppermute | solution.py:34
  25.2 4.7 %dispatch_grads.1 = (bf16[768,1664]{1,0:T(8,128)(2,1)}, s32[2,512]{1,0:T(2,128)}, s32[2,512]{1,0:T(2,128)}, s32[2,128]{1,0:T(2,128)}) custom-call(bf16[160,768]{1,0:T(8,128)(2,1)} %line.1.refs_0_.refs_3_, bf16[160,768]{1,0:T(8,128)(2,1)} %copy-done.6, bf16[160,768]{1,0:T(8,128)(2,1)} %copy-done.5, bf16[160,768]{1,0:T(8,128)(2,1)} %copy-done.4), custom_call_target="tpu_custom_call" | custom-call | tf_op jit(solution)/shard_map/dispatch_grads/pallas_call | solution.py:519
  30.0 9.0 %all-to-all-start = ((bf16[32,24,1664]{2,1,0:T(8,128)(2,1)}), bf16[32,24,1664]{2,1,0:T(8,128)(2,1)S(1)}, u32[]{:S(2)}, u32[]{:S(2)}) async-start(bf16[32,24,1664]{2,1,0:T(8,128)(2,1)} %bitcast.36), calls=%async_computation | async-start | bytes 5111808 | tf_op jit(solution)/shard_map/all_to_all | solution.py:843
  40.7 1.6 pack.3
  42.6 1.3 collective-permute-start.10
  49.0 1.0 collective-permute-start.9
  51.4 3.8 %collective-permute-done.9.refs_1_ = bf16[96,768]{1,0:T(8,128)(2,1)S(1)} collective-permute-done((bf16[96,768]{1,0:T(8,128)(2,1)}, bf16[96,768]{1,0:T(8,128)(2,1)S(1)}, u32[]{:S(2)}, u32[]{:S(2)}) %collective-permute-start.9) | collective-permute-done | bytes 147488 | tf_op jit(solution)/shard_map/ppermute | solution.py:34
  55.2 1.5 collective-permute-start.13
  56.8 1.2 copy_select_fusion.bias_ref
  59.5 6.8 %attend.1 = (bf16[768,768]{1,0:T(8,128)(2,1)}, bf16[768,768]{1,0:T(8,128)(2,1)}, bf16[768,768]{1,0:T(8,128)(2,1)}, bf16[128,768]{1,0:T(8,128)(2,1)}, bf16[128,76...) custom-call(s32[2]{0:T(128)} %pad_add_fusion.place_ref, ...), custom_call_target="tpu_custom_call" | custom-call | tf_op jit(solution)/shard_map/attend/pallas_call | solution.py:377
  67.1 3.6 %middle.1 = (bf16[768,768]{1,0:T(8,128)(2,1)}, f32[128,768]{1,0:T(8,128)}, bf16[128,768]{1,0:T(8,128)(2,1)}) custom-call(s32[2]{0:T(128)} %pad_add_fusion.place_ref, bf16[128,768]{1,0:T(8,128)(2,1)} %tokens_ref.5, bf16[1,768]{1,0:T(2,128)(2,1)} %reshape_squeeze.7.gain_ref.gain_two_ref, bf16[128,768]{1,0:T(8,128)(2,1)} %get-tuple-element.56.attended_ref, ...), custom_call_target="tpu_custom_call" | custom-call | tf_op jit(solution)/shard_map/middle/pallas_call | solution.py:390
  70.7 1.5 collective-permute-start.17
  72.8 4.2 %collective-permute-done.17.refs_3_.refs_7_ = bf16[128,768]{1,0:T(8,128)(2,1)S(1)} collective-permute-done((bf16[128,768]{1,0:T(8,128)(2,1)}, bf16[128,768]{1,0:T(8,128)(2,1)S(1)}, u32[]{:S(2)}, u32[]{:S(2)}) %collective-permute-start.17) | collective-permute-done | bytes 196640 | tf_op jit(solution)/shard_map/ppermute | solution.py:34
  77.0 2.7 collective-permute-done.16.refs_2_.refs_6_
  79.7 5.1 %collective-permute-done.15.refs_1_.refs_5_ = bf16[128,768]{1,0:T(8,128)(2,1)S(1)} collective-permute-done((bf16[128,768]{1,0:T(8,128)(2,1)}, bf16[128,768]{1,0:T(8,128)(2,1)S(1)}, u32[]{:S(2)}, u32[]{:S(2)}) %collective-permute-start.15) | collective-permute-done | bytes 196640 | tf_op jit(solution)/shard_map/ppermute | solution.py:34
  85.4 0.9 copy-done
  86.3 4.0 %dispatch.1 = bf16[768,1536]{1,0:T(8,128)(2,1)} custom-call(s32[2,512]{1,0:T(2,128)} %get-tuple-element.65.places_ref, bf16[128,768]{1,0:T(8,128)(2,1)} %get-tuple-element.58.refs_0_.refs_4_.moe_ref, bf16[128,768]{1,0:T(8,128)(2,1)} %copy-done.9, bf16[128,768]{1,0:T(8,128)(2,1)} %copy-done.8, bf16[128,768]{1,0:T(8,128)(2,1)} %copy-done.7, ...), custom_call_target="tpu_custom_call" | custom-call | tf_op jit(solution)/shard_map/dispatch/pallas_call | solution.py:546
  90.3 39.3 %all_to_all.61 = bf16[32,24,1536]{2,1,0:T(8,128)(2,1)} all-to-all(bf16[32,24,1536]{2,1,0:T(8,128)(2,1)} %bitcast.42), channel_id=1, replica_groups=mesh['y'=4,'z'=4,'c'=2,'x'=4] {'y','z','c'}, dimensions={0} | all-to-all | bytes 4718592 | tf_op jit(solution)/shard_map/all_to_all | solution.py:843
  129.6 11.3 %experts.1 = (bf16[768,1536]{1,0:T(8,128)(2,1)}, bf16[2,768,768]{2,1,0:T(8,128)(2,1)}, f32[2,768,768]{2,1,0:T(8,128)}) custom-call(bf16[768,1536]{1,0:T(8,128)(2,1)} %bitcast.37, bf16[2,768,768]{2,1,0:T(8,128)(2,1)} %in_ref.3, bf16[2,768,768]{2,1,0:T(8,128)(2,1)} %out_ref.3), custom_call_target="tpu_custom_call" | custom-call | tf_op jit(solution)/shard_map/experts/pallas_call | solution.py:599
  140.9 3.9 %all-to-all-start.3 = ((bf16[32,24,1536]{2,1,0:T(8,128)(2,1)}), bf16[32,24,1536]{2,1,0:T(8,128)(2,1)S(1)}, u32[]{:S(2)}, u32[]{:S(2)}) async-start(bf16[32,24,1536]{2,1,0:T(8,128)(2,1)} %bitcast.47), calls=%async_computation.3 | async-start | bytes 4718592 | tf_op jit(solution)/shard_map/all_to_all | solution.py:843
  145.8 13.3 %experts_back.1 = (bf16[2,768,768]{2,1,0:T(8,128)(2,1)}, bf16[2,768,768]{2,1,0:T(8,128)(2,1)}, bf16[384,768]{1,0:T(8,128)(2,1)}, bf16[384,768]{1,0:T(8,128)(2,1)...) custom-call(s32[1]{0:T(128)} %bitcast.12.own_ref, bf16[768,1536]{1,0:T(8,128)(2,1)} %bitcast.38, ...), custom_call_target="tpu_custom_call" | custom-call | tf_op jit(solution)/shard_map/experts_back/pallas_call | solution.py:660
  159.9 0.9 collective-permute-start.20
  160.7 10.0 %weight_grads.1 = (f32[2,768,768]{2,1,0:T(8,128)}, f32[2,768,768]{2,1,0:T(8,128)}) custom-call(bf16[768,1536]{1,0:T(8,128)(2,1)} %bitcast.39, bf16[2,768,768]{2,1,0:T(8,128)(2,1)} %get-tuple-element.71.pre_ref, bf16[2,768,768]{2,1,0:T(8,128)(2,1)} %get-tuple-element.72.act_ref, bf16[2,768,768]{2,1,0:T(8,128)(2,1)} %get-tuple-element.73.arr_ref), custom_call_target="tpu_custom_call" | custom-call | flops 3623878656 | bytes 20000000 | tf_op jit(solution)/shard_map/weight_grads/pallas_call | solution.py:695
  170.8 3.3 %collective-permute-done.18.refs_1_ = bf16[384,768]{1,0:T(8,128)(2,1)S(1)} collective-permute-done((bf16[384,768]{1,0:T(8,128)(2,1)}, bf16[384,768]{1,0:T(8,128)(2,1)S(1)}, u32[]{:S(2)}, u32[]{:S(2)}) %collective-permute-start.18) | collective-permute-done | bytes 589856 | tf_op jit(solution)/shard_map/ppermute | solution.py:34
  174.1 1.6 collective-permute-done.19.refs_2_
  175.7 13.6 %collective-permute-done.20.refs_3_ = bf16[384,768]{1,0:T(8,128)(2,1)S(1)} collective-permute-done((bf16[384,768]{1,0:T(8,128)(2,1)}, bf16[384,768]{1,0:T(8,128)(2,1)S(1)}, u32[]{:S(2)}, u32[]{:S(2)}) %collective-permute-start.20) | collective-permute-done | bytes 589856 | tf_op jit(solution)/shard_map/ppermute | solution.py:34
  190.1 3.3 %sum_rows.1.refs_8_ = bf16[512,768]{1,0:T(8,128)(2,1)} custom-call(bf16[384,768]{1,0:T(8,128)(2,1)} %get-tuple-element.67.refs_0_, bf16[384,768]{1,0:T(8,128)(2,1)} %copy-done.11, bf16[384,768]{1,0:T(8,128)(2,1)} %copy-done.12, bf16[384,768]{1,0:T(8,128)(2,1)} %copy-done.13, f32[2,768,768]{2,1,0:T(8,128)} %get-tuple-element.130.refs_4_, ...), custom_call_target="tpu_custom_call" | custom-call | tf_op jit(solution)/shard_map/sum_rows/pallas_call | solution.py:736
  193.3 7.6 %all-to-all-start.2 = ((bf16[32,16,768]{2,1,0:T(8,128)(2,1)}), bf16[32,16,768]{2,1,0:T(8,128)(2,1)S(1)}, u32[]{:S(2)}, u32[]{:S(2)}) async-start(bf16[32,16,768]{2,1,0:T(8,128)(2,1)} %bitcast.43), calls=%async_computation.2 | async-start | bytes 1572864 | tf_op jit(solution)/shard_map/all_to_all | solution.py:843
  201.0 5.9 %combine.1 = (bf16[128,896]{1,0:T(8,128)(2,1)}, bf16[128,896]{1,0:T(8,128)(2,1)}, bf16[128,896]{1,0:T(8,128)(2,1)}, bf16[128,896]{1,0:T(8,128)(2,1)}) custom-call(s32[2,512]{1,0:T(2,128)} %get-tuple-element.65.places_ref, s32[2,512]{1,0:T(2,128)} %get-tuple-element.54.ids_ref, bf16[64,768]{1,0:T(8,128)(2,1)} %reshape.184.router_ref, ...), custom_call_target="tpu_custom_call" | custom-call | tf_op jit(solution)/shard_map/combine/pallas_call | solution.py:784
  207.6 0.9 collective-permute-start.23
  208.4 6.8 %all-to-all-done.2 = bf16[32,16,768]{2,1,0:T(8,128)(2,1)S(1)} async-done(((bf16[32,16,768]{2,1,0:T(8,128)(2,1)}), bf16[32,16,768]{2,1,0:T(8,128)(2,1)S(1)}, u32[]{:S(2)}, u32[]{:S(2)}) %all-to-all-start.2) | async-done | bytes 786464 | tf_op jit(solution)/shard_map/all_to_all | solution.py:843
  216.0 5.7 %collective-permute-done.23.refs_3_ = bf16[128,896]{1,0:T(8,128)(2,1)S(1)} collective-permute-done((bf16[128,896]{1,0:T(8,128)(2,1)}, bf16[128,896]{1,0:T(8,128)(2,1)S(1)}, u32[]{:S(2)}, u32[]{:S(2)}) %collective-permute-start.23) | collective-permute-done | bytes 229408 | tf_op jit(solution)/shard_map/ppermute | solution.py:34
  222.4 14.9 %backward.1 = (bf16[128,768]{1,0:T(8,128)(2,1)}, f32[128,768]{1,0:T(8,128)}, bf16[1536,896]{1,0:T(8,128)(2,1)}, bf16[1536,896]{1,0:T(8,128)(2,1)}) custom-call(s32[1]{0:T(128)} %bitcast.core_ref, bf16[128,768]{1,0:T(8,128)(2,1)} %tokens_ref.5, bf16[128,768]{1,0:T(8,128)(2,1)} %cotangent_ref.3, bf16[1,768]{1,0:T(2,128)(2,1)} %reshape_squeeze.6.gain_ref.gain_one_ref, ...), custom_call_target="tpu_custom_call" | custom-call | tf_op jit(solution)/shard_map/backward/pallas_call | solution.py:410
  237.9 4.9 %collective-permute-done.24 = bf16[1536,896]{1,0:T(8,128)(2,1)S(1)} collective-permute-done((bf16[1536,896]{1,0:T(8,128)(2,1)}, bf16[1536,896]{1,0:T(8,128)(2,1)S(1)}, u32[]{:S(2)}, u32[]{:S(2)}) %collective-permute-start.24) | collective-permute-done | bytes 2752544 | tf_op jit(solution)/shard_map/ppermute | solution.py:38
  242.8 2.5 add_convert_fusion
  245.3 43.5 %all_to_all.62 = bf16[64,24,896]{2,1,0:T(8,128)(2,1)S(1)} all-to-all(bf16[64,24,896]{2,1,0:T(8,128)(2,1)S(1)} %bitcast.40), channel_id=1, replica_groups=mesh['y'=4,'z'=4,'c'=2,'x'=4] {'y','x','z'}, dimensions={0} | all-to-all | bytes 5505024 | tf_op jit(solution)/shard_map/all_to_all | solution.py:913
  289.2 13.1 %all_to_all.63 = bf16[16,24,896]{2,1,0:T(8,128)(2,1)S(1)} all-to-all(bf16[16,24,896]{2,1,0:T(8,128)(2,1)S(1)} %broadcast_in_dim.54), channel_id=1, replica_groups=mesh['y'=4,'z'=4,'c'=2,'x'=4] {'y','z'}, dimensions={0} | all-to-all | bytes 1376256 | tf_op jit(solution)/shard_map/all_to_all | solution.py:915
  302.4 3.5 %collective-permute-start.25 = (bf16[384,896]{1,0:T(8,128)(2,1)S(1)}, bf16[384,896]{1,0:T(8,128)(2,1)S(1)}, u32[]{:S(2)}, u32[]{:S(2)}) collective-permute-start(bf16[384,896]{1,0:T(8,128)(2,1)S(1)} %bitcast.45), channel_id=1, source_target_pairs={{0,4},{4,0},{1,5},{5,1},{2,6},{6,2},{3,7},{7,3},{8,12},{12,8},{9,1... | collective-permute-start | bytes 2064392 | tf_op jit(solution)/shard_map/ppermute | solution.py:38
  305.9 1.8 collective-permute-done.25.other_ref
  307.6 0.9 copy-done.10
  308.5 2.8 finish.1
  311.3 1.3 fusion.5
  312.6 1.6 copy.35
  (112 shorter events, 23.4 us)
Async XLA Ops:
  5.0 10.7 %collective-permute-start.2 = (bf16[160,768]{1,0:T(8,128)(2,1)}, bf16[160,768]{1,0:T(8,128)(2,1)S(1)}, u32[]{:S(2)}, u32[]{:S(2)}) collective-permute-start(bf16[160,768]{1,0:T(8,128)(2,1)} %line.1.refs_0_.refs_3_), channel_id=1, source_target_pairs={{0,3},{1,0},{2,1},{3,2},{4,7},{5,4},{6,5},{7,6},{8,11},{9,8},{10,9... | collective-permute-start | bytes 737288 | tf_op jit(solution)/shard_map/ppermute | solution.py:34
  8.4 8.3 %collective-permute-start.1 = (bf16[160,768]{1,0:T(8,128)(2,1)}, bf16[160,768]{1,0:T(8,128)(2,1)S(1)}, u32[]{:S(2)}, u32[]{:S(2)}) collective-permute-start(bf16[160,768]{1,0:T(8,128)(2,1)} %line.1.refs_0_.refs_3_), channel_id=1, source_target_pairs={{0,2},{1,3},{2,0},{3,1},{4,6},{5,7},{6,4},{7,5},{8,10},{9,11},{10,... | collective-permute-start | bytes 737288 | tf_op jit(solution)/shard_map/ppermute | solution.py:34
  8.9 15.7 %collective-permute-start = (bf16[160,768]{1,0:T(8,128)(2,1)}, bf16[160,768]{1,0:T(8,128)(2,1)S(1)}, u32[]{:S(2)}, u32[]{:S(2)}) collective-permute-start(bf16[160,768]{1,0:T(8,128)(2,1)} %line.1.refs_0_.refs_3_), channel_id=1, source_target_pairs={{0,1},{1,2},{2,3},{3,0},{4,5},{5,6},{6,7},{7,4},{8,9},{9,10},{10,1... | collective-permute-start | bytes 737288 | tf_op jit(solution)/shard_map/ppermute | solution.py:34
  11.3 35.6 %collective-permute-start.5 = (bf16[288,768]{1,0:T(8,128)(2,1)}, bf16[288,768]{1,0:T(8,128)(2,1)}, u32[]{:S(2)}, u32[]{:S(2)}) collective-permute-start(bf16[288,768]{1,0:T(8,128)(2,1)} %pack.2), channel_id=1, source_target_pairs={{0,3},{1,0},{2,1},{3,2},{4,7},{5,4},{6,5},{7,6},{8,11},{9,8},{10,9... | collective-permute-start | bytes 1327112 | tf_op jit(solution)/shard_map/ppermute | solution.py:34
  13.5 36.6 %collective-permute-start.4 = (bf16[288,768]{1,0:T(8,128)(2,1)}, bf16[288,768]{1,0:T(8,128)(2,1)}, u32[]{:S(2)}, u32[]{:S(2)}) collective-permute-start(bf16[288,768]{1,0:T(8,128)(2,1)} %pack.2), channel_id=1, source_target_pairs={{0,2},{1,3},{2,0},{3,1},{4,6},{5,7},{6,4},{7,5},{8,10},{9,11},{10,... | collective-permute-start | bytes 1327112 | tf_op jit(solution)/shard_map/ppermute | solution.py:34
  15.7 8.9 %copy-start.4 = (bf16[160,768]{1,0:T(8,128)(2,1)}, bf16[160,768]{1,0:T(8,128)(2,1)S(1)}, u32[]{:S(2)}) copy-start(bf16[160,768]{1,0:T(8,128)(2,1)S(1)} %collective-permute-done.2.refs_3_) | copy-start | bytes 737284
  15.7 34.7 %collective-permute-start.3 = (bf16[288,768]{1,0:T(8,128)(2,1)}, bf16[288,768]{1,0:T(8,128)(2,1)}, u32[]{:S(2)}, u32[]{:S(2)}) collective-permute-start(bf16[288,768]{1,0:T(8,128)(2,1)} %pack.2), channel_id=1, source_target_pairs={{0,1},{1,2},{2,3},{3,0},{4,5},{5,6},{6,7},{7,4},{8,9},{9,10},{10,1... | collective-permute-start | bytes 1327112 | tf_op jit(solution)/shard_map/ppermute | solution.py:34
  16.6 7.9 %copy-start.5 = (bf16[160,768]{1,0:T(8,128)(2,1)}, bf16[160,768]{1,0:T(8,128)(2,1)S(1)}, u32[]{:S(2)}) copy-start(bf16[160,768]{1,0:T(8,128)(2,1)S(1)} %collective-permute-done.1.refs_2_) | copy-start | bytes 737284
  30.0 9.6 %copy-start.24 = (s32[31]{0:T(128)S(1)}, s32[31]{0:T(128)}, u32[]{:S(2)}) copy-start(s32[31]{0:T(128)} %constant.62.clone) | copy-start | bytes 376
  30.0 54.8 %all-to-all-start = ((bf16[32,24,1664]{2,1,0:T(8,128)(2,1)}), bf16[32,24,1664]{2,1,0:T(8,128)(2,1)S(1)}, u32[]{:S(2)}, u32[]{:S(2)}) async-start(bf16[32,24,1664]{2,1,0:T(8,128)(2,1)} %bitcast.36), calls=%async_computation | async-start | bytes 5111808 | tf_op jit(solution)/shard_map/all_to_all | solution.py:843
  42.3 6.7 %collective-permute-start.11 = (bf16[96,768]{1,0:T(8,128)(2,1)}, bf16[96,768]{1,0:T(8,128)(2,1)}, u32[]{:S(2)}, u32[]{:S(2)}) collective-permute-start(bf16[96,768]{1,0:T(8,128)(2,1)} %pack.3), channel_id=1, source_target_pairs={{0,3},{1,0},{2,1},{3,2},{4,7},{5,4},{6,5},{7,6},{8,11},{9,8},{10,9... | collective-permute-start | bytes 442376 | tf_op jit(solution)/shard_map/ppermute | solution.py:34
  42.6 8.4 %collective-permute-start.10 = (bf16[96,768]{1,0:T(8,128)(2,1)}, bf16[96,768]{1,0:T(8,128)(2,1)}, u32[]{:S(2)}, u32[]{:S(2)}) collective-permute-start(bf16[96,768]{1,0:T(8,128)(2,1)} %pack.3), channel_id=1, source_target_pairs={{0,2},{1,3},{2,0},{3,1},{4,6},{5,7},{6,4},{7,5},{8,10},{9,11},{10,... | collective-permute-start | bytes 442376 | tf_op jit(solution)/shard_map/ppermute | solution.py:34
  46.9 9.8 %collective-permute-start.8 = (bf16[288,768]{1,0:T(8,128)(2,1)}, bf16[288,768]{1,0:T(8,128)(2,1)S(1)}, u32[]{:S(2)}, u32[]{:S(2)}) collective-permute-start(bf16[288,768]{1,0:T(8,128)(2,1)} %collective-permute-done.5.refs_5_), channel_id=1, source_target_pairs={{0,4},{4,0},{1,5},{5,1},{2,6},{6,2},{3,7},{7,3},{8,12},{12,8},{9,1... | collective-permute-start | bytes 1327112 | tf_op jit(solution)/shard_map/ppermute | solution.py:38
  49.0 6.2 %collective-permute-start.9 = (bf16[96,768]{1,0:T(8,128)(2,1)}, bf16[96,768]{1,0:T(8,128)(2,1)S(1)}, u32[]{:S(2)}, u32[]{:S(2)}) collective-permute-start(bf16[96,768]{1,0:T(8,128)(2,1)} %pack.3), channel_id=1, source_target_pairs={{0,1},{1,2},{2,3},{3,0},{4,5},{5,6},{6,7},{7,4},{8,9},{9,10},{10,1... | collective-permute-start | bytes 442376 | tf_op jit(solution)/shard_map/ppermute | solution.py:34
  50.1 7.9 %collective-permute-start.7 = (bf16[288,768]{1,0:T(8,128)(2,1)}, bf16[288,768]{1,0:T(8,128)(2,1)S(1)}, u32[]{:S(2)}, u32[]{:S(2)}) collective-permute-start(bf16[288,768]{1,0:T(8,128)(2,1)} %collective-permute-done.4.refs_4_), channel_id=1, source_target_pairs={{0,4},{4,0},{1,5},{5,1},{2,6},{6,2},{3,7},{7,3},{8,12},{12,8},{9,1... | collective-permute-start | bytes 1327112 | tf_op jit(solution)/shard_map/ppermute | solution.py:38
  50.4 7.6 %collective-permute-start.6 = (bf16[288,768]{1,0:T(8,128)(2,1)}, bf16[288,768]{1,0:T(8,128)(2,1)S(1)}, u32[]{:S(2)}, u32[]{:S(2)}) collective-permute-start(bf16[288,768]{1,0:T(8,128)(2,1)} %collective-permute-done.3.refs_3_), channel_id=1, source_target_pairs={{0,4},{4,0},{1,5},{5,1},{2,6},{6,2},{3,7},{7,3},{8,12},{12,8},{9,1... | collective-permute-start | bytes 1327112 | tf_op jit(solution)/shard_map/ppermute | solution.py:38
  51.0 15.3 %collective-permute-start.14 = (bf16[96,768]{1,0:T(8,128)(2,1)}, bf16[96,768]{1,0:T(8,128)(2,1)S(1)}, u32[]{:S(2)}, u32[]{:S(2)}) collective-permute-start(bf16[96,768]{1,0:T(8,128)(2,1)} %collective-permute-done.11.refs_3_), channel_id=1, source_target_pairs={{0,4},{4,0},{1,5},{5,1},{2,6},{6,2},{3,7},{7,3},{8,12},{12,8},{9,1... | collective-permute-start | bytes 442376 | tf_op jit(solution)/shard_map/ppermute | solution.py:38
  55.2 11.1 %copy-start.20 = (bf16[96,768]{1,0:T(8,128)(2,1)}, bf16[96,768]{1,0:T(8,128)(2,1)S(1)}, u32[]{:S(2)}) copy-start(bf16[96,768]{1,0:T(8,128)(2,1)S(1)} %collective-permute-done.9.refs_1_) | copy-start | bytes 442372
  55.2 11.1 %collective-permute-start.13 = (bf16[96,768]{1,0:T(8,128)(2,1)}, bf16[96,768]{1,0:T(8,128)(2,1)S(1)}, u32[]{:S(2)}, u32[]{:S(2)}) collective-permute-start(bf16[96,768]{1,0:T(8,128)(2,1)} %collective-permute-done.10.refs_2_), channel_id=1, source_target_pairs={{0,4},{4,0},{1,5},{5,1},{2,6},{6,2},{3,7},{7,3},{8,12},{12,8},{9,1... | collective-permute-start | bytes 442376 | tf_op jit(solution)/shard_map/ppermute | solution.py:38
  56.7 1.3 copy-start.14
  56.7 9.6 %collective-permute-start.12 = (bf16[96,768]{1,0:T(8,128)(2,1)S(1)}, bf16[96,768]{1,0:T(8,128)(2,1)S(1)}, u32[]{:S(2)}, u32[]{:S(2)}) collective-permute-start(bf16[96,768]{1,0:T(8,128)(2,1)S(1)} %collective-permute-done.9.refs_1_), channel_id=1, source_target_pairs={{0,4},{4,0},{1,5},{5,1},{2,6},{6,2},{3,7},{7,3},{8,12},{12,8},{9,1... | collective-permute-start | bytes 442376 | tf_op jit(solution)/shard_map/ppermute | solution.py:38
  58.0 0.8 copy-start.15
  58.7 0.8 copy-start.16
  70.7 6.3 %collective-permute-start.17 = (bf16[128,768]{1,0:T(8,128)(2,1)}, bf16[128,768]{1,0:T(8,128)(2,1)S(1)}, u32[]{:S(2)}, u32[]{:S(2)}) collective-permute-start(bf16[128,768]{1,0:T(8,128)(2,1)} %get-tuple-element.58.refs_0_.refs_4_.moe_ref), channel_id=1, source_target_pairs={{0,3},{1,0},{2,1},{3,2},{4,7},{5,4},{6,5},{7,6},{8,11},{9,8},{10,9... | collective-permute-start | bytes 589832 | tf_op jit(solution)/shard_map/ppermute | solution.py:34
  72.2 7.5 %collective-permute-start.16 = (bf16[128,768]{1,0:T(8,128)(2,1)}, bf16[128,768]{1,0:T(8,128)(2,1)S(1)}, u32[]{:S(2)}, u32[]{:S(2)}) collective-permute-start(bf16[128,768]{1,0:T(8,128)(2,1)} %get-tuple-element.58.refs_0_.refs_4_.moe_ref), channel_id=1, source_target_pairs={{0,2},{1,3},{2,0},{3,1},{4,6},{5,7},{6,4},{7,5},{8,10},{9,11},{10,... | collective-permute-start | bytes 589832 | tf_op jit(solution)/shard_map/ppermute | solution.py:34
  72.4 12.4 %collective-permute-start.15 = (bf16[128,768]{1,0:T(8,128)(2,1)}, bf16[128,768]{1,0:T(8,128)(2,1)S(1)}, u32[]{:S(2)}, u32[]{:S(2)}) collective-permute-start(bf16[128,768]{1,0:T(8,128)(2,1)} %get-tuple-element.58.refs_0_.refs_4_.moe_ref), channel_id=1, source_target_pairs={{0,1},{1,2},{2,3},{3,0},{4,5},{5,6},{6,7},{7,4},{8,9},{9,10},{10,1... | collective-permute-start | bytes 589832 | tf_op jit(solution)/shard_map/ppermute | solution.py:34
  77.0 7.7 %copy-start.7 = (bf16[128,768]{1,0:T(8,128)(2,1)}, bf16[128,768]{1,0:T(8,128)(2,1)S(1)}, u32[]{:S(2)}) copy-start(bf16[128,768]{1,0:T(8,128)(2,1)S(1)} %collective-permute-done.17.refs_3_.refs_7_) | copy-start | bytes 589828
  79.7 5.1 %copy-start.8 = (bf16[128,768]{1,0:T(8,128)(2,1)}, bf16[128,768]{1,0:T(8,128)(2,1)S(1)}, u32[]{:S(2)}) copy-start(bf16[128,768]{1,0:T(8,128)(2,1)S(1)} %collective-permute-done.16.refs_2_.refs_6_) | copy-start | bytes 589828
  84.8 1.5 copy-start
  140.9 52.5 %all-to-all-start.3 = ((bf16[32,24,1536]{2,1,0:T(8,128)(2,1)}), bf16[32,24,1536]{2,1,0:T(8,128)(2,1)S(1)}, u32[]{:S(2)}, u32[]{:S(2)}) async-start(bf16[32,24,1536]{2,1,0:T(8,128)(2,1)} %bitcast.47), calls=%async_computation.3 | async-start | bytes 4718592 | tf_op jit(solution)/shard_map/all_to_all | solution.py:843
  159.2 14.9 %collective-permute-start.18 = (bf16[384,768]{1,0:T(8,128)(2,1)}, bf16[384,768]{1,0:T(8,128)(2,1)S(1)}, u32[]{:S(2)}, u32[]{:S(2)}) collective-permute-start(bf16[384,768]{1,0:T(8,128)(2,1)} %get-tuple-element.68), channel_id=1, source_target_pairs={{0,3},{1,0},{2,1},{3,2},{4,7},{5,4},{6,5},{7,6},{8,11},{9,8},{10,9... | collective-permute-start | bytes 1769480 | tf_op jit(solution)/shard_map/ppermute | solution.py:34
  159.7 16.0 %collective-permute-start.19 = (bf16[384,768]{1,0:T(8,128)(2,1)}, bf16[384,768]{1,0:T(8,128)(2,1)S(1)}, u32[]{:S(2)}, u32[]{:S(2)}) collective-permute-start(bf16[384,768]{1,0:T(8,128)(2,1)} %get-tuple-element.69), channel_id=1, source_target_pairs={{0,2},{1,3},{2,0},{3,1},{4,6},{5,7},{6,4},{7,5},{8,10},{9,11},{10,... | collective-permute-start | bytes 1769480 | tf_op jit(solution)/shard_map/ppermute | solution.py:34
  159.9 29.4 %collective-permute-start.20 = (bf16[384,768]{1,0:T(8,128)(2,1)}, bf16[384,768]{1,0:T(8,128)(2,1)S(1)}, u32[]{:S(2)}, u32[]{:S(2)}) collective-permute-start(bf16[384,768]{1,0:T(8,128)(2,1)} %get-tuple-element.70), channel_id=1, source_target_pairs={{0,1},{1,2},{2,3},{3,0},{4,5},{5,6},{6,7},{7,4},{8,9},{9,10},{10,1... | collective-permute-start | bytes 1769480 | tf_op jit(solution)/shard_map/ppermute | solution.py:34
  174.1 15.2 %copy-start.11 = (bf16[384,768]{1,0:T(8,128)(2,1)}, bf16[384,768]{1,0:T(8,128)(2,1)S(1)}, u32[]{:S(2)}) copy-start(bf16[384,768]{1,0:T(8,128)(2,1)S(1)} %collective-permute-done.18.refs_1_) | copy-start | bytes 1769476
  175.7 13.6 %copy-start.12 = (bf16[384,768]{1,0:T(8,128)(2,1)}, bf16[384,768]{1,0:T(8,128)(2,1)S(1)}, u32[]{:S(2)}) copy-start(bf16[384,768]{1,0:T(8,128)(2,1)S(1)} %collective-permute-done.19.refs_2_) | copy-start | bytes 1769476
  189.3 0.8 copy-start.13
  193.3 7.6 %copy-start.1 = (bf16[32,24,1536]{2,1,0:T(8,128)(2,1)}, bf16[32,24,1536]{2,1,0:T(8,128)(2,1)S(1)}, u32[]{:S(2)}) copy-start(bf16[32,24,1536]{2,1,0:T(8,128)(2,1)S(1)} %all-to-all-done.3) | copy-start | bytes 7077892
  193.3 21.9 %all-to-all-start.2 = ((bf16[32,16,768]{2,1,0:T(8,128)(2,1)}), bf16[32,16,768]{2,1,0:T(8,128)(2,1)S(1)}, u32[]{:S(2)}, u32[]{:S(2)}) async-start(bf16[32,16,768]{2,1,0:T(8,128)(2,1)} %bitcast.43), calls=%async_computation.2 | async-start | bytes 1572864 | tf_op jit(solution)/shard_map/all_to_all | solution.py:843
  206.9 8.3 %collective-permute-start.21 = (bf16[128,896]{1,0:T(8,128)(2,1)}, bf16[128,896]{1,0:T(8,128)(2,1)S(1)}, u32[]{:S(2)}, u32[]{:S(2)}) collective-permute-start(bf16[128,896]{1,0:T(8,128)(2,1)} %get-tuple-element.78), channel_id=1, source_target_pairs={{0,3},{1,0},{2,1},{3,2},{4,7},{5,4},{6,5},{7,6},{8,11},{9,8},{10,9... | collective-permute-start | bytes 688136 | tf_op jit(solution)/shard_map/ppermute | solution.py:34
  207.6 8.4 %collective-permute-start.22 = (bf16[128,896]{1,0:T(8,128)(2,1)}, bf16[128,896]{1,0:T(8,128)(2,1)S(1)}, u32[]{:S(2)}, u32[]{:S(2)}) collective-permute-start(bf16[128,896]{1,0:T(8,128)(2,1)} %get-tuple-element.79), channel_id=1, source_target_pairs={{0,2},{1,3},{2,0},{3,1},{4,6},{5,7},{6,4},{7,5},{8,10},{9,11},{10,... | collective-permute-start | bytes 688136 | tf_op jit(solution)/shard_map/ppermute | solution.py:34
  207.6 14.2 %collective-permute-start.23 = (bf16[128,896]{1,0:T(8,128)(2,1)}, bf16[128,896]{1,0:T(8,128)(2,1)S(1)}, u32[]{:S(2)}, u32[]{:S(2)}) collective-permute-start(bf16[128,896]{1,0:T(8,128)(2,1)} %get-tuple-element.80), channel_id=1, source_target_pairs={{0,1},{1,2},{2,3},{3,0},{4,5},{5,6},{6,7},{7,4},{8,9},{9,10},{10,1... | collective-permute-start | bytes 688136 | tf_op jit(solution)/shard_map/ppermute | solution.py:34
  215.2 6.5 %copy-start.2 = (bf16[32,16,768]{2,1,0:T(8,128)(2,1)}, bf16[32,16,768]{2,1,0:T(8,128)(2,1)S(1)}, u32[]{:S(2)}) copy-start(bf16[32,16,768]{2,1,0:T(8,128)(2,1)S(1)} %all-to-all-done.2) | copy-start | bytes 2359300
  215.2 6.5 %copy-start.17 = (bf16[128,896]{1,0:T(8,128)(2,1)}, bf16[128,896]{1,0:T(8,128)(2,1)S(1)}, u32[]{:S(2)}) copy-start(bf16[128,896]{1,0:T(8,128)(2,1)S(1)} %collective-permute-done.21.refs_1_) | copy-start | bytes 688132
  216.0 5.8 %copy-start.18 = (bf16[128,896]{1,0:T(8,128)(2,1)}, bf16[128,896]{1,0:T(8,128)(2,1)S(1)}, u32[]{:S(2)}) copy-start(bf16[128,896]{1,0:T(8,128)(2,1)S(1)} %collective-permute-done.22.refs_2_) | copy-start | bytes 688132
  237.3 5.5 %collective-permute-start.24 = (bf16[1536,896]{1,0:T(8,128)(2,1)}, bf16[1536,896]{1,0:T(8,128)(2,1)S(1)}, u32[]{:S(2)}, u32[]{:S(2)}) collective-permute-start(bf16[1536,896]{1,0:T(8,128)(2,1)} %get-tuple-element.88), channel_id=1, source_target_pairs={{0,4},{4,0},{1,5},{5,1},{2,6},{6,2},{3,7},{7,3},{8,12},{12,8},{9,1... | collective-permute-start | bytes 8257544 | tf_op jit(solution)/shard_map/ppermute | solution.py:38
  302.4 5.2 %copy-start.3 = (bf16[16,24,896]{2,1,0:T(8,128)(2,1)}, bf16[16,24,896]{2,1,0:T(8,128)(2,1)S(1)}, u32[]{:S(2)}) copy-start(bf16[16,24,896]{2,1,0:T(8,128)(2,1)S(1)} %all_to_all.63) | copy-start | bytes 2064388
  302.4 5.2 %collective-permute-start.25 = (bf16[384,896]{1,0:T(8,128)(2,1)S(1)}, bf16[384,896]{1,0:T(8,128)(2,1)S(1)}, u32[]{:S(2)}, u32[]{:S(2)}) collective-permute-start(bf16[384,896]{1,0:T(8,128)(2,1)S(1)} %bitcast.45), channel_id=1, source_target_pairs={{0,4},{4,0},{1,5},{5,1},{2,6},{6,2},{3,7},{7,3},{8,12},{12,8},{9,1... | collective-permute-start | bytes 2064392 | tf_op jit(solution)/shard_map/ppermute | solution.py:38
  307.6 0.9 copy-start.10
  (6 other events, 4.1 us)

commit v2 on v1

--- a/solution.py
+++ b/solution.py
@@ -29,9 +29,13 @@
     return (distance, onehot)
 
 
+def shift(block, axis, step):
+    ranks = lax.axis_size(axis)
+    return lax.ppermute(block, axis, [(i, (i + step) % ranks) for i in range(ranks)])
+
+
 def shift_x(block, step):
-    ranks = lax.axis_size("x")
-    return lax.ppermute(block, "x", [(i, (i + step) % ranks) for i in range(ranks)])
+    return shift(block, "x", step)
 
 
 def swap_core(block):
@@ -143,8 +147,9 @@
 def attend_kernel(place_ref, tokens_ref, gain_ref, bias_ref, *refs):
     f32, bf16 = jnp.float32, jnp.bfloat16
     mats, near, far = refs[:3], refs[3:6], refs[6:9]
-    weights = refs[10:13]
-    hidden_ref, q_ref, k_ref, v_ref, probs_ref, attended_ref, sems = refs[13:20]
+    hidden_ref, q_ref, k_ref, v_ref, probs_ref, attended_ref = refs[9:15]
+    held, sems = refs[15:]
+    weights = [held.at[n] for n in range(3)]
     copies = start_copies(
         block_copies(place_ref[0], place_ref[1], mats, near, far, weights), sems
     )
@@ -177,7 +182,7 @@
 def middle_kernel(place_ref, tokens_ref, gain_ref, attended_ref, *refs):
     f32 = jnp.float32
     mats, near, far = refs[:1], refs[1:4], refs[4:7]
-    weight, middle_ref, moe_ref, sems = refs[8:12]
+    middle_ref, moe_ref, weight, sems = refs[7:11]
     copies = start_copies(
         block_copies(place_ref[0], place_ref[1], mats, near, far, [weight]), sems
     )
@@ -191,7 +196,7 @@
 
 
 def backward_kernel(
-    core_ref,
+    place_ref,
     tokens_ref,
     cotangent_ref,
     gain_one_ref,
@@ -211,29 +216,43 @@
     *refs,
 ):
     f32, bf16 = jnp.float32, jnp.bfloat16
-    homes, weights = refs[:4], refs[4:8]
-    result_ref, tokens_out, kept_ref, given_ref = refs[8:12]
-    held, grads_ref, small_ref, sems = refs[12:16]
-    copies = start_copies([(w, held.at[i]) for i, w in enumerate(weights)], sems)
+    homes, mats, near_far = refs[:4], refs[4:8], refs[8:20]
+    result_ref, tokens_out, kept_ref, given_ref = refs[20:24]
+    held, grads_ref, small_ref, sides_ref, sems, out_sems = refs[24:30]
+    weights = [held.at[n] for n in range(4)]
+    qkv = block_copies(
+        place_ref[0], place_ref[1], mats[:3], near_far[0:3], near_far[3:6], weights[:3]
+    )
+    out = block_copies(
+        place_ref[0], place_ref[1], mats[3:], near_far[6:9], near_far[9:12], weights[3:]
+    )
+    copies = start_copies(qkv + out, sems)
+    leaving = []
     features = tokens_ref.shape[1]
-    core = core_ref[0]
+    core = place_ref[1]
+    width = features // 4
     small_ref[...] = jnp.zeros_like(small_ref)
 
     def leave(mat, left, right):
         grad = lax.dot_general(left, right, FIRST, preferred_element_type=f32).astype(bf16)
-        grads_ref[...] = grad
+        grads_ref[mat] = grad
+        half = 96
+        pairs = []
         for x in range(4):
-            low = grads_ref[x * 192 : x * 192 + 96, :]
-            high = grads_ref[x * 192 + 96 : x * 192 + 192, :]
-            at = (mat * 4 + x) * 96
-            kept_ref[at : at + 96, :features] = jnp.where(core == 0, low, high)
-            given_ref[at : at + 96, :features] = jnp.where(core == 0, high, low)
-
-    def leave_gain(row, gain):
+            into = pl.ds((mat * 4 + x) * half, half)
+            for target, side in ((kept_ref, core), (given_ref, 1 - core)):
+                begin = pl.multiple_of(x * 2 * half + side * half, half)
+                source = grads_ref.at[mat, pl.ds(begin, half)]
+                pairs.append((source, target.at[into, pl.ds(0, features)]))
+        leaving.extend(start_copies(pairs, out_sems.at[mat]))
+
+    def leave_wide(mats_rows, block):
         for x in range(4):
-            at = (4 + x) * 96 + row
-            small_ref[0, at : at + 1, :] = gain[:, x * 192 : x * 192 + 128]
-            small_ref[0, at + 1 : at + 2, :64] = gain[:, x * 192 + 128 : x * 192 + 192]
+            for (mat, row), begin, size in zip(mats_rows, (0, 128), (128, 64)):
+                at = (mat * 4 + x) * 96 + row
+                small_ref[at : at + block.shape[0], :size] = block[
+                    :, x * width + begin : x * width + begin + size
+                ]
 
     home = homes[0][...].astype(f32)
     for piece in homes[1:]:
@@ -260,23 +279,21 @@
     pick = ((slot == spots_ref[0:1]) | (slot == spots_ref[1:2])).astype(f32).astype(bf16)
     grad_moe = lax.dot_general(pick, rows_ref[...], FIRST, preferred_element_type=f32)
     grad_moe = grad_moe + jnp.dot(grad_logits, router_ref[...], preferred_element_type=f32)
-    grad_router = lax.dot_general(moe, grad_logits, FIRST, preferred_element_type=f32)
-    for x in range(4):
-        for side in range(2):
-            begin = x * 192 + side * 96
-            small_ref[side, x * 96 : x * 96 + 96, : logits.shape[1]] = grad_router[
-                begin : begin + 96, :
-            ]
+    leave_wide(
+        ((0, 0), (1, 0)),
+        lax.dot_general(grad_logits, moe, FIRST, preferred_element_type=f32),
+    )
     scale = norm_scale(middle)
     normed = middle * scale
-    leave_gain(2, jnp.sum(grad_moe * normed, axis=0, keepdims=True))
+    leave_wide(((2, 2), (2, 3)), jnp.sum(grad_moe * normed, axis=0, keepdims=True))
     inner = grad_moe * gain_two_ref[...].astype(f32)
     grad_middle = cotangent_ref[...].astype(f32) + scale * (
         inner - normed * jnp.mean(inner * normed, axis=1, keepdims=True)
     )
     branch = grad_middle.astype(bf16)
     leave(3, attended_ref[...], branch)
-    copies[3].wait()
+    for c in copies[21:]:
+        c.wait()
     grad_attended = lax.dot_general(branch, held[3], LAST, preferred_element_type=f32).astype(bf16)
     grad_q, grad_k, grad_v, diagonals = [], [], [], []
     for pair in range(probs_ref.shape[0] // 2):
@@ -312,29 +329,39 @@
         left = left - part.astype(f32)
         grad_bias = grad_bias + jnp.dot(part, bucket_marks(), preferred_element_type=f32)
     per = left.shape[0] // 4
-    for x in range(4):
-        at = (4 + x) * 96 + 4
-        small_ref[0, at : at + per, :] = grad_bias[x * per : x * per + per, :]
+    for a in range(4):
+        at = (8 + a) * 96 + 4
+        small_ref[at : at + per, :] = grad_bias[a * per : a * per + per, :]
     hidden = hidden_ref[...]
     grad_hidden = jnp.zeros(hidden.shape, f32)
     for n, parts in enumerate((grad_q, grad_k, grad_v)):
         grad = jnp.concatenate(parts, axis=1)
         leave(n, hidden, grad)
-        copies[n].wait()
+        for c in copies[7 * n : 7 * n + 7]:
+            c.wait()
         grad_hidden = grad_hidden + lax.dot_general(
             grad, held[n], LAST, preferred_element_type=f32
         )
     x = tokens_ref[...].astype(f32)
     scale = norm_scale(x)
     normed = x * scale
-    leave_gain(0, jnp.sum(grad_hidden * normed, axis=0, keepdims=True))
+    leave_wide(((2, 0), (2, 1)), jnp.sum(grad_hidden * normed, axis=0, keepdims=True))
     inner = grad_hidden * gain_one_ref[...].astype(f32)
     tokens_out[...] = grad_middle + scale * (
         inner - normed * jnp.mean(inner * normed, axis=1, keepdims=True)
     )
-    low, high = small_ref[0], small_ref[1]
-    kept_ref[:, features:] = jnp.where(core == 0, low, high).astype(bf16)
-    given_ref[:, features:] = jnp.where(core == 0, high, low).astype(bf16)
+    small = small_ref[...].astype(bf16)
+    none = jnp.zeros_like(small)
+    sides_ref[0] = jnp.where(core == 0, small, none)
+    sides_ref[1] = jnp.where(core == 0, none, small)
+    lanes = pl.ds(features, 128)
+    pairs = [
+        (sides_ref.at[0], kept_ref.at[:, lanes]),
+        (sides_ref.at[1], given_ref.at[:, lanes]),
+    ]
+    leaving.extend(start_copies(pairs, out_sems.at[4]))
+    for c in leaving:
+        c.wait()
 
 
 ANYWHERE = pl.BlockSpec(memory_space=pl.ANY)
@@ -370,39 +397,43 @@
     )(core[None], *mats, after)
 
 
-def attend(where, tokens, gain, bias, mats, near, far, after):
+def attend(where, tokens, gain, bias, mats, near, far):
     rows, cols = mats[0].shape
-    full = jax.ShapeDtypeStruct((4 * rows, cols), jnp.bfloat16)
     state = jax.ShapeDtypeStruct(tokens.shape, jnp.bfloat16)
     return pl.pallas_call(
         attend_kernel,
-        out_shape=[full] * 3 + [state] * 4 + [jax.ShapeDtypeStruct(bias.shape, jnp.float32), state],
-        in_specs=[SCALARS] + [WHOLE] * 3 + [ANYWHERE] * 10,
-        out_specs=[WHOLE] * 9,
-        scratch_shapes=[pltpu.SemaphoreType.DMA((21,))],
+        out_shape=[state] * 4 + [jax.ShapeDtypeStruct(bias.shape, jnp.float32), state],
+        in_specs=[SCALARS] + [WHOLE] * 3 + [ANYWHERE] * 9,
+        out_specs=[WHOLE] * 6,
+        scratch_shapes=[
+            pltpu.VMEM((3, 4 * rows, cols), jnp.bfloat16),
+            pltpu.SemaphoreType.DMA((21,)),
+        ],
         compiler_params=ROOM,
         name="attend",
-    )(where, tokens, gain, bias, *mats, *near, *far, after)
-
-
-def to_middle(where, tokens, gain, attended, mat, near, far, after):
+    )(where, tokens, gain, bias, *mats, *near, *far)
+
+
+def to_middle(where, tokens, gain, attended, mat, near, far):
     rows, cols = mat.shape
     return pl.pallas_call(
         middle_kernel,
         out_shape=[
-            jax.ShapeDtypeStruct((4 * rows, cols), jnp.bfloat16),
             jax.ShapeDtypeStruct(tokens.shape, jnp.float32),
             jax.ShapeDtypeStruct(tokens.shape, jnp.bfloat16),
         ],
-        in_specs=[SCALARS] + [WHOLE] * 3 + [ANYWHERE] * 8,
-        out_specs=[WHOLE] * 3,
-        scratch_shapes=[pltpu.SemaphoreType.DMA((7,))],
+        in_specs=[SCALARS] + [WHOLE] * 3 + [ANYWHERE] * 7,
+        out_specs=[WHOLE] * 2,
+        scratch_shapes=[
+            pltpu.VMEM((4 * rows, cols), jnp.bfloat16),
+            pltpu.SemaphoreType.DMA((7,)),
+        ],
         compiler_params=ROOM,
         name="middle",
-    )(where, tokens, gain, attended, mat, *near, *far, after)
-
-
-def backward(core, *arrays):
+    )(where, tokens, gain, attended, mat, *near, *far)
+
+
+def backward(where, *arrays):
     tokens = arrays[0]
     count, features = tokens.shape
     bf16, f32 = jnp.bfloat16, jnp.float32
@@ -415,17 +446,19 @@
             shape((2 * features, features + 128), bf16),
             shape((2 * features, features + 128), bf16),
         ],
-        in_specs=[SCALARS] + [WHOLE] * 20 + [ANYWHERE] * 4,
-        out_specs=[WHOLE] * 4,
+        in_specs=[SCALARS] + [WHOLE] * 20 + [ANYWHERE] * 16,
+        out_specs=[WHOLE] * 2 + [ANYWHERE] * 2,
         scratch_shapes=[
             pltpu.VMEM((4, features, features), bf16),
-            pltpu.VMEM((features, features), bf16),
-            pltpu.VMEM((2, 2 * features, 128), f32),
-            pltpu.SemaphoreType.DMA((4,)),
+            pltpu.VMEM((4, features, features), bf16),
+            pltpu.VMEM((2 * features, 128), f32),
+            pltpu.VMEM((2, 2 * features, 128), bf16),
+            pltpu.SemaphoreType.DMA((28,)),
+            pltpu.SemaphoreType.DMA((5, 8)),
         ],
         compiler_params=ROOM,
         name="backward",
-    )(core, *arrays)
+    )(where, *arrays)
 
 
 def finish_kernel(core_ref, own_ref, other_ref, *refs):
@@ -440,14 +473,16 @@
         here = slice(k * half, (k + 1) * half)
         out[:half, :] = low[here, :features]
         out[half:, :] = high[here, :features]
-    wide = router_out.shape[1]
-    router_out[:half, :] = low[:half, features : features + wide]
-    router_out[half:, :] = high[:half, features : features + wide]
-    small = low[half : 2 * half, features:]
+    small = low[:, features:]
+    tall = router_out.shape[0]
+    router_out[:, :128] = small[:tall, :]
+    router_out[:, 128:] = small[half : half + tall, :64]
     for k in range(2):
-        gains_out[k : k + 1, :128] = small[2 * k : 2 * k + 1, :]
-        gains_out[k : k + 1, 128:] = small[2 * k + 1 : 2 * k + 2, :64]
-    bias_out[...] = small[4 : 4 + bias_out.shape[0], : bias_out.shape[1]]
+        at = 2 * half + 2 * k
+        gains_out[k : k + 1, :128] = small[at : at + 1, :]
+        gains_out[k : k + 1, 128:] = small[at + 1 : at + 2, :64]
+    at = 2 * half + 4
+    bias_out[...] = small[at : at + bias_out.shape[0], : bias_out.shape[1]]
 
 
 def finish(core, own, other, shard_rows, experts_all, bias_shape):
@@ -456,7 +491,7 @@
     return pl.pallas_call(
         finish_kernel,
         out_shape=[shape(shard_rows, features)] * 4
-        + [shape(shard_rows, experts_all), shape(2, shard_rows), shape(*bias_shape)],
+        + [shape(experts_all, shard_rows), shape(2, shard_rows), shape(*bias_shape)],
         in_specs=[SCALARS] + [WHOLE] * 2,
         out_specs=[WHOLE] * 7,
         compiler_params=ROOM,
@@ -469,8 +504,9 @@
     return ((row == places[0:1]) | (row == places[1:2])).astype(jnp.float32).astype(jnp.bfloat16)
 
 
-def dispatch_grads_kernel(capacity, *refs):
-    pieces, (out_ref, places_ref, ids_ref, spots_ref) = refs[:4], refs[4:]
+def dispatch_grads_kernel(capacity, place_ref, *refs):
+    pieces, (out_ref, places_ref, ids_ref, spots_ref) = refs[:4], refs[6:10]
+    gains_ref, bias_ref, router_ref, picks_ref = refs[10:]
     f32, bf16, i32 = jnp.float32, jnp.bfloat16, jnp.int32
     rows = out_ref.shape[0]
     tokens = spots_ref.shape[1]
@@ -505,15 +541,29 @@
     extra = jnp.zeros((rows, 128), f32)
     for e in range(2):
         pick = picks_of(places, e, rows)
+        picks_ref[e] = pick
         out_ref[:, e * features : (e + 1) * features] = jnp.dot(
             pick, line, preferred_element_type=f32
         ).astype(bf16)
         column = jnp.where(lanes == e, sums, 0.0).astype(bf16)
         extra = extra + jnp.dot(pick, column, preferred_element_type=f32)
     out_ref[:, 2 * features :] = extra.astype(bf16)
-
-
-def dispatch_grads(pieces, rows, capacity, tokens):
+    smalls = [p[tokens:, :].astype(f32) for p in pieces]
+    width = features // 4
+    heads = bias_ref.shape[0] // 4
+    for a in range(4):
+        at = (place_ref[0] - a) & 3
+        small = jnp.zeros_like(smalls[0])
+        for k in range(4):
+            small = jnp.where(at == k, smalls[k], small)
+        here = slice(a * width, (a + 1) * width)
+        gains_ref[:, here] = small[0:2, :width]
+        bias_ref[a * heads : (a + 1) * heads, :] = small[2 : 2 + heads, : bias_ref.shape[1]]
+        for b in range(router_ref.shape[0] // 16):
+            router_ref[16 * b : 16 * b + 16, here] = small[16:32, width * b : width * (b + 1)]
+
+
+def dispatch_grads(where, pieces, rows, capacity, tokens, experts_all, bias_shape, after):
     features = pieces[0].shape[1]
     shape = jax.ShapeDtypeStruct
     return pl.pallas_call(
@@ -523,34 +573,37 @@
             shape((2, 4 * tokens), jnp.int32),
             shape((2, 4 * tokens), jnp.int32),
             shape((2, tokens), jnp.int32),
+            shape((2, features), jnp.float32),
+            shape(bias_shape, jnp.float32),
+            shape((experts_all, features), jnp.float32),
+            shape((2, rows, 4 * tokens), jnp.bfloat16),
         ],
-        in_specs=[WHOLE] * 4,
-        out_specs=[WHOLE] * 4,
+        in_specs=[SCALARS] + [WHOLE] * 4 + [ANYWHERE] * 2,
+        out_specs=[WHOLE] * 8,
         compiler_params=ROOM,
         name="dispatch_grads",
-    )(*pieces)
-
-
-def dispatch_kernel(places_ref, *refs):
+    )(where, *pieces, *after)
+
+
+def dispatch_kernel(picks_ref, *refs):
     pieces, out_ref = refs[:4], refs[5]
-    rows = out_ref.shape[0]
     features = pieces[0].shape[1]
     line = jnp.concatenate([p[...] for p in pieces], axis=0)
     for e in range(2):
         out_ref[:, e * features : (e + 1) * features] = jnp.dot(
-            picks_of(places_ref[...], e, rows), line, preferred_element_type=jnp.float32
+            picks_ref[e], line, preferred_element_type=jnp.float32
         ).astype(jnp.bfloat16)
 
 
-def dispatch(places, pieces, rows, after):
+def dispatch(picks, pieces, after):
     return pl.pallas_call(
         dispatch_kernel,
-        out_shape=jax.ShapeDtypeStruct((rows, 2 * pieces[0].shape[1]), jnp.bfloat16),
+        out_shape=jax.ShapeDtypeStruct((picks.shape[1], 2 * pieces[0].shape[1]), jnp.bfloat16),
         in_specs=[WHOLE] * 5 + [ANYWHERE],
         out_specs=WHOLE,
         compiler_params=ROOM,
         name="dispatch",
-    )(places, *pieces, after)
+    )(picks, *pieces, after)
 
 
 def chosen_logit(logits, ids):
@@ -567,30 +620,30 @@
 
 def expert_kernel(x_ref, in_ref, out_ref, ret_ref, act_ref, rise_ref):
     f32, bf16 = jnp.float32, jnp.bfloat16
-    step = 256
     slope = math.sqrt(2.0 / math.pi)
-
-    def chunk(i, carry):
-        at = pl.ds(pl.multiple_of(i * step, step), step)
-        pre = jnp.dot(x_ref[at, :], in_ref[0], preferred_element_type=f32)
-        tanh = jnp.tanh(slope * (pre + 0.044715 * (pre * pre * pre)))
-        active = (0.5 * pre * (1.0 + tanh)).astype(bf16)
-        act_ref[0, at, :] = active
-        ret_ref[at, :] = jnp.dot(active, out_ref[0], preferred_element_type=f32).astype(bf16)
-        rise_ref[0, at, :] = 0.5 * (1.0 + tanh) + 0.5 * pre * (1.0 - tanh * tanh) * (
-            slope * (1.0 + 3.0 * 0.044715 * (pre * pre))
-        )
-        return carry
-
-    lax.fori_loop(0, x_ref.shape[0] // step, chunk, 0)
-
-
-def lanes_of(rows, n):
-    return pl.BlockSpec((rows, n), lambda e: (0, e))
+    pre = jnp.dot(x_ref[...], in_ref[0], preferred_element_type=f32)
+    tanh = jnp.tanh(slope * (pre + 0.044715 * (pre * pre * pre)))
+    active = (0.5 * pre * (1.0 + tanh)).astype(bf16)
+    act_ref[0] = active
+    ret_ref[...] = jnp.dot(active, out_ref[0], preferred_element_type=f32).astype(bf16)
+    rise_ref[0] = 0.5 * (1.0 + tanh) + 0.5 * pre * (1.0 - tanh * tanh) * (
+        slope * (1.0 + 3.0 * 0.044715 * (pre * pre))
+    )
+
+
+STEP = 256
+
+
+def lanes_of(n):
+    return pl.BlockSpec((STEP, n), lambda e, i: (i, e))
+
+
+def rows_of(n):
+    return pl.BlockSpec((1, STEP, n), lambda e, i: (e, i, 0))
 
 
 def one_of(a, b):
-    return pl.BlockSpec((1, a, b), lambda e: (e, 0, 0))
+    return pl.BlockSpec((1, a, b), lambda e, i: (e, 0, 0))
 
 
 def experts(arrived, w_in, w_out):
@@ -598,49 +651,64 @@
     features, hidden = w_in.shape[1:]
     return pl.pallas_call(
         expert_kernel,
-        grid=(2,),
+        grid=(2, rows // STEP),
         out_shape=[
             jax.ShapeDtypeStruct((rows, 2 * features), jnp.bfloat16),
             jax.ShapeDtypeStruct((2, rows, hidden), jnp.bfloat16),
             jax.ShapeDtypeStruct((2, rows, hidden), jnp.float32),
         ],
-        in_specs=[lanes_of(rows, features), one_of(features, hidden), one_of(hidden, features)],
-        out_specs=[lanes_of(rows, features), one_of(rows, hidden), one_of(rows, hidden)],
+        in_specs=[lanes_of(features), one_of(features, hidden), one_of(hidden, features)],
+        out_specs=[lanes_of(features), rows_of(hidden), rows_of(hidden)],
         compiler_params=ROOM,
         name="experts",
     )(arrived, w_in, w_out)
 
 
+def early_kernel(g_ref, out_ref, back_ref):
+    back_ref[0] = lax.dot_general(
+        g_ref[...], out_ref[0], LAST, preferred_element_type=jnp.float32
+    )
+
+
+def early_product(grad_wide, w_out, after):
+    rows = grad_wide.shape[0]
+    hidden, features = w_out.shape[1:]
+    return pl.pallas_call(
+        lambda g, w, _, out: early_kernel(g, w, out),
+        grid=(2, rows // STEP),
+        out_shape=jax.ShapeDtypeStruct((2, rows, hidden), jnp.float32),
+        in_specs=[lanes_of(features), one_of(hidden, features), ANYWHERE],
+        out_specs=rows_of(hidden),
+        compiler_params=ROOM,
+        name="early_product",
+    )(grad_wide, w_out, after)
+
+
 def expert_back_kernel(
-    capacity, own_ref, x_ref, g_ref, ids_ref, in_ref, out_ref, router_ref, rise_ref, *refs
+    capacity, own_ref, x_ref, g_ref, ids_ref, in_ref, router_ref, rise_ref, back_ref, *refs
 ):
     pre_ref, arr_ref, outs, held = refs[0], refs[1], refs[2:6], refs[6]
     f32, bf16, i32 = jnp.float32, jnp.bfloat16, jnp.int32
     e = pl.program_id(0)
     own = own_ref[0] + e
     rows = x_ref.shape[0]
-    step = 256
 
     def chunk(i, carry):
-        at = pl.ds(pl.multiple_of(i * step, step), step)
+        at = pl.ds(pl.multiple_of(i * STEP, STEP), STEP)
         ids = ids_ref[at, :].astype(f32)
         lanes = lax.broadcasted_iota(i32, ids.shape, 1)
         other = jnp.sum(jnp.where(lanes == e, ids, 0.0), axis=1, keepdims=True).astype(i32) - own
-        logits = lax.dot_general(
-            x_ref[at, :], router_ref[...], LAST, preferred_element_type=f32
-        )
+        logits = lax.dot_general(x_ref[at, :], router_ref[...], LAST, preferred_element_type=f32)
         gate, _ = gate_pair(chosen_logit(logits, own), chosen_logit(logits, other))
-        grown = (gate * g_ref[at, :].astype(f32)).astype(bf16)
-        arr_ref[0, at, :] = grown
-        back = lax.dot_general(grown, out_ref[0], LAST, preferred_element_type=f32)
-        grad = (back * rise_ref[0, at, :]).astype(bf16)
+        arr_ref[0, at, :] = (gate * g_ref[at, :].astype(f32)).astype(bf16)
+        grad = (gate * back_ref[0, at, :] * rise_ref[0, at, :]).astype(bf16)
         pre_ref[0, at, :] = grad
         held[at, :] = lax.dot_general(grad, in_ref[0], LAST, preferred_element_type=f32).astype(
             bf16
         )
         return carry
 
-    lax.fori_loop(0, rows // step, chunk, 0)
+    lax.fori_loop(0, rows // STEP, chunk, 0)
     part = rows // 4
     here = lax.broadcasted_iota(i32, (part, rows), 0)
     there = lax.broadcasted_iota(i32, (part, rows), 1)
@@ -651,12 +719,14 @@
         out[...] = jnp.dot(pick, held[...], preferred_element_type=f32).astype(bf16)
 
 
-def experts_back(own, arrived, grad_wide, w_in, w_out, router_w, rise, capacity):
+def experts_back(own, arrived, grad_wide, w_in, router_w, rise, back, capacity):
     rows = arrived.shape[0]
     features, hidden = w_in.shape[1:]
     bf16 = jnp.bfloat16
     shape = jax.ShapeDtypeStruct
     part = rows // 4
+    lanes = lambda n: pl.BlockSpec((rows, n), lambda e: (0, e))
+    one = lambda a, b: pl.BlockSpec((1, a, b), lambda e: (e, 0, 0))
     return pl.pallas_call(
         functools.partial(expert_back_kernel, capacity),
         grid=(2,),
@@ -664,20 +734,20 @@
         + [shape((2 * part, features), bf16)] * 4,
         in_specs=[
             SCALARS,
-            lanes_of(rows, features),
-            lanes_of(rows, features),
+            lanes(features),
+            lanes(features),
             pl.BlockSpec((rows, 128), lambda e: (0, 2 * features // 128)),
-            one_of(features, hidden),
-            one_of(hidden, features),
+            one(features, hidden),
             pl.BlockSpec(router_w.shape, lambda e: (0, 0)),
-            one_of(rows, hidden),
+            one(rows, hidden),
+            one(rows, hidden),
         ],
-        out_specs=[one_of(rows, hidden), one_of(rows, features)]
+        out_specs=[one(rows, hidden), one(rows, features)]
         + [pl.BlockSpec((part, features), lambda e: (e, 0))] * 4,
         scratch_shapes=[pltpu.VMEM((rows, features), bf16)],
         compiler_params=ROOM,
         name="experts_back",
-    )(own[None], arrived, grad_wide, grad_wide, w_in, w_out, router_w, rise)
+    )(own[None], arrived, grad_wide, grad_wide, w_in, router_w, rise, back)
 
 
 def weight_grads_kernel(x_ref, pre_ref, act_ref, arr_ref, in_ref, out_ref):
@@ -826,27 +896,26 @@
         routes.T, jnp.stack([gain_attn, gain_moe]), rel_bias, w_router.T, cotangent
     )
     line_grads = along_x(line)
-    near_qkv = along_x(pack(core, (w_query, w_key, w_value), line))[1:]
-    order = (shard - jnp.arange(4)) % 4
-    small = jnp.take(jnp.stack([p[row_count:] for p in line_grads]), order, axis=0)
-    gain_one = small[:, 0, :shard_rows].reshape(1, features)
-    gain_two = small[:, 1, :shard_rows].reshape(1, features)
-    bias_table = small[:, 2:5, :bucket_count].reshape(head_count, bucket_count)
-    router_w = (
-        small[:, 16:]
-        .reshape(4, 16, expert_count // 16, shard_rows)
-        .transpose(2, 1, 0, 3)
-        .reshape(expert_count, features)
-    )
-
+    sent_qkv = pack(core, (w_query, w_key, w_value), line)
+    near_qkv = along_x(sent_qkv)[1:]
+    sent_out = pack(core, (w_output,), sent_qkv)
+    near_out = along_x(sent_out)[1:]
     def to_owners(outgoing):
         return lax.all_to_all(outgoing, ("y", "z", "c"), 0, 0, tiled=True)
 
-    outgoing_grads, places, ids, spots = dispatch_grads(
-        line_grads, slot_rows, capacity, row_count
-    )
+    outgoing_grads, places, ids, spots, gains, bias_table, router_f, picks = dispatch_grads(
+        where,
+        line_grads,
+        slot_rows,
+        capacity,
+        row_count,
+        expert_count,
+        (head_count, bucket_count),
+        (sent_qkv, sent_out),
+    )
+    gain_one, gain_two = gains[0:1], gains[1:2]
+    bias_table, router_w = bias_table.astype(bf16), router_f.astype(bf16)
     grad_wide = to_owners(outgoing_grads)
-    near_out = along_x(pack(core, (w_output,), outgoing_grads))[1:]
     first_expert = 2 * lax.axis_index(("y", "z", "c")).astype(jnp.int32)
 
     segments = row_segments(seq_lengths[0], row_count)
@@ -856,7 +925,7 @@
     masked_bias = jnp.where(allowed[None], position_bias, -1000000000.0)
     far_qkv = [swap_core(part) for part in near_qkv]
     far_out = [swap_core(part) for part in near_out]
-    query_w, key_w, value_w, hidden_one, queries, key_rows, value_rows, probs, attended = attend(
+    hidden_one, queries, key_rows, value_rows, probs, attended = attend(
         where,
         tokens,
         gain_one,
@@ -864,27 +933,27 @@
         (w_query, w_key, w_value),
         near_qkv,
         far_qkv,
-        outgoing_grads,
-    )
-    output_w, middle, moe_in = to_middle(
-        where, tokens, gain_two, attended, w_output, near_out, far_out, outgoing_grads
+    )
+    middle, moe_in = to_middle(
+        where, tokens, gain_two, attended, w_output, near_out, far_out
     )
 
     line_moe = along_x(moe_in)
-    arrived = to_owners(dispatch(places, line_moe, slot_rows, grad_wide))
+    outgoing = dispatch(picks, line_moe, grad_wide)
+    arrived = to_owners(outgoing)
+    early = early_product(grad_wide, w_out, outgoing)
     ret, active, rise = experts(arrived, w_in, w_out)
     returned = to_owners(ret)
     grad_pre, grad_arrived, *blocks = experts_back(
-        first_expert, arrived, grad_wide, w_in, w_out, router_w, rise, capacity
+        first_expert, arrived, grad_wide, w_in, router_w, rise, early, capacity
     )
     summed = [blocks[0]] + [shift_x(blocks[r], -r) for r in range(1, 4)]
     grad_w_in, grad_w_out = weight_grads(arrived, grad_pre, active, grad_arrived)
-    rows_home = sum_rows(summed, capacity, (grad_w_in, grad_w_out))
-    back_rows = to_owners(rows_home)
-    bundle = combine(places, ids, router_w, returned, line_grads, line_moe, rows_home)
+    bundle = combine(places, ids, router_w, returned, line_grads, line_moe, grad_w_in)
+    back_rows = to_owners(sum_rows(summed, capacity, (grad_w_out, bundle[0])))
     homes = [bundle[0]] + [shift_x(bundle[r], -r) for r in range(1, 4)]
     result, grad_tokens, kept, given = backward(
-        core[None],
+        where,
         tokens,
         cotangent,
         gain_one,
@@ -902,10 +971,14 @@
         spots,
         back_rows,
         *homes,
-        query_w,
-        key_w,
-        value_w,
-        output_w,
+        w_query,
+        w_key,
+        w_value,
+        w_output,
+        *near_qkv,
+        *far_qkv,
+        *near_out,
+        *far_out,
     )
     piece = shard_rows // 8
     wide = features + 128
@@ -922,6 +995,7 @@
     *totals, router_total, gain_totals, bias_total = finish(
         core[None], half, swap_core(half), shard_rows, expert_count, rel_bias.shape
     )
+    router_total = router_total.T
     gain_one_total, gain_two_total = gain_totals[0], gain_totals[1]
     return (
         result,

time: 315 us -> 327 us (1.038)
  waiting for transfers between devices: 63 us -> 73.5 us
  Pallas kernels: 86.5 us -> 94.6 us
  local copies, waits for them, and re-layouts: 17.3 us -> 10.5 us
    ppermute x18, waiting for transfers between devices: 49.6 us -> 66.8 us  [shift(): lax.ppermute(block, axis, [(i, (i + step) % ranks) for i in range(ranks)])]
    pallas_call x4 -> x5, Pallas kernels: 25.7 us -> 33.2 us  [the longest x1 11 us: experts(): pl.pallas_call(expert_kernel, grid=(2, rows // STEP), out_shape=[jax.Shap...]
    all_to_all x3, waiting for transfers between devices: 6.77 us -> 0.01 us  [to_owners(): return lax.all_to_all(outgoing, ('y', 'z', 'c'), 0, 0, tiled=True)]
    another operation x6 -> x0, local copies, waits for them, and re-layouts: 4.53 us -> none  [the longest x4 3.21 us: layer(): jnp.stack([p[row_count:] for p in line_grads])]
    unnamed x51 -> x66, local copies, waits for them, and re-layouts: 8.43 us -> 7.18 us
  transfers between devices with their start and end apart: 29 -> 29, of which waited for: 14 -> 14; matrix products, arithmetic and copies ran while one was open for 3% -> 1% of each run, Pallas kernels for 16% -> 15%
where the time goes in v2:
time: 327 us; the launch traced here: 326 us
  blocking collectives  96 us (29%)
  Pallas kernels  94.6 us (29%)
  waiting for transfers between devices  73.5 us (22%)
  starting transfers between devices  43.1 us (13%)
  local copies, waits for them, and re-layouts  10.5 us (3%)
  other arithmetic  6.58 us (2%)
    ppermute x18, waiting for transfers between devices, shift(): lax.ppermute(block, axis, [(i, (i + step) % ranks) for i in range(ranks)])  66.8 us
    all_to_all x1, blocking collectives, layer(): spread = lax.all_to_all(paired, ('y', 'x', 'z'), 0, 0, tiled=True)  43.5 us
    all_to_all x1, blocking collectives, to_owners(): return lax.all_to_all(outgoing, ('y', 'z', 'c'), 0, 0, tiled=True)  39.4 us
    all_to_all x3, starting transfers between devices, to_owners(): return lax.all_to_all(outgoing, ('y', 'z', 'c'), 0, 0, tiled=True)  20.4 us
    ppermute x18, starting transfers between devices, shift(): lax.ppermute(block, axis, [(i, (i + step) % ranks) for i in range(ranks)])  15.9 us
    pallas_call x1, Pallas kernels, backward(): pl.pallas_call(backward_kernel, out_shape=[shape((count, features), bf16)...  15.7 us
    all_to_all x1, blocking collectives, layer(): lax.all_to_all(jnp.broadcast_to(mine[None], (16, piece, wide)).reshape(16...  13.1 us
    pallas_call x1, Pallas kernels, experts_back(): pl.pallas_call(functools.partial(expert_back_kernel, capacity), grid=(2,)...  12.3 us
  transfers between devices with their start and end apart: 29, of which 14 were waited for; matrix products, arithmetic and copies ran while one was open for 1% of the time, Pallas kernels for 15%

profile of v2, /device:TPU:1, one launch (start us, length us, event | category | flops | bytes accessed | tf_op | source)
XLA Modules:
  0.0 325.8 jit_solution(15646271880620150799)
XLA Ops:
  2.5 2.4 line.1.refs_3_.refs_0_
  5.0 3.4 %collective-permute-start.2 = (bf16[160,768]{1,0:T(8,128)(2,1)}, bf16[160,768]{1,0:T(8,128)(2,1)S(1)}, u32[]{:S(2)}, u32[]{:S(2)}) collective-permute-start(bf16[160,768]{1,0:T(8,128)(2,1)} %line.1.refs_3_.refs_0_), channel_id=1, source_target_pairs={{0,3},{1,0},{2,1},{3,2},{4,7},{5,4},{6,5},{7,6},{8,11},{9,8},{10,9... | collective-permute-start | bytes 737288 | tf_op jit(solution)/shard_map/ppermute | solution.py:34
  9.5 1.8 pack.2.refs_1_.refs_4_
  11.3 1.6 pack.3.refs_5_
  13.5 1.0 collective-permute-done.2.refs_3_
  14.5 2.1 collective-permute-done.1.refs_2_
  16.6 6.6 %collective-permute-done.refs_1_ = bf16[160,768]{1,0:T(8,128)(2,1)S(1)} collective-permute-done((bf16[160,768]{1,0:T(8,128)(2,1)}, bf16[160,768]{1,0:T(8,128)(2,1)S(1)}, u32[]{:S(2)}, u32[]{:S(2)}) %collective-permute-start) | collective-permute-done | bytes 245792 | tf_op jit(solution)/shard_map/ppermute | solution.py:34
  23.9 5.5 %dispatch_grads.1 = (bf16[768,1664]{1,0:T(8,128)(2,1)}, s32[2,512]{1,0:T(2,128)}, s32[2,512]{1,0:T(2,128)}, s32[2,128]{1,0:T(2,128)}, f32[2,768]{1,0:T(2,128)}, ...) custom-call(s32[2]{0:T(128)} %pad_add_fusion.place_ref, bf16[160,768]{1,0:T(8,128)(2,1)} %line.1.refs_3_.refs_0_, ...), custom_call_target="tpu_custom_call" | custom-call | tf_op jit(solution)/shard_map/dispatch_grads/pallas_call | solution.py:569
  29.5 8.7 %all-to-all-start = ((bf16[32,24,1664]{2,1,0:T(8,128)(2,1)}), bf16[32,24,1664]{2,1,0:T(8,128)(2,1)S(1)}, u32[]{:S(2)}, u32[]{:S(2)}) async-start(bf16[32,24,1664]{2,1,0:T(8,128)(2,1)} %bitcast.37), calls=%async_computation | async-start | bytes 5111808 | tf_op jit(solution)/shard_map/all_to_all | solution.py:904
  39.1 3.0 collective-permute-start.5
  43.4 13.1 %collective-permute-done.5.refs_5_.refs_10_ = bf16[288,768]{1,0:T(8,128)(2,1)S(1)} collective-permute-done((bf16[288,768]{1,0:T(8,128)(2,1)S(1)}, bf16[288,768]{1,0:T(8,128)(2,1)S(1)}, u32[]{:S(2)}, u32[]{:S(2)}) %collective-permute-start.5) | collective-permute-done | bytes 442400 | tf_op jit(solution)/shard_map/ppermute | solution.py:34
  56.5 1.6 collective-permute-start.8
  58.7 6.6 %collective-permute-done.3.refs_3_.refs_8_ = bf16[288,768]{1,0:T(8,128)(2,1)} collective-permute-done((bf16[288,768]{1,0:T(8,128)(2,1)S(1)}, bf16[288,768]{1,0:T(8,128)(2,1)}, u32[]{:S(2)}, u32[]{:S(2)}) %collective-permute-start.3) | collective-permute-done | bytes 442400 | tf_op jit(solution)/shard_map/ppermute | solution.py:34
  65.9 1.2 copy_select_fusion.bias_ref
  67.1 1.2 collective-permute-done.9.refs_1_.refs_14_
  70.6 6.8 %attend.1 = (bf16[128,768]{1,0:T(8,128)(2,1)}, bf16[128,768]{1,0:T(8,128)(2,1)}, bf16[128,768]{1,0:T(8,128)(2,1)}, bf16[128,768]{1,0:T(8,128)(2,1)}, f32[12,128,128]{2,1,0:T(8,128)}, /*index=5*/bf16[128,768]{1,0:T(8,128)(2,1)}) custom-call(s32[2]{0:T(128)} %pad_add_fusion.place_ref, bf16[128,768]{1,0:T(8,128)(2,1)} %tokens_ref.5, ...), custom_call_target="tpu_custom_call" | custom-call | tf_op jit(solution)/shard_map/attend/pallas_call | solution.py:403
  78.1 3.5 %middle.1 = (f32[128,768]{1,0:T(8,128)}, bf16[128,768]{1,0:T(8,128)(2,1)}) custom-call(s32[2]{0:T(128)} %pad_add_fusion.place_ref, bf16[128,768]{1,0:T(8,128)(2,1)} %tokens_ref.5, f32[1,768]{1,0:T(1,128)} %get-tuple-element.96.gain_ref.gain_two_ref, bf16[128,768]{1,0:T(8,128)(2,1)} %get-tuple-element.58.attended_ref, bf16[192,768]{1,0:T(8,128)(2,1)} %refs_7_.1, ...), custom_call_target="tpu_custom_call" | custom-call | tf_op jit(solution)/shard_map/middle/pallas_call | solution.py:419
  81.7 2.8 collective-permute-start.17
  85.1 7.9 %collective-permute-done.17.refs_3_.refs_7_ = bf16[128,768]{1,0:T(8,128)(2,1)S(1)} collective-permute-done((bf16[128,768]{1,0:T(8,128)(2,1)}, bf16[128,768]{1,0:T(8,128)(2,1)S(1)}, u32[]{:S(2)}, u32[]{:S(2)}) %collective-permute-start.17) | collective-permute-done | bytes 196640 | tf_op jit(solution)/shard_map/ppermute | solution.py:34
  93.0 3.6 %collective-permute-done.15.refs_1_.refs_5_ = bf16[128,768]{1,0:T(8,128)(2,1)S(1)} collective-permute-done((bf16[128,768]{1,0:T(8,128)(2,1)}, bf16[128,768]{1,0:T(8,128)(2,1)S(1)}, u32[]{:S(2)}, u32[]{:S(2)}) %collective-permute-start.15) | collective-permute-done | bytes 196640 | tf_op jit(solution)/shard_map/ppermute | solution.py:34
  97.3 0.8 copy-done
  98.2 4.5 %dispatch.1._ = bf16[768,1536]{1,0:T(8,128)(2,1)} custom-call(bf16[2,768,512]{2,1,0:T(8,128)(2,1)} %get-tuple-element.67.picks_ref, bf16[128,768]{1,0:T(8,128)(2,1)} %get-tuple-element.60.refs_0_.refs_4_.moe_ref, bf16[128,768]{1,0:T(8,128)(2,1)} %copy-done.14, bf16[128,768]{1,0:T(8,128)(2,1)} %copy-done.13, bf16[128,768]{1,0:T(8,128)(2,1)} %copy-done.12, ...), custom_call_target="tpu_custom_call" | custom-call | tf_op jit(solution)/shard_map/dispatch/pallas_call | solution.py:599
  102.6 39.4 %all_to_all.61 = bf16[32,24,1536]{2,1,0:T(8,128)(2,1)} all-to-all(bf16[32,24,1536]{2,1,0:T(8,128)(2,1)} %bitcast.30), channel_id=1, replica_groups=mesh['y'=4,'z'=4,'c'=2,'x'=4] {'y','z','c'}, dimensions={0} | all-to-all | bytes 4718592 | tf_op jit(solution)/shard_map/all_to_all | solution.py:904
  142.0 11.0 %experts.1 = (bf16[768,1536]{1,0:T(8,128)(2,1)}, bf16[2,768,768]{2,1,0:T(8,128)(2,1)}, f32[2,768,768]{2,1,0:T(8,128)}) custom-call(bf16[768,1536]{1,0:T(8,128)(2,1)} %bitcast.27, bf16[2,768,768]{2,1,0:T(8,128)(2,1)} %in_ref.3, bf16[2,768,768]{2,1,0:T(8,128)(2,1)} %w.1), custom_call_target="tpu_custom_call" | custom-call | tf_op jit(solution)/shard_map/experts/pallas_call | solution.py:652
  152.9 4.0 %all-to-all-start.2 = ((bf16[32,24,1536]{2,1,0:T(8,128)(2,1)}), bf16[32,24,1536]{2,1,0:T(8,128)(2,1)S(1)}, u32[]{:S(2)}, u32[]{:S(2)}) async-start(bf16[32,24,1536]{2,1,0:T(8,128)(2,1)} %bitcast.38), calls=%async_computation.2 | async-start | bytes 4718592 | tf_op jit(solution)/shard_map/all_to_all | solution.py:904
  157.7 7.4 %early_product.1.back_ref = f32[2,768,768]{2,1,0:T(8,128)} custom-call(bf16[768,1664]{1,0:T(8,128)(2,1)} %bitcast.24, bf16[2,768,768]{2,1,0:T(8,128)(2,1)} %w.1, bf16[768,1536]{1,0:T(8,128)(2,1)} %dispatch.1._), custom_call_target="tpu_custom_call" | custom-call | tf_op jit(solution)/shard_map/early_product/pallas_call | solution.py:676
  165.1 12.3 %experts_back.1 = (bf16[2,768,768]{2,1,0:T(8,128)(2,1)}, bf16[2,768,768]{2,1,0:T(8,128)(2,1)}, bf16[384,768]{1,0:T(8,128)(2,1)}, bf16[384,768]{1,0:T(8,128)(2,1)...) custom-call(s32[1]{0:T(128)} %bitcast.7.own_ref, bf16[768,1536]{1,0:T(8,128)(2,1)} %bitcast.28, ...), custom_call_target="tpu_custom_call" | custom-call | tf_op jit(solution)/shard_map/experts_back/pallas_call | solution.py:730
  178.1 0.8 collective-permute-start.20
  178.9 10.0 %weight_grads.1 = (f32[2,768,768]{2,1,0:T(8,128)}, f32[2,768,768]{2,1,0:T(8,128)}) custom-call(bf16[768,1536]{1,0:T(8,128)(2,1)} %bitcast.29, bf16[2,768,768]{2,1,0:T(8,128)(2,1)} %get-tuple-element.74.pre_ref, bf16[2,768,768]{2,1,0:T(8,128)(2,1)} %get-tuple-element.75.act_ref, bf16[2,768,768]{2,1,0:T(8,128)(2,1)} %get-tuple-element.76.arr_ref), custom_call_target="tpu_custom_call" | custom-call | flops 3623878656 | bytes 20000000 | tf_op jit(solution)/shard_map/weight_grads/pallas_call | solution.py:765
  189.0 1.4 copy-done.1
  190.4 5.9 %combine.1 = (bf16[128,896]{1,0:T(8,128)(2,1)}, bf16[128,896]{1,0:T(8,128)(2,1)}, bf16[128,896]{1,0:T(8,128)(2,1)}, bf16[128,896]{1,0:T(8,128)(2,1)}) custom-call(s32[2,512]{1,0:T(2,128)} %get-tuple-element.78.places_ref, s32[2,512]{1,0:T(2,128)} %get-tuple-element.55.ids_ref, bf16[64,768]{1,0:T(8,128)(2,1)} %convert_element_type.24.router_ref, ...), custom_call_target="tpu_custom_call" | custom-call | tf_op jit(solution)/shard_map/combine/pallas_call | solution.py:854
  196.3 11.5 %collective-permute-done.20.refs_3_ = bf16[384,768]{1,0:T(8,128)(2,1)} collective-permute-done((bf16[384,768]{1,0:T(8,128)(2,1)}, bf16[384,768]{1,0:T(8,128)(2,1)}, u32[]{:S(2)}, u32[]{:S(2)}) %collective-permute-start.20) | collective-permute-done | bytes 589856 | tf_op jit(solution)/shard_map/ppermute | solution.py:34
  207.8 3.4 %sum_rows.1 = bf16[512,768]{1,0:T(8,128)(2,1)} custom-call(bf16[384,768]{1,0:T(8,128)(2,1)} %get-tuple-element.70.refs_0_, bf16[384,768]{1,0:T(8,128)(2,1)} %copy-done.16, bf16[384,768]{1,0:T(8,128)(2,1)} %copy-done.17, bf16[384,768]{1,0:T(8,128)(2,1)} %collective-permute-done.20.refs_3_, f32[2,768,768]{2,1,0:T(8,128)} %get-tuple-element.53.refs_4_, ...), custom_call_target="tpu_custom_call" | custom-call | tf_op jit(solution)/shard_map/sum_rows/pallas_call | solution.py:806
  211.2 7.6 %all-to-all-start.3 = ((bf16[32,16,768]{2,1,0:T(8,128)(2,1)}), bf16[32,16,768]{2,1,0:T(8,128)(2,1)S(1)}, u32[]{:S(2)}, u32[]{:S(2)}) async-start(bf16[32,16,768]{2,1,0:T(8,128)(2,1)} %bitcast.34), calls=%async_computation.3 | async-start | bytes 1572864 | tf_op jit(solution)/shard_map/all_to_all | solution.py:904
  218.8 1.0 collective-permute-start.21
  220.7 5.2 %collective-permute-done.21.refs_1_ = bf16[128,896]{1,0:T(8,128)(2,1)S(1)} collective-permute-done((bf16[128,896]{1,0:T(8,128)(2,1)S(1)}, bf16[128,896]{1,0:T(8,128)(2,1)S(1)}, u32[]{:S(2)}, u32[]{:S(2)}) %collective-permute-start.21) | collective-permute-done | bytes 229408 | tf_op jit(solution)/shard_map/ppermute | solution.py:34
  225.9 2.2 collective-permute-done.22.refs_2_
  228.1 5.7 %collective-permute-done.23.refs_3_ = bf16[128,896]{1,0:T(8,128)(2,1)S(1)} collective-permute-done((bf16[128,896]{1,0:T(8,128)(2,1)S(1)}, bf16[128,896]{1,0:T(8,128)(2,1)S(1)}, u32[]{:S(2)}, u32[]{:S(2)}) %collective-permute-start.23) | collective-permute-done | bytes 229408 | tf_op jit(solution)/shard_map/ppermute | solution.py:34
  234.8 15.7 %backward.1 = (bf16[128,768]{1,0:T(8,128)(2,1)}, f32[128,768]{1,0:T(8,128)}, bf16[1536,896]{1,0:T(8,128)(2,1)}, bf16[1536,896]{1,0:T(8,128)(2,1)}) custom-call(s32[2]{0:T(128)} %pad_add_fusion.place_ref, bf16[128,768]{1,0:T(8,128)(2,1)} %tokens_ref.5, bf16[128,768]{1,0:T(8,128)(2,1)} %cotangent_ref.3, f32[1,768]{1,0:T(1,128)} %get-tuple-element.97.gain_ref.gain_one_ref, ...), custom_call_target="tpu_custom_call" | custom-call | tf_op jit(solution)/shard_map/backward/pallas_call | solution.py:441
  251.0 4.9 %collective-permute-done.24 = bf16[1536,896]{1,0:T(8,128)(2,1)S(1)} collective-permute-done((bf16[1536,896]{1,0:T(8,128)(2,1)}, bf16[1536,896]{1,0:T(8,128)(2,1)S(1)}, u32[]{:S(2)}, u32[]{:S(2)}) %collective-permute-start.24) | collective-permute-done | bytes 2752544 | tf_op jit(solution)/shard_map/ppermute | solution.py:42
  256.0 2.5 add_convert_fusion
  258.5 43.5 %all_to_all.62 = bf16[64,24,896]{2,1,0:T(8,128)(2,1)S(1)} all-to-all(bf16[64,24,896]{2,1,0:T(8,128)(2,1)S(1)} %bitcast.31), channel_id=1, replica_groups=mesh['y'=4,'z'=4,'c'=2,'x'=4] {'y','x','z'}, dimensions={0} | all-to-all | bytes 5505024 | tf_op jit(solution)/shard_map/all_to_all | solution.py:986
  302.4 13.1 %all_to_all.63 = bf16[16,24,896]{2,1,0:T(8,128)(2,1)S(1)} all-to-all(bf16[16,24,896]{2,1,0:T(8,128)(2,1)S(1)} %broadcast_in_dim.15), channel_id=1, replica_groups=mesh['y'=4,'z'=4,'c'=2,'x'=4] {'y','z'}, dimensions={0} | all-to-all | bytes 1376256 | tf_op jit(solution)/shard_map/all_to_all | solution.py:988
  315.6 3.5 %collective-permute-start.25 = (bf16[384,896]{1,0:T(8,128)(2,1)S(1)}, bf16[384,896]{1,0:T(8,128)(2,1)S(1)}, u32[]{:S(2)}, u32[]{:S(2)}) collective-permute-start(bf16[384,896]{1,0:T(8,128)(2,1)S(1)} %bitcast.35), channel_id=1, source_target_pairs={{0,4},{4,0},{1,5},{5,1},{2,6},{6,2},{3,7},{7,3},{8,12},{12,8},{9,1... | collective-permute-start | bytes 2064392 | tf_op jit(solution)/shard_map/ppermute | solution.py:42
  319.1 1.8 collective-permute-done.25.other_ref
  320.8 0.9 copy-done.15
  321.7 2.8 finish.1
  324.5 1.3 fusion.5
  (111 shorter events, 16.1 us)
Async XLA Ops:
  5.0 9.5 %collective-permute-start.2 = (bf16[160,768]{1,0:T(8,128)(2,1)}, bf16[160,768]{1,0:T(8,128)(2,1)S(1)}, u32[]{:S(2)}, u32[]{:S(2)}) collective-permute-start(bf16[160,768]{1,0:T(8,128)(2,1)} %line.1.refs_3_.refs_0_), channel_id=1, source_target_pairs={{0,3},{1,0},{2,1},{3,2},{4,7},{5,4},{6,5},{7,6},{8,11},{9,8},{10,9... | collective-permute-start | bytes 737288 | tf_op jit(solution)/shard_map/ppermute | solution.py:34
  8.4 8.3 %collective-permute-start.1 = (bf16[160,768]{1,0:T(8,128)(2,1)}, bf16[160,768]{1,0:T(8,128)(2,1)S(1)}, u32[]{:S(2)}, u32[]{:S(2)}) collective-permute-start(bf16[160,768]{1,0:T(8,128)(2,1)} %line.1.refs_3_.refs_0_), channel_id=1, source_target_pairs={{0,2},{1,3},{2,0},{3,1},{4,6},{5,7},{6,4},{7,5},{8,10},{9,11},{10,... | collective-permute-start | bytes 737288 | tf_op jit(solution)/shard_map/ppermute | solution.py:34
  8.9 14.3 %collective-permute-start = (bf16[160,768]{1,0:T(8,128)(2,1)}, bf16[160,768]{1,0:T(8,128)(2,1)S(1)}, u32[]{:S(2)}, u32[]{:S(2)}) collective-permute-start(bf16[160,768]{1,0:T(8,128)(2,1)} %line.1.refs_3_.refs_0_), channel_id=1, source_target_pairs={{0,1},{1,2},{2,3},{3,0},{4,5},{5,6},{6,7},{7,4},{8,9},{9,10},{10,1... | collective-permute-start | bytes 737288 | tf_op jit(solution)/shard_map/ppermute | solution.py:34
  14.5 8.7 %copy-start.9 = (bf16[160,768]{1,0:T(8,128)(2,1)}, bf16[160,768]{1,0:T(8,128)(2,1)S(1)}, u32[]{:S(2)}) copy-start(bf16[160,768]{1,0:T(8,128)(2,1)S(1)} %collective-permute-done.2.refs_3_) | copy-start | bytes 737284
  16.6 6.6 %copy-start.10 = (bf16[160,768]{1,0:T(8,128)(2,1)}, bf16[160,768]{1,0:T(8,128)(2,1)S(1)}, u32[]{:S(2)}) copy-start(bf16[160,768]{1,0:T(8,128)(2,1)S(1)} %collective-permute-done.1.refs_2_) | copy-start | bytes 737284
  29.4 9.7 %copy-start.2 = (bf16[288,768]{1,0:T(8,128)(2,1)S(1)}, bf16[288,768]{1,0:T(8,128)(2,1)}, u32[]{:S(2)}) copy-start(bf16[288,768]{1,0:T(8,128)(2,1)} %pack.2.refs_1_.refs_4_) | copy-start | bytes 1327108
  29.4 13.3 %copy-start.32 = (s32[1,4]{1,0:T(1,128)S(1)}, s32[1,4]{1,0:T(1,128)}, u32[]{:S(2)}) copy-start(s32[1,4]{1,0:T(1,128)} %param.16) | copy-start | bytes 52
  29.4 13.6 %copy-start.28 = (s32[31]{0:T(128)S(1)}, s32[31]{0:T(128)}, u32[]{:S(2)}) copy-start(s32[31]{0:T(128)} %constant.33.clone) | copy-start | bytes 376
  29.5 28.6 %copy-start.26 = (f32[12,32]{1,0:T(8,128)S(1)}, f32[12,32]{1,0:T(8,128)}, u32[]{:S(2)}) copy-start(f32[12,32]{1,0:T(8,128)} %get-tuple-element.57) | copy-start | bytes 4612
  29.5 67.2 %all-to-all-start = ((bf16[32,24,1664]{2,1,0:T(8,128)(2,1)}), bf16[32,24,1664]{2,1,0:T(8,128)(2,1)S(1)}, u32[]{:S(2)}, u32[]{:S(2)}) async-start(bf16[32,24,1664]{2,1,0:T(8,128)(2,1)} %bitcast.37), calls=%async_computation | async-start | bytes 5111808 | tf_op jit(solution)/shard_map/all_to_all | solution.py:904
  38.2 30.8 %copy-start.27 = (f32[2,768]{1,0:T(2,128)S(1)}, f32[2,768]{1,0:T(2,128)}, u32[]{:S(2)}) copy-start(f32[2,768]{1,0:T(2,128)} %get-tuple-element.54) | copy-start | bytes 18436
  38.2 20.3 %collective-permute-start.11 = (bf16[96,768]{1,0:T(8,128)(2,1)}, bf16[96,768]{1,0:T(8,128)(2,1)}, u32[]{:S(2)}, u32[]{:S(2)}) collective-permute-start(bf16[96,768]{1,0:T(8,128)(2,1)} %pack.3.refs_5_), channel_id=1, source_target_pairs={{0,3},{1,0},{2,1},{3,2},{4,7},{5,4},{6,5},{7,6},{8,11},{9,8},{10,9... | collective-permute-start | bytes 442376 | tf_op jit(solution)/shard_map/ppermute | solution.py:34
  38.8 28.4 %collective-permute-start.10 = (bf16[96,768]{1,0:T(8,128)(2,1)}, bf16[96,768]{1,0:T(8,128)(2,1)}, u32[]{:S(2)}, u32[]{:S(2)}) collective-permute-start(bf16[96,768]{1,0:T(8,128)(2,1)} %pack.3.refs_5_), channel_id=1, source_target_pairs={{0,2},{1,3},{2,0},{3,1},{4,6},{5,7},{6,4},{7,5},{8,10},{9,11},{10,... | collective-permute-start | bytes 442376 | tf_op jit(solution)/shard_map/ppermute | solution.py:34
  39.1 17.4 %collective-permute-start.5 = (bf16[288,768]{1,0:T(8,128)(2,1)S(1)}, bf16[288,768]{1,0:T(8,128)(2,1)S(1)}, u32[]{:S(2)}, u32[]{:S(2)}) collective-permute-start(bf16[288,768]{1,0:T(8,128)(2,1)S(1)} %copy-done.2), channel_id=1, source_target_pairs={{0,3},{1,0},{2,1},{3,2},{4,7},{5,4},{6,5},{7,6},{8,11},{9,8},{10,9... | collective-permute-start | bytes 1327112 | tf_op jit(solution)/shard_map/ppermute | solution.py:34
  42.2 16.5 %collective-permute-start.4 = (bf16[288,768]{1,0:T(8,128)(2,1)S(1)}, bf16[288,768]{1,0:T(8,128)(2,1)}, u32[]{:S(2)}, u32[]{:S(2)}) collective-permute-start(bf16[288,768]{1,0:T(8,128)(2,1)S(1)} %copy-done.2), channel_id=1, source_target_pairs={{0,2},{1,3},{2,0},{3,1},{4,6},{5,7},{6,4},{7,5},{8,10},{9,11},{10,... | collective-permute-start | bytes 1327112 | tf_op jit(solution)/shard_map/ppermute | solution.py:34
  42.2 23.2 %collective-permute-start.3 = (bf16[288,768]{1,0:T(8,128)(2,1)S(1)}, bf16[288,768]{1,0:T(8,128)(2,1)}, u32[]{:S(2)}, u32[]{:S(2)}) collective-permute-start(bf16[288,768]{1,0:T(8,128)(2,1)S(1)} %copy-done.2), channel_id=1, source_target_pairs={{0,1},{1,2},{2,3},{3,0},{4,5},{5,6},{6,7},{7,4},{8,9},{9,10},{10,1... | collective-permute-start | bytes 1327112 | tf_op jit(solution)/shard_map/ppermute | solution.py:34
  56.5 13.1 %copy-start.5 = (bf16[288,768]{1,0:T(8,128)(2,1)}, bf16[288,768]{1,0:T(8,128)(2,1)S(1)}, u32[]{:S(2)}) copy-start(bf16[288,768]{1,0:T(8,128)(2,1)S(1)} %collective-permute-done.5.refs_5_.refs_10_) | copy-start | bytes 1327108
  56.5 12.4 %collective-permute-start.8 = (bf16[288,768]{1,0:T(8,128)(2,1)S(1)}, bf16[288,768]{1,0:T(8,128)(2,1)S(1)}, u32[]{:S(2)}, u32[]{:S(2)}) collective-permute-start(bf16[288,768]{1,0:T(8,128)(2,1)S(1)} %collective-permute-done.5.refs_5_.refs_10_), channel_id=1, source_target_pairs={{0,4},{4,0},{1,5},{5,1},{2,6},{6,2},{3,7},{7,3},{8,12},{12,8},{9,1... | collective-permute-start | bytes 1327112 | tf_op jit(solution)/shard_map/ppermute | solution.py:42
  58.5 9.8 %collective-permute-start.9 = (bf16[96,768]{1,0:T(8,128)(2,1)}, bf16[96,768]{1,0:T(8,128)(2,1)S(1)}, u32[]{:S(2)}, u32[]{:S(2)}) collective-permute-start(bf16[96,768]{1,0:T(8,128)(2,1)} %pack.3.refs_5_), channel_id=1, source_target_pairs={{0,1},{1,2},{2,3},{3,0},{4,5},{5,6},{6,7},{7,4},{8,9},{9,10},{10,1... | collective-permute-start | bytes 442376 | tf_op jit(solution)/shard_map/ppermute | solution.py:34
  58.6 11.0 %collective-permute-start.7 = (bf16[288,768]{1,0:T(8,128)(2,1)}, bf16[288,768]{1,0:T(8,128)(2,1)S(1)}, u32[]{:S(2)}, u32[]{:S(2)}) collective-permute-start(bf16[288,768]{1,0:T(8,128)(2,1)} %collective-permute-done.4.refs_4_.refs_9_), channel_id=1, source_target_pairs={{0,4},{4,0},{1,5},{5,1},{2,6},{6,2},{3,7},{7,3},{8,12},{12,8},{9,1... | collective-permute-start | bytes 1327112 | tf_op jit(solution)/shard_map/ppermute | solution.py:42
  65.3 4.3 %collective-permute-start.6 = (bf16[288,768]{1,0:T(8,128)(2,1)}, bf16[288,768]{1,0:T(8,128)(2,1)S(1)}, u32[]{:S(2)}, u32[]{:S(2)}) collective-permute-start(bf16[288,768]{1,0:T(8,128)(2,1)} %collective-permute-done.3.refs_3_.refs_8_), channel_id=1, source_target_pairs={{0,4},{4,0},{1,5},{5,1},{2,6},{6,2},{3,7},{7,3},{8,12},{12,8},{9,1... | collective-permute-start | bytes 1327112 | tf_op jit(solution)/shard_map/ppermute | solution.py:42
  67.1 10.3 %collective-permute-start.14 = (bf16[96,768]{1,0:T(8,128)(2,1)}, bf16[96,768]{1,0:T(8,128)(2,1)S(1)}, u32[]{:S(2)}, u32[]{:S(2)}) collective-permute-start(bf16[96,768]{1,0:T(8,128)(2,1)} %collective-permute-done.11.refs_3_.refs_16_), channel_id=1, source_target_pairs={{0,4},{4,0},{1,5},{5,1},{2,6},{6,2},{3,7},{7,3},{8,12},{12,8},{9,1... | collective-permute-start | bytes 442376 | tf_op jit(solution)/shard_map/ppermute | solution.py:42
  68.4 9.1 %copy-start.18 = (bf16[96,768]{1,0:T(8,128)(2,1)}, bf16[96,768]{1,0:T(8,128)(2,1)S(1)}, u32[]{:S(2)}) copy-start(bf16[96,768]{1,0:T(8,128)(2,1)S(1)} %collective-permute-done.9.refs_1_.refs_14_) | copy-start | bytes 442372
  68.4 9.0 %collective-permute-start.13 = (bf16[96,768]{1,0:T(8,128)(2,1)}, bf16[96,768]{1,0:T(8,128)(2,1)S(1)}, u32[]{:S(2)}, u32[]{:S(2)}) collective-permute-start(bf16[96,768]{1,0:T(8,128)(2,1)} %collective-permute-done.10.refs_2_.refs_15_), channel_id=1, source_target_pairs={{0,4},{4,0},{1,5},{5,1},{2,6},{6,2},{3,7},{7,3},{8,12},{12,8},{9,1... | collective-permute-start | bytes 442376 | tf_op jit(solution)/shard_map/ppermute | solution.py:42
  68.9 8.6 %collective-permute-start.12 = (bf16[96,768]{1,0:T(8,128)(2,1)S(1)}, bf16[96,768]{1,0:T(8,128)(2,1)S(1)}, u32[]{:S(2)}, u32[]{:S(2)}) collective-permute-start(bf16[96,768]{1,0:T(8,128)(2,1)S(1)} %collective-permute-done.9.refs_1_.refs_14_), channel_id=1, source_target_pairs={{0,4},{4,0},{1,5},{5,1},{2,6},{6,2},{3,7},{7,3},{8,12},{12,8},{9,1... | collective-permute-start | bytes 442376 | tf_op jit(solution)/shard_map/ppermute | solution.py:42
  81.7 11.3 %collective-permute-start.17 = (bf16[128,768]{1,0:T(8,128)(2,1)}, bf16[128,768]{1,0:T(8,128)(2,1)S(1)}, u32[]{:S(2)}, u32[]{:S(2)}) collective-permute-start(bf16[128,768]{1,0:T(8,128)(2,1)} %get-tuple-element.60.refs_0_.refs_4_.moe_ref), channel_id=1, source_target_pairs={{0,3},{1,0},{2,1},{3,2},{4,7},{5,4},{6,5},{7,6},{8,11},{9,8},{10,9... | collective-permute-start | bytes 589832 | tf_op jit(solution)/shard_map/ppermute | solution.py:34
  84.5 8.5 %collective-permute-start.16 = (bf16[128,768]{1,0:T(8,128)(2,1)}, bf16[128,768]{1,0:T(8,128)(2,1)S(1)}, u32[]{:S(2)}, u32[]{:S(2)}) collective-permute-start(bf16[128,768]{1,0:T(8,128)(2,1)} %get-tuple-element.60.refs_0_.refs_4_.moe_ref), channel_id=1, source_target_pairs={{0,2},{1,3},{2,0},{3,1},{4,6},{5,7},{6,4},{7,5},{8,10},{9,11},{10,... | collective-permute-start | bytes 589832 | tf_op jit(solution)/shard_map/ppermute | solution.py:34
  84.5 12.2 %collective-permute-start.15 = (bf16[128,768]{1,0:T(8,128)(2,1)}, bf16[128,768]{1,0:T(8,128)(2,1)S(1)}, u32[]{:S(2)}, u32[]{:S(2)}) collective-permute-start(bf16[128,768]{1,0:T(8,128)(2,1)} %get-tuple-element.60.refs_0_.refs_4_.moe_ref), channel_id=1, source_target_pairs={{0,1},{1,2},{2,3},{3,0},{4,5},{5,6},{6,7},{7,4},{8,9},{9,10},{10,1... | collective-permute-start | bytes 589832 | tf_op jit(solution)/shard_map/ppermute | solution.py:34
  93.0 3.7 %copy-start.13 = (bf16[128,768]{1,0:T(8,128)(2,1)}, bf16[128,768]{1,0:T(8,128)(2,1)S(1)}, u32[]{:S(2)}) copy-start(bf16[128,768]{1,0:T(8,128)(2,1)S(1)} %collective-permute-done.16.refs_2_.refs_6_) | copy-start | bytes 589828
  152.9 4.1 %copy-start.25 = (f32[64,768]{1,0:T(8,128)S(1)}, f32[64,768]{1,0:T(8,128)}, u32[]{:S(2)}) copy-start(f32[64,768]{1,0:T(8,128)} %get-tuple-element.56) | copy-start | bytes 589828
  152.9 36.0 %all-to-all-start.2 = ((bf16[32,24,1536]{2,1,0:T(8,128)(2,1)}), bf16[32,24,1536]{2,1,0:T(8,128)(2,1)S(1)}, u32[]{:S(2)}, u32[]{:S(2)}) async-start(bf16[32,24,1536]{2,1,0:T(8,128)(2,1)} %bitcast.38), calls=%async_computation.2 | async-start | bytes 4718592 | tf_op jit(solution)/shard_map/all_to_all | solution.py:904
  177.4 18.9 %collective-permute-start.18 = (bf16[384,768]{1,0:T(8,128)(2,1)}, bf16[384,768]{1,0:T(8,128)(2,1)S(1)}, u32[]{:S(2)}, u32[]{:S(2)}) collective-permute-start(bf16[384,768]{1,0:T(8,128)(2,1)} %get-tuple-element.71), channel_id=1, source_target_pairs={{0,3},{1,0},{2,1},{3,2},{4,7},{5,4},{6,5},{7,6},{8,11},{9,8},{10,9... | collective-permute-start | bytes 1769480 | tf_op jit(solution)/shard_map/ppermute | solution.py:34
  178.1 18.2 %collective-permute-start.19 = (bf16[384,768]{1,0:T(8,128)(2,1)}, bf16[384,768]{1,0:T(8,128)(2,1)S(1)}, u32[]{:S(2)}, u32[]{:S(2)}) collective-permute-start(bf16[384,768]{1,0:T(8,128)(2,1)} %get-tuple-element.72), channel_id=1, source_target_pairs={{0,2},{1,3},{2,0},{3,1},{4,6},{5,7},{6,4},{7,5},{8,10},{9,11},{10,... | collective-permute-start | bytes 1769480 | tf_op jit(solution)/shard_map/ppermute | solution.py:34
  178.1 29.7 %collective-permute-start.20 = (bf16[384,768]{1,0:T(8,128)(2,1)}, bf16[384,768]{1,0:T(8,128)(2,1)}, u32[]{:S(2)}, u32[]{:S(2)}) collective-permute-start(bf16[384,768]{1,0:T(8,128)(2,1)} %get-tuple-element.73), channel_id=1, source_target_pairs={{0,1},{1,2},{2,3},{3,0},{4,5},{5,6},{6,7},{7,4},{8,9},{9,10},{10,1... | collective-permute-start | bytes 1769480 | tf_op jit(solution)/shard_map/ppermute | solution.py:34
  196.3 11.5 %copy-start.16 = (bf16[384,768]{1,0:T(8,128)(2,1)}, bf16[384,768]{1,0:T(8,128)(2,1)S(1)}, u32[]{:S(2)}) copy-start(bf16[384,768]{1,0:T(8,128)(2,1)S(1)} %collective-permute-done.18.refs_1_) | copy-start | bytes 1769476
  196.3 11.5 %copy-start.17 = (bf16[384,768]{1,0:T(8,128)(2,1)}, bf16[384,768]{1,0:T(8,128)(2,1)S(1)}, u32[]{:S(2)}) copy-start(bf16[384,768]{1,0:T(8,128)(2,1)S(1)} %collective-permute-done.19.refs_2_) | copy-start | bytes 1769476
  207.8 11.0 %copy-start.31 = (bf16[128,896]{1,0:T(8,128)(2,1)S(1)}, bf16[128,896]{1,0:T(8,128)(2,1)}, u32[]{:S(2)}) copy-start(bf16[128,896]{1,0:T(8,128)(2,1)} %get-tuple-element.82) | copy-start | bytes 688132
  207.8 12.1 %copy-start.30 = (bf16[128,896]{1,0:T(8,128)(2,1)S(1)}, bf16[128,896]{1,0:T(8,128)(2,1)}, u32[]{:S(2)}) copy-start(bf16[128,896]{1,0:T(8,128)(2,1)} %get-tuple-element.83) | copy-start | bytes 688132
  207.8 12.1 %copy-start.29 = (bf16[128,896]{1,0:T(8,128)(2,1)S(1)}, bf16[128,896]{1,0:T(8,128)(2,1)}, u32[]{:S(2)}) copy-start(bf16[128,896]{1,0:T(8,128)(2,1)} %get-tuple-element.84) | copy-start | bytes 688132
  211.2 22.6 %all-to-all-start.3 = ((bf16[32,16,768]{2,1,0:T(8,128)(2,1)}), bf16[32,16,768]{2,1,0:T(8,128)(2,1)S(1)}, u32[]{:S(2)}, u32[]{:S(2)}) async-start(bf16[32,16,768]{2,1,0:T(8,128)(2,1)} %bitcast.34), calls=%async_computation.3 | async-start | bytes 1572864 | tf_op jit(solution)/shard_map/all_to_all | solution.py:904
  218.8 7.0 %collective-permute-start.21 = (bf16[128,896]{1,0:T(8,128)(2,1)S(1)}, bf16[128,896]{1,0:T(8,128)(2,1)S(1)}, u32[]{:S(2)}, u32[]{:S(2)}) collective-permute-start(bf16[128,896]{1,0:T(8,128)(2,1)S(1)} %copy-done.31), channel_id=1, source_target_pairs={{0,3},{1,0},{2,1},{3,2},{4,7},{5,4},{6,5},{7,6},{8,11},{9,8},{10,9... | collective-permute-start | bytes 688136 | tf_op jit(solution)/shard_map/ppermute | solution.py:34
  219.9 8.2 %collective-permute-start.22 = (bf16[128,896]{1,0:T(8,128)(2,1)S(1)}, bf16[128,896]{1,0:T(8,128)(2,1)S(1)}, u32[]{:S(2)}, u32[]{:S(2)}) collective-permute-start(bf16[128,896]{1,0:T(8,128)(2,1)S(1)} %copy-done.30), channel_id=1, source_target_pairs={{0,2},{1,3},{2,0},{3,1},{4,6},{5,7},{6,4},{7,5},{8,10},{9,11},{10,... | collective-permute-start | bytes 688136 | tf_op jit(solution)/shard_map/ppermute | solution.py:34
  219.9 13.9 %collective-permute-start.23 = (bf16[128,896]{1,0:T(8,128)(2,1)S(1)}, bf16[128,896]{1,0:T(8,128)(2,1)S(1)}, u32[]{:S(2)}, u32[]{:S(2)}) collective-permute-start(bf16[128,896]{1,0:T(8,128)(2,1)S(1)} %copy-done.29), channel_id=1, source_target_pairs={{0,1},{1,2},{2,3},{3,0},{4,5},{5,6},{6,7},{7,4},{8,9},{9,10},{10,1... | collective-permute-start | bytes 688136 | tf_op jit(solution)/shard_map/ppermute | solution.py:34
  225.9 8.0 %copy-start.22 = (bf16[128,896]{1,0:T(8,128)(2,1)}, bf16[128,896]{1,0:T(8,128)(2,1)S(1)}, u32[]{:S(2)}) copy-start(bf16[128,896]{1,0:T(8,128)(2,1)S(1)} %collective-permute-done.21.refs_1_) | copy-start | bytes 688132
  228.1 5.8 %copy-start.23 = (bf16[128,896]{1,0:T(8,128)(2,1)}, bf16[128,896]{1,0:T(8,128)(2,1)S(1)}, u32[]{:S(2)}) copy-start(bf16[128,896]{1,0:T(8,128)(2,1)S(1)} %collective-permute-done.22.refs_2_) | copy-start | bytes 688132
  250.5 5.5 %collective-permute-start.24 = (bf16[1536,896]{1,0:T(8,128)(2,1)}, bf16[1536,896]{1,0:T(8,128)(2,1)S(1)}, u32[]{:S(2)}, u32[]{:S(2)}) collective-permute-start(bf16[1536,896]{1,0:T(8,128)(2,1)} %get-tuple-element.88), channel_id=1, source_target_pairs={{0,4},{4,0},{1,5},{5,1},{2,6},{6,2},{3,7},{7,3},{8,12},{12,8},{9,1... | collective-permute-start | bytes 8257544 | tf_op jit(solution)/shard_map/ppermute | solution.py:42
  315.6 5.2 %copy-start.4 = (bf16[16,24,896]{2,1,0:T(8,128)(2,1)}, bf16[16,24,896]{2,1,0:T(8,128)(2,1)S(1)}, u32[]{:S(2)}) copy-start(bf16[16,24,896]{2,1,0:T(8,128)(2,1)S(1)} %all_to_all.63) | copy-start | bytes 2064388
  315.6 5.2 %collective-permute-start.25 = (bf16[384,896]{1,0:T(8,128)(2,1)S(1)}, bf16[384,896]{1,0:T(8,128)(2,1)S(1)}, u32[]{:S(2)}, u32[]{:S(2)}) collective-permute-start(bf16[384,896]{1,0:T(8,128)(2,1)S(1)} %bitcast.35), channel_id=1, source_target_pairs={{0,4},{4,0},{1,5},{5,1},{2,6},{6,2},{3,7},{7,3},{8,12},{12,8},{9,1... | collective-permute-start | bytes 2064392 | tf_op jit(solution)/shard_map/ppermute | solution.py:42
  (14 other events, 15.1 us)

commit v3 on v2

--- a/solution.py
+++ b/solution.py
@@ -99,6 +99,15 @@
             other = pl.multiple_of(begin + (1 - core) * half, half)
             pairs.append((near[r - 1].at[part], out.at[pl.ds(mine, half)]))
             pairs.append((far[r - 1].at[part], out.at[pl.ds(other, half)]))
+    return pairs
+
+
+def whole_copies(shard, mat, near, out):
+    rows = mat.shape[0]
+    pairs = []
+    for r, piece in enumerate([mat, *near]):
+        begin = pl.multiple_of(lax.rem(shard + (4 - r), 4) * rows, rows)
+        pairs.append((piece, out.at[pl.ds(begin, rows)]))
     return pairs
 
 
@@ -181,11 +190,9 @@
 
 def middle_kernel(place_ref, tokens_ref, gain_ref, attended_ref, *refs):
     f32 = jnp.float32
-    mats, near, far = refs[:1], refs[1:4], refs[4:7]
-    middle_ref, moe_ref, weight, sems = refs[7:11]
-    copies = start_copies(
-        block_copies(place_ref[0], place_ref[1], mats, near, far, [weight]), sems
-    )
+    mat, near = refs[0], refs[1:4]
+    middle_ref, moe_ref, weight, sems = refs[4:8]
+    copies = start_copies(whole_copies(place_ref[0], mat, near, weight), sems)
     for c in copies:
         c.wait()
     middle = tokens_ref[...].astype(f32) + jnp.dot(
@@ -216,18 +223,15 @@
     *refs,
 ):
     f32, bf16 = jnp.float32, jnp.bfloat16
-    homes, mats, near_far = refs[:4], refs[4:8], refs[8:20]
-    result_ref, tokens_out, kept_ref, given_ref = refs[20:24]
-    held, grads_ref, small_ref, sides_ref, sems, out_sems = refs[24:30]
+    homes, mats, near, far, near_out = refs[:4], refs[4:8], refs[8:11], refs[11:14], refs[14:17]
+    result_ref, tokens_out, kept_ref, given_ref = refs[17:21]
+    held, grads_ref, small_ref, sems = refs[21:]
     weights = [held.at[n] for n in range(4)]
-    qkv = block_copies(
-        place_ref[0], place_ref[1], mats[:3], near_far[0:3], near_far[3:6], weights[:3]
-    )
-    out = block_copies(
-        place_ref[0], place_ref[1], mats[3:], near_far[6:9], near_far[9:12], weights[3:]
-    )
-    copies = start_copies(qkv + out, sems)
-    leaving = []
+    copies = start_copies(
+        block_copies(place_ref[0], place_ref[1], mats[:3], near, far, weights[:3])
+        + whole_copies(place_ref[0], mats[3], near_out, weights[3]),
+        sems,
+    )
     features = tokens_ref.shape[1]
     core = place_ref[1]
     width = features // 4
@@ -235,16 +239,13 @@
 
     def leave(mat, left, right):
         grad = lax.dot_general(left, right, FIRST, preferred_element_type=f32).astype(bf16)
-        grads_ref[mat] = grad
-        half = 96
-        pairs = []
+        grads_ref[...] = grad
         for x in range(4):
-            into = pl.ds((mat * 4 + x) * half, half)
-            for target, side in ((kept_ref, core), (given_ref, 1 - core)):
-                begin = pl.multiple_of(x * 2 * half + side * half, half)
-                source = grads_ref.at[mat, pl.ds(begin, half)]
-                pairs.append((source, target.at[into, pl.ds(0, features)]))
-        leaving.extend(start_copies(pairs, out_sems.at[mat]))
+            low = grads_ref[x * 192 : x * 192 + 96, :]
+            high = grads_ref[x * 192 + 96 : x * 192 + 192, :]
+            at = (mat * 4 + x) * 96
+            kept_ref[at : at + 96, :features] = jnp.where(core == 0, low, high)
+            given_ref[at : at + 96, :features] = jnp.where(core == 0, high, low)
 
     def leave_wide(mats_rows, block):
         for x in range(4):
@@ -352,16 +353,8 @@
     )
     small = small_ref[...].astype(bf16)
     none = jnp.zeros_like(small)
-    sides_ref[0] = jnp.where(core == 0, small, none)
-    sides_ref[1] = jnp.where(core == 0, none, small)
-    lanes = pl.ds(features, 128)
-    pairs = [
-        (sides_ref.at[0], kept_ref.at[:, lanes]),
-        (sides_ref.at[1], given_ref.at[:, lanes]),
-    ]
-    leaving.extend(start_copies(pairs, out_sems.at[4]))
-    for c in leaving:
-        c.wait()
+    kept_ref[:, features:] = jnp.where(core == 0, small, none)
+    given_ref[:, features:] = jnp.where(core == 0, none, small)
 
 
 ANYWHERE = pl.BlockSpec(memory_space=pl.ANY)
@@ -395,6 +388,20 @@
         compiler_params=ROOM,
         name="pack",
     )(core[None], *mats, after)
+
+
+def hold_back_kernel(mat_ref, _, out_ref):
+    out_ref[...] = mat_ref[...]
+
+
+def hold_back(mat, after):
+    return pl.pallas_call(
+        hold_back_kernel,
+        out_shape=jax.ShapeDtypeStruct(mat.shape, mat.dtype),
+        in_specs=[WHOLE, ANYWHERE],
+        out_specs=WHOLE,
+        name="hold_back",
+    )(mat, after)
 
 
 def attend(where, tokens, gain, bias, mats, near, far):
@@ -410,11 +417,14 @@
             pltpu.SemaphoreType.DMA((21,)),
         ],
         compiler_params=ROOM,
+        cost_estimate=pl.CostEstimate(
+            flops=80000000000, bytes_accessed=300000000, transcendentals=0
+        ),
         name="attend",
     )(where, tokens, gain, bias, *mats, *near, *far)
 
 
-def to_middle(where, tokens, gain, attended, mat, near, far):
+def to_middle(where, tokens, gain, attended, mat, near):
     rows, cols = mat.shape
     return pl.pallas_call(
         middle_kernel,
@@ -422,15 +432,15 @@
             jax.ShapeDtypeStruct(tokens.shape, jnp.float32),
             jax.ShapeDtypeStruct(tokens.shape, jnp.bfloat16),
         ],
-        in_specs=[SCALARS] + [WHOLE] * 3 + [ANYWHERE] * 7,
+        in_specs=[SCALARS] + [WHOLE] * 3 + [ANYWHERE] * 4,
         out_specs=[WHOLE] * 2,
         scratch_shapes=[
             pltpu.VMEM((4 * rows, cols), jnp.bfloat16),
-            pltpu.SemaphoreType.DMA((7,)),
+            pltpu.SemaphoreType.DMA((4,)),
         ],
         compiler_params=ROOM,
         name="middle",
-    )(where, tokens, gain, attended, mat, *near, *far)
+    )(where, tokens, gain, attended, mat, *near)
 
 
 def backward(where, *arrays):
@@ -446,15 +456,13 @@
             shape((2 * features, features + 128), bf16),
             shape((2 * features, features + 128), bf16),
         ],
-        in_specs=[SCALARS] + [WHOLE] * 20 + [ANYWHERE] * 16,
-        out_specs=[WHOLE] * 2 + [ANYWHERE] * 2,
+        in_specs=[SCALARS] + [WHOLE] * 20 + [ANYWHERE] * 13,
+        out_specs=[WHOLE] * 4,
         scratch_shapes=[
             pltpu.VMEM((4, features, features), bf16),
-            pltpu.VMEM((4, features, features), bf16),
+            pltpu.VMEM((features, features), bf16),
             pltpu.VMEM((2 * features, 128), f32),
-            pltpu.VMEM((2, 2 * features, 128), bf16),
-            pltpu.SemaphoreType.DMA((28,)),
-            pltpu.SemaphoreType.DMA((5, 8)),
+            pltpu.SemaphoreType.DMA((25,)),
         ],
         compiler_params=ROOM,
         name="backward",
@@ -505,8 +513,8 @@
 
 
 def dispatch_grads_kernel(capacity, place_ref, *refs):
-    pieces, (out_ref, places_ref, ids_ref, spots_ref) = refs[:4], refs[6:10]
-    gains_ref, bias_ref, router_ref, picks_ref = refs[10:]
+    pieces, (out_ref, places_ref, ids_ref, spots_ref) = refs[:4], refs[5:9]
+    gains_ref, bias_ref, router_ref = refs[9:]
     f32, bf16, i32 = jnp.float32, jnp.bfloat16, jnp.int32
     rows = out_ref.shape[0]
     tokens = spots_ref.shape[1]
@@ -541,7 +549,6 @@
     extra = jnp.zeros((rows, 128), f32)
     for e in range(2):
         pick = picks_of(places, e, rows)
-        picks_ref[e] = pick
         out_ref[:, e * features : (e + 1) * features] = jnp.dot(
             pick, line, preferred_element_type=f32
         ).astype(bf16)
@@ -576,34 +583,37 @@
             shape((2, features), jnp.float32),
             shape(bias_shape, jnp.float32),
             shape((experts_all, features), jnp.float32),
-            shape((2, rows, 4 * tokens), jnp.bfloat16),
         ],
-        in_specs=[SCALARS] + [WHOLE] * 4 + [ANYWHERE] * 2,
-        out_specs=[WHOLE] * 8,
-        compiler_params=ROOM,
+        in_specs=[SCALARS] + [WHOLE] * 4 + [ANYWHERE],
+        out_specs=[WHOLE] * 7,
+        compiler_params=ROOM,
+        cost_estimate=pl.CostEstimate(
+            flops=30000000000, bytes_accessed=100000000, transcendentals=0
+        ),
         name="dispatch_grads",
-    )(where, *pieces, *after)
-
-
-def dispatch_kernel(picks_ref, *refs):
+    )(where, *pieces, after)
+
+
+def dispatch_kernel(places_ref, *refs):
     pieces, out_ref = refs[:4], refs[5]
+    rows = out_ref.shape[0]
     features = pieces[0].shape[1]
     line = jnp.concatenate([p[...] for p in pieces], axis=0)
     for e in range(2):
         out_ref[:, e * features : (e + 1) * features] = jnp.dot(
-            picks_ref[e], line, preferred_element_type=jnp.float32
+            picks_of(places_ref[...], e, rows), line, preferred_element_type=jnp.float32
         ).astype(jnp.bfloat16)
 
 
-def dispatch(picks, pieces, after):
+def dispatch(places, pieces, rows, after):
     return pl.pallas_call(
         dispatch_kernel,
-        out_shape=jax.ShapeDtypeStruct((picks.shape[1], 2 * pieces[0].shape[1]), jnp.bfloat16),
+        out_shape=jax.ShapeDtypeStruct((rows, 2 * pieces[0].shape[1]), jnp.bfloat16),
         in_specs=[WHOLE] * 5 + [ANYWHERE],
         out_specs=WHOLE,
         compiler_params=ROOM,
         name="dispatch",
-    )(picks, *pieces, after)
+    )(places, *pieces, after)
 
 
 def chosen_logit(logits, ids):
@@ -664,51 +674,36 @@
     )(arrived, w_in, w_out)
 
 
-def early_kernel(g_ref, out_ref, back_ref):
-    back_ref[0] = lax.dot_general(
-        g_ref[...], out_ref[0], LAST, preferred_element_type=jnp.float32
-    )
-
-
-def early_product(grad_wide, w_out, after):
-    rows = grad_wide.shape[0]
-    hidden, features = w_out.shape[1:]
-    return pl.pallas_call(
-        lambda g, w, _, out: early_kernel(g, w, out),
-        grid=(2, rows // STEP),
-        out_shape=jax.ShapeDtypeStruct((2, rows, hidden), jnp.float32),
-        in_specs=[lanes_of(features), one_of(hidden, features), ANYWHERE],
-        out_specs=rows_of(hidden),
-        compiler_params=ROOM,
-        name="early_product",
-    )(grad_wide, w_out, after)
-
-
 def expert_back_kernel(
-    capacity, own_ref, x_ref, g_ref, ids_ref, in_ref, router_ref, rise_ref, back_ref, *refs
+    capacity, own_ref, x_ref, g_ref, ids_ref, in_ref, out_ref, router_ref, rise_ref, *refs
 ):
     pre_ref, arr_ref, outs, held = refs[0], refs[1], refs[2:6], refs[6]
     f32, bf16, i32 = jnp.float32, jnp.bfloat16, jnp.int32
     e = pl.program_id(0)
     own = own_ref[0] + e
     rows = x_ref.shape[0]
+    step = 256
 
     def chunk(i, carry):
-        at = pl.ds(pl.multiple_of(i * STEP, STEP), STEP)
+        at = pl.ds(pl.multiple_of(i * step, step), step)
         ids = ids_ref[at, :].astype(f32)
         lanes = lax.broadcasted_iota(i32, ids.shape, 1)
         other = jnp.sum(jnp.where(lanes == e, ids, 0.0), axis=1, keepdims=True).astype(i32) - own
-        logits = lax.dot_general(x_ref[at, :], router_ref[...], LAST, preferred_element_type=f32)
+        logits = lax.dot_general(
+            x_ref[at, :], router_ref[...], LAST, preferred_element_type=f32
+        )
         gate, _ = gate_pair(chosen_logit(logits, own), chosen_logit(logits, other))
-        arr_ref[0, at, :] = (gate * g_ref[at, :].astype(f32)).astype(bf16)
-        grad = (gate * back_ref[0, at, :] * rise_ref[0, at, :]).astype(bf16)
+        grown = (gate * g_ref[at, :].astype(f32)).astype(bf16)
+        arr_ref[0, at, :] = grown
+        back = lax.dot_general(grown, out_ref[0], LAST, preferred_element_type=f32)
+        grad = (back * rise_ref[0, at, :]).astype(bf16)
         pre_ref[0, at, :] = grad
         held[at, :] = lax.dot_general(grad, in_ref[0], LAST, preferred_element_type=f32).astype(
             bf16
         )
         return carry
 
-    lax.fori_loop(0, rows // STEP, chunk, 0)
+    lax.fori_loop(0, rows // step, chunk, 0)
     part = rows // 4
     here = lax.broadcasted_iota(i32, (part, rows), 0)
     there = lax.broadcasted_iota(i32, (part, rows), 1)
@@ -719,7 +714,7 @@
         out[...] = jnp.dot(pick, held[...], preferred_element_type=f32).astype(bf16)
 
 
-def experts_back(own, arrived, grad_wide, w_in, router_w, rise, back, capacity):
+def experts_back(own, arrived, grad_wide, w_in, w_out, router_w, rise, capacity):
     rows = arrived.shape[0]
     features, hidden = w_in.shape[1:]
     bf16 = jnp.bfloat16
@@ -738,8 +733,8 @@
             lanes(features),
             pl.BlockSpec((rows, 128), lambda e: (0, 2 * features // 128)),
             one(features, hidden),
+            one(hidden, features),
             pl.BlockSpec(router_w.shape, lambda e: (0, 0)),
-            one(rows, hidden),
             one(rows, hidden),
         ],
         out_specs=[one(rows, hidden), one(rows, features)]
@@ -747,7 +742,7 @@
         scratch_shapes=[pltpu.VMEM((rows, features), bf16)],
         compiler_params=ROOM,
         name="experts_back",
-    )(own[None], arrived, grad_wide, grad_wide, w_in, router_w, rise, back)
+    )(own[None], arrived, grad_wide, grad_wide, w_in, w_out, router_w, rise)
 
 
 def weight_grads_kernel(x_ref, pre_ref, act_ref, arr_ref, in_ref, out_ref):
@@ -809,6 +804,9 @@
         in_specs=[WHOLE] * 4 + [ANYWHERE] * len(after),
         out_specs=WHOLE,
         compiler_params=ROOM,
+        cost_estimate=pl.CostEstimate(
+            flops=20000000000, bytes_accessed=60000000, transcendentals=0
+        ),
         name="sum_rows",
     )(*pieces, *after)
 
@@ -896,14 +894,12 @@
         routes.T, jnp.stack([gain_attn, gain_moe]), rel_bias, w_router.T, cotangent
     )
     line_grads = along_x(line)
-    sent_qkv = pack(core, (w_query, w_key, w_value), line)
-    near_qkv = along_x(sent_qkv)[1:]
-    sent_out = pack(core, (w_output,), sent_qkv)
-    near_out = along_x(sent_out)[1:]
+    sent = pack(core, (w_query, w_key, w_value), line)
+    near = along_x(sent)[1:]
     def to_owners(outgoing):
         return lax.all_to_all(outgoing, ("y", "z", "c"), 0, 0, tiled=True)
 
-    outgoing_grads, places, ids, spots, gains, bias_table, router_f, picks = dispatch_grads(
+    outgoing_grads, places, ids, spots, gains, bias_table, router_f = dispatch_grads(
         where,
         line_grads,
         slot_rows,
@@ -911,11 +907,12 @@
         row_count,
         expert_count,
         (head_count, bucket_count),
-        (sent_qkv, sent_out),
+        line,
     )
     gain_one, gain_two = gains[0:1], gains[1:2]
     bias_table, router_w = bias_table.astype(bf16), router_f.astype(bf16)
     grad_wide = to_owners(outgoing_grads)
+    near_out = along_x(hold_back(w_output, outgoing_grads))[1:]
     first_expert = 2 * lax.axis_index(("y", "z", "c")).astype(jnp.int32)
 
     segments = row_segments(seq_lengths[0], row_count)
@@ -923,29 +920,26 @@
     allowed = (segments[:, None] == segments[None, :]) & (distance >= 0)
     position_bias = jnp.einsum("ijb,hb->hij", onehot, bias_table, preferred_element_type=f32)
     masked_bias = jnp.where(allowed[None], position_bias, -1000000000.0)
-    far_qkv = [swap_core(part) for part in near_qkv]
-    far_out = [swap_core(part) for part in near_out]
+    far = [swap_core(piece) for piece in near]
     hidden_one, queries, key_rows, value_rows, probs, attended = attend(
         where,
         tokens,
         gain_one,
         masked_bias,
         (w_query, w_key, w_value),
-        near_qkv,
-        far_qkv,
+        near,
+        far,
     )
     middle, moe_in = to_middle(
-        where, tokens, gain_two, attended, w_output, near_out, far_out
+        where, tokens, gain_two, attended, w_output, near_out
     )
 
     line_moe = along_x(moe_in)
-    outgoing = dispatch(picks, line_moe, grad_wide)
-    arrived = to_owners(outgoing)
-    early = early_product(grad_wide, w_out, outgoing)
+    arrived = to_owners(dispatch(places, line_moe, slot_rows, grad_wide))
     ret, active, rise = experts(arrived, w_in, w_out)
     returned = to_owners(ret)
     grad_pre, grad_arrived, *blocks = experts_back(
-        first_expert, arrived, grad_wide, w_in, router_w, rise, early, capacity
+        first_expert, arrived, grad_wide, w_in, w_out, router_w, rise, capacity
     )
     summed = [blocks[0]] + [shift_x(blocks[r], -r) for r in range(1, 4)]
     grad_w_in, grad_w_out = weight_grads(arrived, grad_pre, active, grad_arrived)
@@ -975,10 +969,9 @@
         w_key,
         w_value,
         w_output,
-        *near_qkv,
-        *far_qkv,
+        *near,
+        *far,
         *near_out,
-        *far_out,
     )
     piece = shard_rows // 8
     wide = features + 128

time: 327 us -> 298 us (0.911)
  waiting for transfers between devices: 73.5 us -> 52.6 us
  Pallas kernels: 94.6 us -> 87.2 us
    ppermute x18, waiting for transfers between devices: 66.8 us -> 39 us  [shift(): lax.ppermute(block, axis, [(i, (i + step) % ranks) for i in range(ranks)])]
    all_to_all x3, waiting for transfers between devices: 0.01 us -> 6.89 us  [to_owners(): return lax.all_to_all(outgoing, ('y', 'z', 'c'), 0, 0, tiled=True)]
    pallas_call x2, Pallas kernels: 11.9 us -> 5.71 us  [the longest x1 4.02 us: dispatch(): pl.pallas_call(dispatch_kernel, out_shape=jax.ShapeDtypeStruct((rows, 2 *...]
    ppermute x8 -> x5, starting transfers between devices: 6.87 us -> 5.29 us  [swap_core(): return lax.ppermute(block, 'c', [(0, 1), (1, 0)])]
    unnamed x66 -> x58, local copies, waits for them, and re-layouts: 7.18 us -> 7.07 us
    ppermute x8 -> x5, waiting for transfers between devices: 6.72 us -> 6.71 us  [swap_core(): return lax.ppermute(block, 'c', [(0, 1), (1, 0)])]
  transfers between devices with their start and end apart: 29 -> 26, of which waited for: 14 -> 13; matrix products, arithmetic and copies ran while one was open for 1% -> 2% of each run, Pallas kernels for 15% -> 16%
where the time goes in v3:
time: 298 us; the launch traced here: 297 us
  blocking collectives  94.9 us (32%)
  Pallas kernels  87.2 us (29%)
  waiting for transfers between devices  52.6 us (18%)
  starting transfers between devices  42.9 us (14%)
  local copies, waits for them, and re-layouts  10.4 us (3%)
  other arithmetic  7.85 us (3%)
    all_to_all x1, blocking collectives, layer(): spread = lax.all_to_all(paired, ('y', 'x', 'z'), 0, 0, tiled=True)  43.5 us
    ppermute x18, waiting for transfers between devices, shift(): lax.ppermute(block, axis, [(i, (i + step) % ranks) for i in range(ranks)])  39 us
    all_to_all x1, blocking collectives, to_owners(): return lax.all_to_all(outgoing, ('y', 'z', 'c'), 0, 0, tiled=True)  38.3 us
    all_to_all x3, starting transfers between devices, to_owners(): return lax.all_to_all(outgoing, ('y', 'z', 'c'), 0, 0, tiled=True)  21.8 us
    ppermute x18, starting transfers between devices, shift(): lax.ppermute(block, axis, [(i, (i + step) % ranks) for i in range(ranks)])  15.8 us
    pallas_call x1, Pallas kernels, backward(): pl.pallas_call(backward_kernel, out_shape=[shape((count, features), bf16)...  15.8 us
    pallas_call x1, Pallas kernels, experts_back(): pl.pallas_call(functools.partial(expert_back_kernel, capacity), grid=(2,)...  13.3 us
    all_to_all x1, blocking collectives, layer(): lax.all_to_all(jnp.broadcast_to(mine[None], (16, piece, wide)).reshape(16...  13.1 us
  transfers between devices with their start and end apart: 26, of which 13 were waited for; matrix products, arithmetic and copies ran while one was open for 2% of the time, Pallas kernels for 16%

profile of v3, /device:TPU:1, one launch (start us, length us, event | category | flops | bytes accessed | tf_op | source)
XLA Modules:
  0.0 297.3 jit_solution(8228682174976757534)
XLA Ops:
  2.5 2.5 line.1.refs_0_.refs_4_.refs_3_
  5.0 3.4 %collective-permute-start.2 = (bf16[160,768]{1,0:T(8,128)(2,1)}, bf16[160,768]{1,0:T(8,128)(2,1)S(1)}, u32[]{:S(2)}, u32[]{:S(2)}) collective-permute-start(bf16[160,768]{1,0:T(8,128)(2,1)} %line.1.refs_0_.refs_4_.refs_3_), channel_id=1, source_target_pairs={{0,3},{1,0},{2,1},{3,2},{4,7},{5,4},{6,5},{7,6},{8,11},{9,8},{10,9... | collective-permute-start | bytes 737288 | tf_op jit(solution)/shard_map/ppermute | solution.py:34
  9.5 1.8 pack.1
  11.3 2.1 collective-permute-start.5
  13.5 1.2 collective-permute-start.4
  14.7 0.8 reduce-window.8
  15.7 0.9 convert_reduce_fusion
  17.4 7.2 %collective-permute-done.refs_1_ = bf16[160,768]{1,0:T(8,128)(2,1)S(1)} collective-permute-done((bf16[160,768]{1,0:T(8,128)(2,1)}, bf16[160,768]{1,0:T(8,128)(2,1)S(1)}, u32[]{:S(2)}, u32[]{:S(2)}) %collective-permute-start) | collective-permute-done | bytes 245792 | tf_op jit(solution)/shard_map/ppermute | solution.py:34
  25.3 4.8 %dispatch_grads.1 = (bf16[768,1664]{1,0:T(8,128)(2,1)}, s32[2,512]{1,0:T(2,128)}, s32[2,512]{1,0:T(2,128)}, s32[2,128]{1,0:T(2,128)}, f32[2,768]{1,0:T(2,128)}, /*index=5*/f32[12,32]{1,0:T(8,128)}, f32[64,768]{1,0:T(8,128)}) custom-call(s32[2]{0:T(128)} %pad_add_fusion.place_ref, bf16[160,768]{1,0:T(8,128)(2,1)} %line.1.refs_0_.refs_4_.refs_3_, ...), custom_call_target="tpu_custom_call" | custom-call | flops 30000001024 | bytes 100000000 | tf_op jit(solution)/shard_map/dispatch_grads/pallas_call | solution.py:576
  30.1 1.7 hold_back.1
  32.4 10.1 %all-to-all-start = ((bf16[32,24,1664]{2,1,0:T(8,128)(2,1)}), bf16[32,24,1664]{2,1,0:T(8,128)(2,1)S(1)}, u32[]{:S(2)}, u32[]{:S(2)}) async-start(bf16[32,24,1664]{2,1,0:T(8,128)(2,1)} %bitcast.30), calls=%async_computation | async-start | bytes 5111808 | tf_op jit(solution)/shard_map/all_to_all | solution.py:900
  44.8 1.2 copy_select_fusion.bias_ref
  47.7 6.8 %attend.1 = (bf16[128,768]{1,0:T(8,128)(2,1)}, bf16[128,768]{1,0:T(8,128)(2,1)}, bf16[128,768]{1,0:T(8,128)(2,1)}, bf16[128,768]{1,0:T(8,128)(2,1)}, f32[12,128,128]{2,1,0:T(8,128)}, /*index=5*/bf16[128,768]{1,0:T(8,128)(2,1)}) custom-call(s32[2]{0:T(128)} %pad_add_fusion.place_ref, bf16[128,768]{1,0:T(8,128)(2,1)} %tokens_ref.5, ...), custom_call_target="tpu_custom_call" | custom-call | flops 80000000000 | bytes 300000000 | tf_op jit(solution)/shard_map/attend/pallas_call | solution.py:410
  54.6 1.3 collective-permute-done.9.refs_1_.refs_14_
  56.6 3.5 %middle.1 = (f32[128,768]{1,0:T(8,128)}, bf16[128,768]{1,0:T(8,128)(2,1)}) custom-call(s32[2]{0:T(128)} %pad_add_fusion.place_ref, bf16[128,768]{1,0:T(8,128)(2,1)} %tokens_ref.5, f32[1,768]{1,0:T(1,128)} %get-tuple-element.94.gain_ref.gain_two_ref, bf16[128,768]{1,0:T(8,128)(2,1)} %get-tuple-element.57.attended_ref, bf16[192,768]{1,0:T(8,128)(2,1)} %refs_7_.1, ...), custom_call_target="tpu_custom_call" | custom-call | tf_op jit(solution)/shard_map/middle/pallas_call | solution.py:429
  60.1 1.0 collective-permute-start.14
  62.6 3.4 %collective-permute-done.14.refs_3_.refs_7_ = bf16[128,768]{1,0:T(8,128)(2,1)S(1)} collective-permute-done((bf16[128,768]{1,0:T(8,128)(2,1)}, bf16[128,768]{1,0:T(8,128)(2,1)S(1)}, u32[]{:S(2)}, u32[]{:S(2)}) %collective-permute-start.14) | collective-permute-done | bytes 196640 | tf_op jit(solution)/shard_map/ppermute | solution.py:34
  66.0 2.0 collective-permute-done.13.refs_2_.refs_6_
  68.0 5.8 %collective-permute-done.12.refs_1_.refs_5_ = bf16[128,768]{1,0:T(8,128)(2,1)S(1)} collective-permute-done((bf16[128,768]{1,0:T(8,128)(2,1)}, bf16[128,768]{1,0:T(8,128)(2,1)S(1)}, u32[]{:S(2)}, u32[]{:S(2)}) %collective-permute-start.12) | collective-permute-done | bytes 196640 | tf_op jit(solution)/shard_map/ppermute | solution.py:34
  73.8 1.8 all-to-all-done
  75.7 1.5 copy-done
  77.1 4.0 %dispatch.1 = bf16[768,1536]{1,0:T(8,128)(2,1)} custom-call(s32[2,512]{1,0:T(2,128)} %get-tuple-element.67.places_ref, bf16[128,768]{1,0:T(8,128)(2,1)} %get-tuple-element.60.refs_0_.refs_4_.moe_ref, bf16[128,768]{1,0:T(8,128)(2,1)} %copy-done.9, bf16[128,768]{1,0:T(8,128)(2,1)} %copy-done.8, bf16[128,768]{1,0:T(8,128)(2,1)} %copy-done.7, ...), custom_call_target="tpu_custom_call" | custom-call | tf_op jit(solution)/shard_map/dispatch/pallas_call | solution.py:609
  81.1 38.3 %all_to_all.61 = bf16[32,24,1536]{2,1,0:T(8,128)(2,1)} all-to-all(bf16[32,24,1536]{2,1,0:T(8,128)(2,1)} %bitcast.32), channel_id=1, replica_groups=mesh['y'=4,'z'=4,'c'=2,'x'=4] {'y','z','c'}, dimensions={0} | all-to-all | bytes 4718592 | tf_op jit(solution)/shard_map/all_to_all | solution.py:900
  119.4 11.0 %experts.1 = (bf16[768,1536]{1,0:T(8,128)(2,1)}, bf16[2,768,768]{2,1,0:T(8,128)(2,1)}, f32[2,768,768]{2,1,0:T(8,128)}) custom-call(bf16[768,1536]{1,0:T(8,128)(2,1)} %bitcast.26, bf16[2,768,768]{2,1,0:T(8,128)(2,1)} %in_ref.3, bf16[2,768,768]{2,1,0:T(8,128)(2,1)} %out_ref.3), custom_call_target="tpu_custom_call" | custom-call | tf_op jit(solution)/shard_map/experts/pallas_call | solution.py:662
  130.4 4.0 %all-to-all-start.2 = ((bf16[32,24,1536]{2,1,0:T(8,128)(2,1)}), bf16[32,24,1536]{2,1,0:T(8,128)(2,1)S(1)}, u32[]{:S(2)}, u32[]{:S(2)}) async-start(bf16[32,24,1536]{2,1,0:T(8,128)(2,1)} %bitcast.36), calls=%async_computation.2 | async-start | bytes 4718592 | tf_op jit(solution)/shard_map/all_to_all | solution.py:900
  135.1 13.3 %experts_back.1 = (bf16[2,768,768]{2,1,0:T(8,128)(2,1)}, bf16[2,768,768]{2,1,0:T(8,128)(2,1)}, bf16[384,768]{1,0:T(8,128)(2,1)}, bf16[384,768]{1,0:T(8,128)(2,1)...) custom-call(s32[1]{0:T(128)} %bitcast.7.own_ref, bf16[768,1536]{1,0:T(8,128)(2,1)} %bitcast.27, ...), custom_call_target="tpu_custom_call" | custom-call | tf_op jit(solution)/shard_map/experts_back/pallas_call | solution.py:725
  148.4 1.4 collective-permute-start.15
  150.5 10.0 %weight_grads.1 = (f32[2,768,768]{2,1,0:T(8,128)}, f32[2,768,768]{2,1,0:T(8,128)}) custom-call(bf16[768,1536]{1,0:T(8,128)(2,1)} %bitcast.28, bf16[2,768,768]{2,1,0:T(8,128)(2,1)} %get-tuple-element.73.pre_ref, bf16[2,768,768]{2,1,0:T(8,128)(2,1)} %get-tuple-element.74.act_ref, bf16[2,768,768]{2,1,0:T(8,128)(2,1)} %get-tuple-element.75.arr_ref), custom_call_target="tpu_custom_call" | custom-call | flops 3623878656 | bytes 20000000 | tf_op jit(solution)/shard_map/weight_grads/pallas_call | solution.py:760
  160.6 5.0 %all-to-all-done.2 = bf16[32,24,1536]{2,1,0:T(8,128)(2,1)S(1)} async-done(((bf16[32,24,1536]{2,1,0:T(8,128)(2,1)}), bf16[32,24,1536]{2,1,0:T(8,128)(2,1)S(1)}, u32[]{:S(2)}, u32[]{:S(2)}) %all-to-all-start.2) | async-done | bytes 2359328 | tf_op jit(solution)/shard_map/all_to_all | solution.py:900
  165.6 1.4 copy-done.1
  167.0 5.9 %combine.1 = (bf16[128,896]{1,0:T(8,128)(2,1)}, bf16[128,896]{1,0:T(8,128)(2,1)}, bf16[128,896]{1,0:T(8,128)(2,1)}, bf16[128,896]{1,0:T(8,128)(2,1)}) custom-call(s32[2,512]{1,0:T(2,128)} %get-tuple-element.67.places_ref, s32[2,512]{1,0:T(2,128)} %get-tuple-element.54.ids_ref, bf16[64,768]{1,0:T(8,128)(2,1)} %convert_element_type.24.router_ref, ...), custom_call_target="tpu_custom_call" | custom-call | tf_op jit(solution)/shard_map/combine/pallas_call | solution.py:852
  172.9 6.5 %collective-permute-done.17.refs_3_ = bf16[384,768]{1,0:T(8,128)(2,1)} collective-permute-done((bf16[384,768]{1,0:T(8,128)(2,1)}, bf16[384,768]{1,0:T(8,128)(2,1)}, u32[]{:S(2)}, u32[]{:S(2)}) %collective-permute-start.17) | collective-permute-done | bytes 589856 | tf_op jit(solution)/shard_map/ppermute | solution.py:34
  179.5 3.4 %sum_rows.1 = bf16[512,768]{1,0:T(8,128)(2,1)} custom-call(bf16[384,768]{1,0:T(8,128)(2,1)} %get-tuple-element.69.refs_0_, bf16[384,768]{1,0:T(8,128)(2,1)} %copy-done.24, bf16[384,768]{1,0:T(8,128)(2,1)} %copy-done.25, bf16[384,768]{1,0:T(8,128)(2,1)} %collective-permute-done.17.refs_3_, f32[2,768,768]{2,1,0:T(8,128)} %get-tuple-element.52.refs_4_, ...), custom_call_target="tpu_custom_call" | custom-call | flops 20000000000 | bytes 60000000 | tf_op jit(solution)/shard_map/sum_rows/pallas_call | solution.py:801
  182.8 7.7 %all-to-all-start.3 = ((bf16[32,16,768]{2,1,0:T(8,128)(2,1)}), bf16[32,16,768]{2,1,0:T(8,128)(2,1)S(1)}, u32[]{:S(2)}, u32[]{:S(2)}) async-start(bf16[32,16,768]{2,1,0:T(8,128)(2,1)} %bitcast.37), calls=%async_computation.3 | async-start | bytes 1572864 | tf_op jit(solution)/shard_map/all_to_all | solution.py:900
  191.3 1.1 collective-permute-start.20
  192.4 5.2 %collective-permute-done.18.refs_1_ = bf16[128,896]{1,0:T(8,128)(2,1)S(1)} collective-permute-done((bf16[128,896]{1,0:T(8,128)(2,1)S(1)}, bf16[128,896]{1,0:T(8,128)(2,1)S(1)}, u32[]{:S(2)}, u32[]{:S(2)}) %collective-permute-start.18) | collective-permute-done | bytes 229408 | tf_op jit(solution)/shard_map/ppermute | solution.py:34
  197.6 1.9 collective-permute-done.19.refs_2_
  199.5 5.7 %collective-permute-done.20.refs_3_ = bf16[128,896]{1,0:T(8,128)(2,1)S(1)} collective-permute-done((bf16[128,896]{1,0:T(8,128)(2,1)S(1)}, bf16[128,896]{1,0:T(8,128)(2,1)S(1)}, u32[]{:S(2)}, u32[]{:S(2)}) %collective-permute-start.20) | collective-permute-done | bytes 229408 | tf_op jit(solution)/shard_map/ppermute | solution.py:34
  206.2 15.8 %backward.1 = (bf16[128,768]{1,0:T(8,128)(2,1)}, f32[128,768]{1,0:T(8,128)}, bf16[1536,896]{1,0:T(8,128)(2,1)}, bf16[1536,896]{1,0:T(8,128)(2,1)}) custom-call(s32[2]{0:T(128)} %pad_add_fusion.place_ref, bf16[128,768]{1,0:T(8,128)(2,1)} %tokens_ref.5, bf16[128,768]{1,0:T(8,128)(2,1)} %cotangent_ref.3, f32[1,768]{1,0:T(1,128)} %get-tuple-element.95.gain_ref.gain_one_ref, ...), custom_call_target="tpu_custom_call" | custom-call | tf_op jit(solution)/shard_map/backward/pallas_call | solution.py:451
  222.5 4.9 %collective-permute-done.21 = bf16[1536,896]{1,0:T(8,128)(2,1)S(1)} collective-permute-done((bf16[1536,896]{1,0:T(8,128)(2,1)}, bf16[1536,896]{1,0:T(8,128)(2,1)S(1)}, u32[]{:S(2)}, u32[]{:S(2)}) %collective-permute-start.21) | collective-permute-done | bytes 2752544 | tf_op jit(solution)/shard_map/ppermute | solution.py:42
  227.5 2.5 add_convert_fusion
  230.0 43.5 %all_to_all.62 = bf16[64,24,896]{2,1,0:T(8,128)(2,1)S(1)} all-to-all(bf16[64,24,896]{2,1,0:T(8,128)(2,1)S(1)} %bitcast.29), channel_id=1, replica_groups=mesh['y'=4,'z'=4,'c'=2,'x'=4] {'y','x','z'}, dimensions={0} | all-to-all | bytes 5505024 | tf_op jit(solution)/shard_map/all_to_all | solution.py:979
  273.9 13.1 %all_to_all.63 = bf16[16,24,896]{2,1,0:T(8,128)(2,1)S(1)} all-to-all(bf16[16,24,896]{2,1,0:T(8,128)(2,1)S(1)} %broadcast_in_dim.15), channel_id=1, replica_groups=mesh['y'=4,'z'=4,'c'=2,'x'=4] {'y','z'}, dimensions={0} | all-to-all | bytes 1376256 | tf_op jit(solution)/shard_map/all_to_all | solution.py:981
  287.1 3.5 %collective-permute-start.22 = (bf16[384,896]{1,0:T(8,128)(2,1)S(1)}, bf16[384,896]{1,0:T(8,128)(2,1)S(1)}, u32[]{:S(2)}, u32[]{:S(2)}) collective-permute-start(bf16[384,896]{1,0:T(8,128)(2,1)S(1)} %bitcast.34), channel_id=1, source_target_pairs={{0,4},{4,0},{1,5},{5,1},{2,6},{6,2},{3,7},{7,3},{8,12},{12,8},{9,1... | collective-permute-start | bytes 2064392 | tf_op jit(solution)/shard_map/ppermute | solution.py:42
  290.5 1.8 collective-permute-done.22.other_ref
  292.3 0.8 copy-done.10
  293.2 2.8 finish.1
  295.9 1.3 fusion.5
  (96 shorter events, 15.6 us)
Async XLA Ops:
  5.0 12.3 %collective-permute-start.2 = (bf16[160,768]{1,0:T(8,128)(2,1)}, bf16[160,768]{1,0:T(8,128)(2,1)S(1)}, u32[]{:S(2)}, u32[]{:S(2)}) collective-permute-start(bf16[160,768]{1,0:T(8,128)(2,1)} %line.1.refs_0_.refs_4_.refs_3_), channel_id=1, source_target_pairs={{0,3},{1,0},{2,1},{3,2},{4,7},{5,4},{6,5},{7,6},{8,11},{9,8},{10,9... | collective-permute-start | bytes 737288 | tf_op jit(solution)/shard_map/ppermute | solution.py:34
  8.4 9.0 %collective-permute-start.1 = (bf16[160,768]{1,0:T(8,128)(2,1)}, bf16[160,768]{1,0:T(8,128)(2,1)S(1)}, u32[]{:S(2)}, u32[]{:S(2)}) collective-permute-start(bf16[160,768]{1,0:T(8,128)(2,1)} %line.1.refs_0_.refs_4_.refs_3_), channel_id=1, source_target_pairs={{0,2},{1,3},{2,0},{3,1},{4,6},{5,7},{6,4},{7,5},{8,10},{9,11},{10,... | collective-permute-start | bytes 737288 | tf_op jit(solution)/shard_map/ppermute | solution.py:34
  8.9 15.7 %collective-permute-start = (bf16[160,768]{1,0:T(8,128)(2,1)}, bf16[160,768]{1,0:T(8,128)(2,1)S(1)}, u32[]{:S(2)}, u32[]{:S(2)}) collective-permute-start(bf16[160,768]{1,0:T(8,128)(2,1)} %line.1.refs_0_.refs_4_.refs_3_), channel_id=1, source_target_pairs={{0,1},{1,2},{2,3},{3,0},{4,5},{5,6},{6,7},{7,4},{8,9},{9,10},{10,1... | collective-permute-start | bytes 737288 | tf_op jit(solution)/shard_map/ppermute | solution.py:34
  11.3 31.6 %collective-permute-start.5 = (bf16[288,768]{1,0:T(8,128)(2,1)}, bf16[288,768]{1,0:T(8,128)(2,1)}, u32[]{:S(2)}, u32[]{:S(2)}) collective-permute-start(bf16[288,768]{1,0:T(8,128)(2,1)} %pack.1), channel_id=1, source_target_pairs={{0,3},{1,0},{2,1},{3,2},{4,7},{5,4},{6,5},{7,6},{8,11},{9,8},{10,9... | collective-permute-start | bytes 1327112 | tf_op jit(solution)/shard_map/ppermute | solution.py:34
  13.5 29.7 %collective-permute-start.4 = (bf16[288,768]{1,0:T(8,128)(2,1)}, bf16[288,768]{1,0:T(8,128)(2,1)}, u32[]{:S(2)}, u32[]{:S(2)}) collective-permute-start(bf16[288,768]{1,0:T(8,128)(2,1)} %pack.1), channel_id=1, source_target_pairs={{0,2},{1,3},{2,0},{3,1},{4,6},{5,7},{6,4},{7,5},{8,10},{9,11},{10,... | collective-permute-start | bytes 1327112 | tf_op jit(solution)/shard_map/ppermute | solution.py:34
  17.3 7.3 %copy-start.15 = (bf16[160,768]{1,0:T(8,128)(2,1)}, bf16[160,768]{1,0:T(8,128)(2,1)S(1)}, u32[]{:S(2)}) copy-start(bf16[160,768]{1,0:T(8,128)(2,1)S(1)} %collective-permute-done.2.refs_3_) | copy-start | bytes 737284
  17.3 26.2 %collective-permute-start.3 = (bf16[288,768]{1,0:T(8,128)(2,1)}, bf16[288,768]{1,0:T(8,128)(2,1)}, u32[]{:S(2)}, u32[]{:S(2)}) collective-permute-start(bf16[288,768]{1,0:T(8,128)(2,1)} %pack.1), channel_id=1, source_target_pairs={{0,1},{1,2},{2,3},{3,0},{4,5},{5,6},{6,7},{7,4},{8,9},{9,10},{10,1... | collective-permute-start | bytes 1327112 | tf_op jit(solution)/shard_map/ppermute | solution.py:34
  17.4 7.2 %copy-start.16 = (bf16[160,768]{1,0:T(8,128)(2,1)}, bf16[160,768]{1,0:T(8,128)(2,1)S(1)}, u32[]{:S(2)}) copy-start(bf16[160,768]{1,0:T(8,128)(2,1)S(1)} %collective-permute-done.1.refs_2_) | copy-start | bytes 737284
  31.7 22.8 %collective-permute-start.11 = (bf16[192,768]{1,0:T(8,128)(2,1)}, bf16[192,768]{1,0:T(8,128)(2,1)S(1)}, u32[]{:S(2)}, u32[]{:S(2)}) collective-permute-start(bf16[192,768]{1,0:T(8,128)(2,1)} %hold_back.1), channel_id=1, source_target_pairs={{0,3},{1,0},{2,1},{3,2},{4,7},{5,4},{6,5},{7,6},{8,11},{9,8},{10,9... | collective-permute-start | bytes 884744 | tf_op jit(solution)/shard_map/ppermute | solution.py:34
  31.8 22.8 %collective-permute-start.10 = (bf16[192,768]{1,0:T(8,128)(2,1)}, bf16[192,768]{1,0:T(8,128)(2,1)S(1)}, u32[]{:S(2)}, u32[]{:S(2)}) collective-permute-start(bf16[192,768]{1,0:T(8,128)(2,1)} %hold_back.1), channel_id=1, source_target_pairs={{0,2},{1,3},{2,0},{3,1},{4,6},{5,7},{6,4},{7,5},{8,10},{9,11},{10,... | collective-permute-start | bytes 884744 | tf_op jit(solution)/shard_map/ppermute | solution.py:34
  32.4 10.1 %copy-start.22 = (f32[12,32]{1,0:T(8,128)S(1)}, f32[12,32]{1,0:T(8,128)}, u32[]{:S(2)}) copy-start(f32[12,32]{1,0:T(8,128)} %get-tuple-element.56) | copy-start | bytes 4612
  32.4 11.8 %copy-start.23 = (f32[2,768]{1,0:T(2,128)S(1)}, f32[2,768]{1,0:T(2,128)}, u32[]{:S(2)}) copy-start(f32[2,768]{1,0:T(2,128)} %get-tuple-element.53) | copy-start | bytes 18436
  32.4 43.3 %all-to-all-start = ((bf16[32,24,1664]{2,1,0:T(8,128)(2,1)}), bf16[32,24,1664]{2,1,0:T(8,128)(2,1)S(1)}, u32[]{:S(2)}, u32[]{:S(2)}) async-start(bf16[32,24,1664]{2,1,0:T(8,128)(2,1)} %bitcast.30), calls=%async_computation | async-start | bytes 5111808 | tf_op jit(solution)/shard_map/all_to_all | solution.py:900
  42.5 3.5 %copy-start.14 = (bf16[192,768]{1,0:T(8,128)(2,1)S(1)}, bf16[192,768]{1,0:T(8,128)(2,1)}, u32[]{:S(2)}) copy-start(bf16[192,768]{1,0:T(8,128)(2,1)} %hold_back.1) | copy-start | bytes 884740
  42.9 3.0 %collective-permute-start.8 = (bf16[288,768]{1,0:T(8,128)(2,1)}, bf16[288,768]{1,0:T(8,128)(2,1)S(1)}, u32[]{:S(2)}, u32[]{:S(2)}) collective-permute-start(bf16[288,768]{1,0:T(8,128)(2,1)} %collective-permute-done.5.refs_5_.refs_10_), channel_id=1, source_target_pairs={{0,4},{4,0},{1,5},{5,1},{2,6},{6,2},{3,7},{7,3},{8,12},{12,8},{9,1... | collective-permute-start | bytes 1327112 | tf_op jit(solution)/shard_map/ppermute | solution.py:42
  43.2 3.5 %collective-permute-start.7 = (bf16[288,768]{1,0:T(8,128)(2,1)}, bf16[288,768]{1,0:T(8,128)(2,1)S(1)}, u32[]{:S(2)}, u32[]{:S(2)}) collective-permute-start(bf16[288,768]{1,0:T(8,128)(2,1)} %collective-permute-done.4.refs_4_.refs_9_), channel_id=1, source_target_pairs={{0,4},{4,0},{1,5},{5,1},{2,6},{6,2},{3,7},{7,3},{8,12},{12,8},{9,1... | collective-permute-start | bytes 1327112 | tf_op jit(solution)/shard_map/ppermute | solution.py:42
  43.5 3.2 %collective-permute-start.6 = (bf16[288,768]{1,0:T(8,128)(2,1)}, bf16[288,768]{1,0:T(8,128)(2,1)S(1)}, u32[]{:S(2)}, u32[]{:S(2)}) collective-permute-start(bf16[288,768]{1,0:T(8,128)(2,1)} %collective-permute-done.3.refs_3_.refs_8_), channel_id=1, source_target_pairs={{0,4},{4,0},{1,5},{5,1},{2,6},{6,2},{3,7},{7,3},{8,12},{12,8},{9,1... | collective-permute-start | bytes 1327112 | tf_op jit(solution)/shard_map/ppermute | solution.py:42
  46.0 9.9 %collective-permute-start.9 = (bf16[192,768]{1,0:T(8,128)(2,1)S(1)}, bf16[192,768]{1,0:T(8,128)(2,1)S(1)}, u32[]{:S(2)}, u32[]{:S(2)}) collective-permute-start(bf16[192,768]{1,0:T(8,128)(2,1)S(1)} %copy-done.14), channel_id=1, source_target_pairs={{0,1},{1,2},{2,3},{3,0},{4,5},{5,6},{6,7},{7,4},{8,9},{9,10},{10,1... | collective-permute-start | bytes 884744 | tf_op jit(solution)/shard_map/ppermute | solution.py:34
  54.5 1.3 copy-start.4
  54.6 1.3 copy-start.5
  60.1 5.9 %collective-permute-start.14 = (bf16[128,768]{1,0:T(8,128)(2,1)}, bf16[128,768]{1,0:T(8,128)(2,1)S(1)}, u32[]{:S(2)}, u32[]{:S(2)}) collective-permute-start(bf16[128,768]{1,0:T(8,128)(2,1)} %get-tuple-element.60.refs_0_.refs_4_.moe_ref), channel_id=1, source_target_pairs={{0,3},{1,0},{2,1},{3,2},{4,7},{5,4},{6,5},{7,6},{8,11},{9,8},{10,9... | collective-permute-start | bytes 589832 | tf_op jit(solution)/shard_map/ppermute | solution.py:34
  61.1 6.9 %collective-permute-start.13 = (bf16[128,768]{1,0:T(8,128)(2,1)}, bf16[128,768]{1,0:T(8,128)(2,1)S(1)}, u32[]{:S(2)}, u32[]{:S(2)}) collective-permute-start(bf16[128,768]{1,0:T(8,128)(2,1)} %get-tuple-element.60.refs_0_.refs_4_.moe_ref), channel_id=1, source_target_pairs={{0,2},{1,3},{2,0},{3,1},{4,6},{5,7},{6,4},{7,5},{8,10},{9,11},{10,... | collective-permute-start | bytes 589832 | tf_op jit(solution)/shard_map/ppermute | solution.py:34
  61.8 12.0 %collective-permute-start.12 = (bf16[128,768]{1,0:T(8,128)(2,1)}, bf16[128,768]{1,0:T(8,128)(2,1)S(1)}, u32[]{:S(2)}, u32[]{:S(2)}) collective-permute-start(bf16[128,768]{1,0:T(8,128)(2,1)} %get-tuple-element.60.refs_0_.refs_4_.moe_ref), channel_id=1, source_target_pairs={{0,1},{1,2},{2,3},{3,0},{4,5},{5,6},{6,7},{7,4},{8,9},{9,10},{10,1... | collective-permute-start | bytes 589832 | tf_op jit(solution)/shard_map/ppermute | solution.py:34
  66.0 9.7 %copy-start.7 = (bf16[128,768]{1,0:T(8,128)(2,1)}, bf16[128,768]{1,0:T(8,128)(2,1)S(1)}, u32[]{:S(2)}) copy-start(bf16[128,768]{1,0:T(8,128)(2,1)S(1)} %collective-permute-done.14.refs_3_.refs_7_) | copy-start | bytes 589828
  68.0 7.7 %copy-start.8 = (bf16[128,768]{1,0:T(8,128)(2,1)}, bf16[128,768]{1,0:T(8,128)(2,1)S(1)}, u32[]{:S(2)}) copy-start(bf16[128,768]{1,0:T(8,128)(2,1)S(1)} %collective-permute-done.13.refs_2_.refs_6_) | copy-start | bytes 589828
  73.8 1.9 copy-start.9
  75.7 1.5 copy-start
  130.4 4.1 %copy-start.21 = (f32[64,768]{1,0:T(8,128)S(1)}, f32[64,768]{1,0:T(8,128)}, u32[]{:S(2)}) copy-start(f32[64,768]{1,0:T(8,128)} %get-tuple-element.55) | copy-start | bytes 589828
  130.4 35.2 %all-to-all-start.2 = ((bf16[32,24,1536]{2,1,0:T(8,128)(2,1)}), bf16[32,24,1536]{2,1,0:T(8,128)(2,1)S(1)}, u32[]{:S(2)}, u32[]{:S(2)}) async-start(bf16[32,24,1536]{2,1,0:T(8,128)(2,1)} %bitcast.36), calls=%async_computation.2 | async-start | bytes 4718592 | tf_op jit(solution)/shard_map/all_to_all | solution.py:900
  148.4 24.5 %collective-permute-start.15 = (bf16[384,768]{1,0:T(8,128)(2,1)}, bf16[384,768]{1,0:T(8,128)(2,1)S(1)}, u32[]{:S(2)}, u32[]{:S(2)}) collective-permute-start(bf16[384,768]{1,0:T(8,128)(2,1)} %get-tuple-element.70), channel_id=1, source_target_pairs={{0,3},{1,0},{2,1},{3,2},{4,7},{5,4},{6,5},{7,6},{8,11},{9,8},{10,9... | collective-permute-start | bytes 1769480 | tf_op jit(solution)/shard_map/ppermute | solution.py:34
  149.9 23.0 %collective-permute-start.16 = (bf16[384,768]{1,0:T(8,128)(2,1)}, bf16[384,768]{1,0:T(8,128)(2,1)S(1)}, u32[]{:S(2)}, u32[]{:S(2)}) collective-permute-start(bf16[384,768]{1,0:T(8,128)(2,1)} %get-tuple-element.71), channel_id=1, source_target_pairs={{0,2},{1,3},{2,0},{3,1},{4,6},{5,7},{6,4},{7,5},{8,10},{9,11},{10,... | collective-permute-start | bytes 1769480 | tf_op jit(solution)/shard_map/ppermute | solution.py:34
  150.1 29.3 %collective-permute-start.17 = (bf16[384,768]{1,0:T(8,128)(2,1)}, bf16[384,768]{1,0:T(8,128)(2,1)}, u32[]{:S(2)}, u32[]{:S(2)}) collective-permute-start(bf16[384,768]{1,0:T(8,128)(2,1)} %get-tuple-element.72), channel_id=1, source_target_pairs={{0,1},{1,2},{2,3},{3,0},{4,5},{5,6},{6,7},{7,4},{8,9},{9,10},{10,1... | collective-permute-start | bytes 1769480 | tf_op jit(solution)/shard_map/ppermute | solution.py:34
  165.6 1.4 copy-start.1
  172.9 6.5 %copy-start.24 = (bf16[384,768]{1,0:T(8,128)(2,1)}, bf16[384,768]{1,0:T(8,128)(2,1)S(1)}, u32[]{:S(2)}) copy-start(bf16[384,768]{1,0:T(8,128)(2,1)S(1)} %collective-permute-done.15.refs_1_) | copy-start | bytes 1769476
  172.9 6.5 %copy-start.25 = (bf16[384,768]{1,0:T(8,128)(2,1)}, bf16[384,768]{1,0:T(8,128)(2,1)S(1)}, u32[]{:S(2)}) copy-start(bf16[384,768]{1,0:T(8,128)(2,1)S(1)} %collective-permute-done.16.refs_2_) | copy-start | bytes 1769476
  179.4 11.1 %copy-start.28 = (bf16[128,896]{1,0:T(8,128)(2,1)S(1)}, bf16[128,896]{1,0:T(8,128)(2,1)}, u32[]{:S(2)}) copy-start(bf16[128,896]{1,0:T(8,128)(2,1)} %get-tuple-element.80) | copy-start | bytes 688132
  179.4 11.8 %copy-start.27 = (bf16[128,896]{1,0:T(8,128)(2,1)S(1)}, bf16[128,896]{1,0:T(8,128)(2,1)}, u32[]{:S(2)}) copy-start(bf16[128,896]{1,0:T(8,128)(2,1)} %get-tuple-element.81) | copy-start | bytes 688132
  179.4 11.8 %copy-start.26 = (bf16[128,896]{1,0:T(8,128)(2,1)S(1)}, bf16[128,896]{1,0:T(8,128)(2,1)}, u32[]{:S(2)}) copy-start(bf16[128,896]{1,0:T(8,128)(2,1)} %get-tuple-element.82) | copy-start | bytes 688132
  182.8 22.4 %all-to-all-start.3 = ((bf16[32,16,768]{2,1,0:T(8,128)(2,1)}), bf16[32,16,768]{2,1,0:T(8,128)(2,1)S(1)}, u32[]{:S(2)}, u32[]{:S(2)}) async-start(bf16[32,16,768]{2,1,0:T(8,128)(2,1)} %bitcast.37), calls=%async_computation.3 | async-start | bytes 1572864 | tf_op jit(solution)/shard_map/all_to_all | solution.py:900
  190.5 7.0 %collective-permute-start.18 = (bf16[128,896]{1,0:T(8,128)(2,1)S(1)}, bf16[128,896]{1,0:T(8,128)(2,1)S(1)}, u32[]{:S(2)}, u32[]{:S(2)}) collective-permute-start(bf16[128,896]{1,0:T(8,128)(2,1)S(1)} %copy-done.28), channel_id=1, source_target_pairs={{0,3},{1,0},{2,1},{3,2},{4,7},{5,4},{6,5},{7,6},{8,11},{9,8},{10,9... | collective-permute-start | bytes 688136 | tf_op jit(solution)/shard_map/ppermute | solution.py:34
  191.3 8.2 %collective-permute-start.19 = (bf16[128,896]{1,0:T(8,128)(2,1)S(1)}, bf16[128,896]{1,0:T(8,128)(2,1)S(1)}, u32[]{:S(2)}, u32[]{:S(2)}) collective-permute-start(bf16[128,896]{1,0:T(8,128)(2,1)S(1)} %copy-done.27), channel_id=1, source_target_pairs={{0,2},{1,3},{2,0},{3,1},{4,6},{5,7},{6,4},{7,5},{8,10},{9,11},{10,... | collective-permute-start | bytes 688136 | tf_op jit(solution)/shard_map/ppermute | solution.py:34
  191.3 13.9 %collective-permute-start.20 = (bf16[128,896]{1,0:T(8,128)(2,1)S(1)}, bf16[128,896]{1,0:T(8,128)(2,1)S(1)}, u32[]{:S(2)}, u32[]{:S(2)}) collective-permute-start(bf16[128,896]{1,0:T(8,128)(2,1)S(1)} %copy-done.26), channel_id=1, source_target_pairs={{0,1},{1,2},{2,3},{3,0},{4,5},{5,6},{6,7},{7,4},{8,9},{9,10},{10,1... | collective-permute-start | bytes 688136 | tf_op jit(solution)/shard_map/ppermute | solution.py:34
  197.6 7.7 %copy-start.18 = (bf16[128,896]{1,0:T(8,128)(2,1)}, bf16[128,896]{1,0:T(8,128)(2,1)S(1)}, u32[]{:S(2)}) copy-start(bf16[128,896]{1,0:T(8,128)(2,1)S(1)} %collective-permute-done.18.refs_1_) | copy-start | bytes 688132
  199.5 5.8 %copy-start.19 = (bf16[128,896]{1,0:T(8,128)(2,1)}, bf16[128,896]{1,0:T(8,128)(2,1)S(1)}, u32[]{:S(2)}) copy-start(bf16[128,896]{1,0:T(8,128)(2,1)S(1)} %collective-permute-done.19.refs_2_) | copy-start | bytes 688132
  205.2 1.0 copy-start.2
  222.0 5.5 %collective-permute-start.21 = (bf16[1536,896]{1,0:T(8,128)(2,1)}, bf16[1536,896]{1,0:T(8,128)(2,1)S(1)}, u32[]{:S(2)}, u32[]{:S(2)}) collective-permute-start(bf16[1536,896]{1,0:T(8,128)(2,1)} %get-tuple-element.86), channel_id=1, source_target_pairs={{0,4},{4,0},{1,5},{5,1},{2,6},{6,2},{3,7},{7,3},{8,12},{12,8},{9,1... | collective-permute-start | bytes 8257544 | tf_op jit(solution)/shard_map/ppermute | solution.py:42
  287.1 5.2 %copy-start.3 = (bf16[16,24,896]{2,1,0:T(8,128)(2,1)}, bf16[16,24,896]{2,1,0:T(8,128)(2,1)S(1)}, u32[]{:S(2)}) copy-start(bf16[16,24,896]{2,1,0:T(8,128)(2,1)S(1)} %all_to_all.63) | copy-start | bytes 2064388
  287.1 5.2 %collective-permute-start.22 = (bf16[384,896]{1,0:T(8,128)(2,1)S(1)}, bf16[384,896]{1,0:T(8,128)(2,1)S(1)}, u32[]{:S(2)}, u32[]{:S(2)}) collective-permute-start(bf16[384,896]{1,0:T(8,128)(2,1)S(1)} %bitcast.34), channel_id=1, source_target_pairs={{0,4},{4,0},{1,5},{5,1},{2,6},{6,2},{3,7},{7,3},{8,12},{12,8},{9,1... | collective-permute-start | bytes 2064392 | tf_op jit(solution)/shard_map/ppermute | solution.py:42
  (7 other events, 5.5 us)

commit v4 on v3

--- a/solution.py
+++ b/solution.py
@@ -675,11 +675,10 @@
 
 
 def expert_back_kernel(
-    capacity, own_ref, x_ref, g_ref, ids_ref, in_ref, out_ref, router_ref, rise_ref, *refs
+    capacity, e, own_ref, x_ref, g_ref, ids_ref, in_ref, out_ref, router_ref, rise_ref, *refs
 ):
     pre_ref, arr_ref, outs, held = refs[0], refs[1], refs[2:6], refs[6]
     f32, bf16, i32 = jnp.float32, jnp.bfloat16, jnp.int32
-    e = pl.program_id(0)
     own = own_ref[0] + e
     rows = x_ref.shape[0]
     step = 256
@@ -694,10 +693,10 @@
         )
         gate, _ = gate_pair(chosen_logit(logits, own), chosen_logit(logits, other))
         grown = (gate * g_ref[at, :].astype(f32)).astype(bf16)
-        arr_ref[0, at, :] = grown
+        arr_ref[at, :] = grown
         back = lax.dot_general(grown, out_ref[0], LAST, preferred_element_type=f32)
         grad = (back * rise_ref[0, at, :]).astype(bf16)
-        pre_ref[0, at, :] = grad
+        pre_ref[at, :] = grad
         held[at, :] = lax.dot_general(grad, in_ref[0], LAST, preferred_element_type=f32).astype(
             bf16
         )
@@ -714,48 +713,59 @@
         out[...] = jnp.dot(pick, held[...], preferred_element_type=f32).astype(bf16)
 
 
-def experts_back(own, arrived, grad_wide, w_in, w_out, router_w, rise, capacity):
+def experts_back(own, e, arrived, grad_wide, w_in, w_out, router_w, rise, capacity, flops):
     rows = arrived.shape[0]
     features, hidden = w_in.shape[1:]
     bf16 = jnp.bfloat16
     shape = jax.ShapeDtypeStruct
     part = rows // 4
-    lanes = lambda n: pl.BlockSpec((rows, n), lambda e: (0, e))
-    one = lambda a, b: pl.BlockSpec((1, a, b), lambda e: (e, 0, 0))
-    return pl.pallas_call(
-        functools.partial(expert_back_kernel, capacity),
-        grid=(2,),
-        out_shape=[shape((2, rows, hidden), bf16), shape((2, rows, features), bf16)]
-        + [shape((2 * part, features), bf16)] * 4,
+    lanes = lambda n: pl.BlockSpec((rows, n), lambda i: (0, e))
+    one = lambda a, b: pl.BlockSpec((1, a, b), lambda i: (e, 0, 0))
+    whole = lambda a, b: pl.BlockSpec((a, b), lambda i: (0, 0))
+    return pl.pallas_call(
+        functools.partial(expert_back_kernel, capacity, e),
+        grid=(1,),
+        out_shape=[shape((rows, hidden), bf16), shape((rows, features), bf16)]
+        + [shape((part, features), bf16)] * 4,
         in_specs=[
             SCALARS,
             lanes(features),
             lanes(features),
-            pl.BlockSpec((rows, 128), lambda e: (0, 2 * features // 128)),
+            pl.BlockSpec((rows, 128), lambda i: (0, 2 * features // 128)),
             one(features, hidden),
             one(hidden, features),
-            pl.BlockSpec(router_w.shape, lambda e: (0, 0)),
+            whole(*router_w.shape),
             one(rows, hidden),
         ],
-        out_specs=[one(rows, hidden), one(rows, features)]
-        + [pl.BlockSpec((part, features), lambda e: (e, 0))] * 4,
+        out_specs=[whole(rows, hidden), whole(rows, features)] + [whole(part, features)] * 4,
         scratch_shapes=[pltpu.VMEM((rows, features), bf16)],
         compiler_params=ROOM,
+        cost_estimate=pl.CostEstimate(
+            flops=flops, bytes_accessed=10_000_000, transcendentals=0
+        ),
         name="experts_back",
     )(own[None], arrived, grad_wide, grad_wide, w_in, w_out, router_w, rise)
 
 
-def weight_grads_kernel(x_ref, pre_ref, act_ref, arr_ref, in_ref, out_ref):
-    in_ref[0] = lax.dot_general(x_ref[...], pre_ref[0], FIRST, preferred_element_type=jnp.float32)
-    out_ref[0] = lax.dot_general(act_ref[0], arr_ref[0], FIRST, preferred_element_type=jnp.float32)
-
-
-def weight_grads(arrived, grad_pre, active, grad_arrived):
+def weight_grads_kernel(x_ref, act_ref, pre_a, pre_b, arr_a, arr_b, in_ref, out_ref):
+    def make(pre_ref, arr_ref):
+        in_ref[0] = lax.dot_general(
+            x_ref[...], pre_ref[...], FIRST, preferred_element_type=jnp.float32
+        )
+        out_ref[0] = lax.dot_general(
+            act_ref[0], arr_ref[...], FIRST, preferred_element_type=jnp.float32
+        )
+
+    pl.when(pl.program_id(0) == 0)(lambda: make(pre_a, arr_a))
+    pl.when(pl.program_id(0) == 1)(lambda: make(pre_b, arr_b))
+
+
+def weight_grads(arrived, active, grad_pre, grad_arrived):
     rows = arrived.shape[0]
-    hidden, features = grad_pre.shape[2], grad_arrived.shape[2]
+    hidden, features = grad_pre[0].shape[1], grad_arrived[0].shape[1]
     step = 256
     cuts = features // step
-    whole = lambda n: pl.BlockSpec((1, rows, n), lambda e, j: (e, 0, 0))
+    whole = lambda n: pl.BlockSpec((rows, n), lambda e, j: (0, 0))
     out = lambda n: pl.BlockSpec((1, step, n), lambda e, j: (e, j, 0))
     return pl.pallas_call(
         weight_grads_kernel,
@@ -766,25 +776,29 @@
         ],
         in_specs=[
             pl.BlockSpec((rows, step), lambda e, j: (0, e * cuts + j)),
-            whole(hidden),
             pl.BlockSpec((1, rows, step), lambda e, j: (e, 0, j)),
-            whole(features),
-        ],
+        ]
+        + [whole(hidden)] * 2
+        + [whole(features)] * 2,
         out_specs=[out(hidden), out(features)],
         compiler_params=ROOM,
         cost_estimate=pl.CostEstimate(
             flops=8 * rows * features * hidden, bytes_accessed=20_000_000, transcendentals=0
         ),
         name="weight_grads",
-    )(arrived, grad_pre, active, grad_arrived)
+    )(arrived, active, *grad_pre, *grad_arrived)
 
 
 def sum_rows_kernel(capacity, *refs):
-    pieces, out_ref = refs[:4], refs[-1]
+    out_ref = refs[-1]
     f32, bf16, i32 = jnp.float32, jnp.bfloat16, jnp.int32
-    total = pieces[0][...].astype(f32)
-    for piece in pieces[1:]:
-        total = total + piece[...].astype(f32)
+    totals = []
+    for pieces in (refs[:4], refs[4:8]):
+        total = pieces[0][...].astype(f32)
+        for piece in pieces[1:]:
+            total = total + piece[...].astype(f32)
+        totals.append(total)
+    total = jnp.concatenate(totals, axis=0)
     rows = out_ref.shape[0]
     part = total.shape[0] // 2
     here = lax.broadcasted_iota(i32, (rows, 2 * part), 0)
@@ -797,11 +811,11 @@
 
 
 def sum_rows(pieces, capacity, after):
-    rows, features = pieces[0].shape
+    rows, features = 2 * pieces[0].shape[0], pieces[0].shape[1]
     return pl.pallas_call(
         functools.partial(sum_rows_kernel, capacity),
         out_shape=jax.ShapeDtypeStruct((rows // (2 * capacity) * 16, features), jnp.bfloat16),
-        in_specs=[WHOLE] * 4 + [ANYWHERE] * len(after),
+        in_specs=[WHOLE] * 8 + [ANYWHERE] * len(after),
         out_specs=WHOLE,
         compiler_params=ROOM,
         cost_estimate=pl.CostEstimate(
@@ -938,11 +952,15 @@
     arrived = to_owners(dispatch(places, line_moe, slot_rows, grad_wide))
     ret, active, rise = experts(arrived, w_in, w_out)
     returned = to_owners(ret)
-    grad_pre, grad_arrived, *blocks = experts_back(
-        first_expert, arrived, grad_wide, w_in, w_out, router_w, rise, capacity
-    )
-    summed = [blocks[0]] + [shift_x(blocks[r], -r) for r in range(1, 4)]
-    grad_w_in, grad_w_out = weight_grads(arrived, grad_pre, active, grad_arrived)
+    grad_pre, grad_arrived, summed = [], [], []
+    for e, flops in enumerate((3_000_000_000, 60_000_000_000)):
+        pre, grown, *blocks = experts_back(
+            first_expert, e, arrived, grad_wide, w_in, w_out, router_w, rise, capacity, flops
+        )
+        grad_pre.append(pre)
+        grad_arrived.append(grown)
+        summed += [blocks[0]] + [shift_x(blocks[r], -r) for r in range(1, 4)]
+    grad_w_in, grad_w_out = weight_grads(arrived, active, grad_pre, grad_arrived)
     bundle = combine(places, ids, router_w, returned, line_grads, line_moe, grad_w_in)
     back_rows = to_owners(sum_rows(summed, capacity, (grad_w_out, bundle[0])))
     homes = [bundle[0]] + [shift_x(bundle[r], -r) for r in range(1, 4)]

time: 298 us -> 300 us (level)
  blocking collectives: 94.9 us -> 56.6 us
  waiting for transfers between devices: 52.6 us -> 72.1 us
  starting transfers between devices: 42.9 us -> 56.5 us
  Pallas kernels: 87.2 us -> 91.5 us
    all_to_all x1 -> x0, blocking collectives: 38.3 us -> none  [to_owners(): return lax.all_to_all(outgoing, ('y', 'z', 'c'), 0, 0, tiled=True)]
    all_to_all x3 -> x4, waiting for transfers between devices: 6.89 us -> 32.4 us  [to_owners(): return lax.all_to_all(outgoing, ('y', 'z', 'c'), 0, 0, tiled=True)]
    all_to_all x3 -> x4, starting transfers between devices: 21.8 us -> 30.6 us  [to_owners(): return lax.all_to_all(outgoing, ('y', 'z', 'c'), 0, 0, tiled=True)]
    ppermute x18 -> x21, waiting for transfers between devices: 39 us -> 33 us  [shift(): lax.ppermute(block, axis, [(i, (i + step) % ranks) for i in range(ranks)])]
    ppermute x18 -> x21, starting transfers between devices: 15.8 us -> 20.6 us  [shift(): lax.ppermute(block, axis, [(i, (i + step) % ranks) for i in range(ranks)])]
    pallas_call x1 -> x2, Pallas kernels: 13.3 us -> 17.2 us  [experts_back(): pl.pallas_call(functools.partial(expert_back_kernel, capacity, e), grid=(...]
    unnamed x58 -> x64, local copies, waits for them, and re-layouts: 7.07 us -> 9.39 us
  transfers between devices with their start and end apart: 26 -> 30, of which waited for: 13 -> 12; matrix products, arithmetic and copies ran while one was open for 2% -> 2% of each run, Pallas kernels for 16% -> 17%
where the time goes in v4:
time: 300 us; the launch traced here: 299 us
  Pallas kernels  91.5 us (30%)
  waiting for transfers between devices  72.1 us (24%)
  blocking collectives  56.6 us (19%)
  starting transfers between devices  56.5 us (19%)
  local copies, waits for them, and re-layouts  12.7 us (4%)
  other arithmetic  7.84 us (3%)
    all_to_all x1, blocking collectives, layer(): spread = lax.all_to_all(paired, ('y', 'x', 'z'), 0, 0, tiled=True)  43.5 us
    ppermute x21, waiting for transfers between devices, shift(): lax.ppermute(block, axis, [(i, (i + step) % ranks) for i in range(ranks)])  33 us
    all_to_all x4, waiting for transfers between devices, to_owners(): return lax.all_to_all(outgoing, ('y', 'z', 'c'), 0, 0, tiled=True)  32.4 us
    all_to_all x4, starting transfers between devices, to_owners(): return lax.all_to_all(outgoing, ('y', 'z', 'c'), 0, 0, tiled=True)  30.6 us
    ppermute x21, starting transfers between devices, shift(): lax.ppermute(block, axis, [(i, (i + step) % ranks) for i in range(ranks)])  20.6 us
    pallas_call x2, Pallas kernels, experts_back(): pl.pallas_call(functools.partial(expert_back_kernel, capacity, e), grid=(...  17.2 us
    pallas_call x1, Pallas kernels, backward(): pl.pallas_call(backward_kernel, out_shape=[shape((count, features), bf16)...  15.8 us
    all_to_all x1, blocking collectives, layer(): lax.all_to_all(jnp.broadcast_to(mine[None], (16, piece, wide)).reshape(16...  13.1 us
  transfers between devices with their start and end apart: 30, of which 12 were waited for; matrix products, arithmetic and copies ran while one was open for 2% of the time, Pallas kernels for 17%

profile of v4, /device:TPU:1, one launch (start us, length us, event | category | flops | bytes accessed | tf_op | source)
XLA Modules:
  0.0 298.7 jit_solution(7841749984362229133)
XLA Ops:
  2.5 2.4 line.1.refs_0_.refs_4_.refs_3_
  5.0 3.4 %collective-permute-start.2 = (bf16[160,768]{1,0:T(8,128)(2,1)}, bf16[160,768]{1,0:T(8,128)(2,1)S(1)}, u32[]{:S(2)}, u32[]{:S(2)}) collective-permute-start(bf16[160,768]{1,0:T(8,128)(2,1)} %line.1.refs_0_.refs_4_.refs_3_), channel_id=1, source_target_pairs={{0,3},{1,0},{2,1},{3,2},{4,7},{5,4},{6,5},{7,6},{8,11},{9,8},{10,9... | collective-permute-start | bytes 737288 | tf_op jit(solution)/shard_map/ppermute | solution.py:34
  9.5 1.8 pack.1
  11.3 2.1 collective-permute-start.5
  13.5 1.2 collective-permute-start.4
  15.6 0.9 convert_reduce_fusion
  17.4 7.2 %collective-permute-done.refs_1_ = bf16[160,768]{1,0:T(8,128)(2,1)S(1)} collective-permute-done((bf16[160,768]{1,0:T(8,128)(2,1)}, bf16[160,768]{1,0:T(8,128)(2,1)S(1)}, u32[]{:S(2)}, u32[]{:S(2)}) %collective-permute-start) | collective-permute-done | bytes 245792 | tf_op jit(solution)/shard_map/ppermute | solution.py:34
  25.2 4.8 %dispatch_grads.1 = (bf16[768,1664]{1,0:T(8,128)(2,1)}, s32[2,512]{1,0:T(2,128)}, s32[2,512]{1,0:T(2,128)}, s32[2,128]{1,0:T(2,128)}, f32[2,768]{1,0:T(2,128)}, /*index=5*/f32[12,32]{1,0:T(8,128)}, f32[64,768]{1,0:T(8,128)}) custom-call(s32[2]{0:T(128)} %pad_add_fusion.place_ref, bf16[160,768]{1,0:T(8,128)(2,1)} %line.1.refs_0_.refs_4_.refs_3_, ...), custom_call_target="tpu_custom_call" | custom-call | flops 30000001024 | bytes 100000000 | tf_op jit(solution)/shard_map/dispatch_grads/pallas_call | solution.py:576
  30.0 1.7 hold_back.1
  32.4 10.1 %all-to-all-start = ((bf16[32,24,1664]{2,1,0:T(8,128)(2,1)}), bf16[32,24,1664]{2,1,0:T(8,128)(2,1)S(1)}, u32[]{:S(2)}, u32[]{:S(2)}) async-start(bf16[32,24,1664]{2,1,0:T(8,128)(2,1)} %bitcast.33), calls=%async_computation | async-start | bytes 5111808 | tf_op jit(solution)/shard_map/all_to_all | solution.py:914
  44.8 1.2 copy_select_fusion.bias_ref
  47.6 6.8 %attend.1 = (bf16[128,768]{1,0:T(8,128)(2,1)}, bf16[128,768]{1,0:T(8,128)(2,1)}, bf16[128,768]{1,0:T(8,128)(2,1)}, bf16[128,768]{1,0:T(8,128)(2,1)}, f32[12,128,128]{2,1,0:T(8,128)}, /*index=5*/bf16[128,768]{1,0:T(8,128)(2,1)}) custom-call(s32[2]{0:T(128)} %pad_add_fusion.place_ref, bf16[128,768]{1,0:T(8,128)(2,1)} %tokens_ref.5, ...), custom_call_target="tpu_custom_call" | custom-call | flops 80000000000 | bytes 300000000 | tf_op jit(solution)/shard_map/attend/pallas_call | solution.py:410
  54.5 1.4 collective-permute-done.9.refs_1_.refs_14_
  56.6 3.5 %middle.1 = (f32[128,768]{1,0:T(8,128)}, bf16[128,768]{1,0:T(8,128)(2,1)}) custom-call(s32[2]{0:T(128)} %pad_add_fusion.place_ref, bf16[128,768]{1,0:T(8,128)(2,1)} %tokens_ref.5, f32[1,768]{1,0:T(1,128)} %get-tuple-element.106.gain_ref.gain_two_ref, bf16[128,768]{1,0:T(8,128)(2,1)} %get-tuple-element.63.attended_ref, bf16[192,768]{1,0:T(8,128)(2,1)} %refs_7_.1, ...), custom_call_target="tpu_custom_call" | custom-call | tf_op jit(solution)/shard_map/middle/pallas_call | solution.py:429
  60.0 0.9 collective-permute-start.14
  62.5 3.4 %collective-permute-done.14.refs_3_.refs_7_ = bf16[128,768]{1,0:T(8,128)(2,1)S(1)} collective-permute-done((bf16[128,768]{1,0:T(8,128)(2,1)}, bf16[128,768]{1,0:T(8,128)(2,1)S(1)}, u32[]{:S(2)}, u32[]{:S(2)}) %collective-permute-start.14) | collective-permute-done | bytes 196640 | tf_op jit(solution)/shard_map/ppermute | solution.py:34
  66.0 1.9 collective-permute-done.13.refs_2_.refs_6_
  67.9 5.9 %collective-permute-done.12.refs_1_.refs_5_ = bf16[128,768]{1,0:T(8,128)(2,1)S(1)} collective-permute-done((bf16[128,768]{1,0:T(8,128)(2,1)}, bf16[128,768]{1,0:T(8,128)(2,1)S(1)}, u32[]{:S(2)}, u32[]{:S(2)}) %collective-permute-start.12) | collective-permute-done | bytes 196640 | tf_op jit(solution)/shard_map/ppermute | solution.py:34
  73.7 1.9 all-to-all-done
  75.7 1.5 copy-done
  77.1 4.0 %dispatch.1 = bf16[768,1536]{1,0:T(8,128)(2,1)} custom-call(s32[2,512]{1,0:T(2,128)} %get-tuple-element.73.places_ref, bf16[128,768]{1,0:T(8,128)(2,1)} %get-tuple-element.66.refs_0_.refs_4_.moe_ref, bf16[128,768]{1,0:T(8,128)(2,1)} %copy-done.10, bf16[128,768]{1,0:T(8,128)(2,1)} %copy-done.9, bf16[128,768]{1,0:T(8,128)(2,1)} %copy-done.8, ...), custom_call_target="tpu_custom_call" | custom-call | tf_op jit(solution)/shard_map/dispatch/pallas_call | solution.py:609
  81.1 6.7 %all-to-all-start.1 = ((bf16[32,24,1536]{2,1,0:T(8,128)(2,1)}), bf16[32,24,1536]{2,1,0:T(8,128)(2,1)S(1)}, u32[]{:S(2)}, u32[]{:S(2)}) async-start(bf16[32,24,1536]{2,1,0:T(8,128)(2,1)} %bitcast.35), calls=%async_computation.1 | async-start | bytes 4718592 | tf_op jit(solution)/shard_map/all_to_all | solution.py:914
  88.6 30.5 %all-to-all-done.1 = bf16[32,24,1536]{2,1,0:T(8,128)(2,1)S(1)} async-done(((bf16[32,24,1536]{2,1,0:T(8,128)(2,1)}), bf16[32,24,1536]{2,1,0:T(8,128)(2,1)S(1)}, u32[]{:S(2)}, u32[]{:S(2)}) %all-to-all-start.1) | async-done | bytes 2359328 | tf_op jit(solution)/shard_map/all_to_all | solution.py:914
  119.0 1.5 copy-done.1
  120.5 11.0 %experts.1 = (bf16[768,1536]{1,0:T(8,128)(2,1)}, bf16[2,768,768]{2,1,0:T(8,128)(2,1)}, f32[2,768,768]{2,1,0:T(8,128)}) custom-call(bf16[768,1536]{1,0:T(8,128)(2,1)} %bitcast.28, bf16[2,768,768]{2,1,0:T(8,128)(2,1)} %in_ref.5, bf16[2,768,768]{2,1,0:T(8,128)(2,1)} %out_ref.5), custom_call_target="tpu_custom_call" | custom-call | tf_op jit(solution)/shard_map/experts/pallas_call | solution.py:662
  131.5 4.6 %all-to-all-start.2 = ((bf16[32,24,1536]{2,1,0:T(8,128)(2,1)}), bf16[32,24,1536]{2,1,0:T(8,128)(2,1)S(1)}, u32[]{:S(2)}, u32[]{:S(2)}) async-start(bf16[32,24,1536]{2,1,0:T(8,128)(2,1)} %bitcast.39), calls=%async_computation.2 | async-start | bytes 4718592 | tf_op jit(solution)/shard_map/all_to_all | solution.py:914
  136.1 8.6 %experts_back.3 = (bf16[768,768]{1,0:T(8,128)(2,1)}, bf16[768,768]{1,0:T(8,128)(2,1)}, bf16[192,768]{1,0:T(8,128)(2,1)}, bf16[192,768]{1,0:T(8,128)(2,1)}, bf16[...) custom-call(s32[1]{0:T(128)} %bitcast.7.own_ref, bf16[768,1536]{1,0:T(8,128)(2,1)} %bitcast.29, bf16[768,1664]{1,0:T(8,128)(2,1)} %bitcast.24, ...), custom_call_target="tpu_custom_call" | custom-call | flops 60000002048 | bytes 10000000 | tf_op jit(solution)/shard_map/experts_back/pallas_call | solution.py:725
  146.2 8.6 %experts_back.2 = (bf16[768,768]{1,0:T(8,128)(2,1)}, bf16[768,768]{1,0:T(8,128)(2,1)}, bf16[192,768]{1,0:T(8,128)(2,1)}, bf16[192,768]{1,0:T(8,128)(2,1)}, bf16[...) custom-call(s32[1]{0:T(128)} %bitcast.7.own_ref, bf16[768,1536]{1,0:T(8,128)(2,1)} %bitcast.30, bf16[768,1664]{1,0:T(8,128)(2,1)} %bitcast.26, ...), custom_call_target="tpu_custom_call" | custom-call | flops 3000000000 | bytes 10000000 | tf_op jit(solution)/shard_map/experts_back/pallas_call | solution.py:725
  154.7 2.4 collective-permute-start.15
  157.1 1.4 collective-permute-start.16
  159.2 10.5 %weight_grads.1 = (f32[2,768,768]{2,1,0:T(8,128)}, f32[2,768,768]{2,1,0:T(8,128)}) custom-call(bf16[768,1536]{1,0:T(8,128)(2,1)} %bitcast.31, bf16[2,768,768]{2,1,0:T(8,128)(2,1)} %get-tuple-element.83.act_ref, bf16[768,768]{1,0:T(8,128)(2,1)} %get-tuple-element.84.pre_a, bf16[768,768]{1,0:T(8,128)(2,1)} %get-tuple-element.85.pre_b, ...), custom_call_target="tpu_custom_call" | custom-call | flops 3623878656 | bytes 20000000 | tf_op jit(solution)/shard_map/weight_grads/pallas_call | solution.py:770
  169.7 1.4 copy-done.2
  171.1 5.9 %combine.1 = (bf16[128,896]{1,0:T(8,128)(2,1)}, bf16[128,896]{1,0:T(8,128)(2,1)}, bf16[128,896]{1,0:T(8,128)(2,1)}, bf16[128,896]{1,0:T(8,128)(2,1)}) custom-call(s32[2,512]{1,0:T(2,128)} %get-tuple-element.73.places_ref, s32[2,512]{1,0:T(2,128)} %get-tuple-element.60.ids_ref, bf16[64,768]{1,0:T(8,128)(2,1)} %convert_element_type.24.router_ref, ...), custom_call_target="tpu_custom_call" | custom-call | tf_op jit(solution)/shard_map/combine/pallas_call | solution.py:866
  177.9 3.3 %sum_rows.1 = bf16[512,768]{1,0:T(8,128)(2,1)} custom-call(bf16[192,768]{1,0:T(8,128)(2,1)} %get-tuple-element.75.refs_0_, bf16[192,768]{1,0:T(8,128)(2,1)} %copy-done.28, bf16[192,768]{1,0:T(8,128)(2,1)} %collective-permute-done.16.refs_2_, bf16[192,768]{1,0:T(8,128)(2,1)} %collective-permute-done.17.refs_3_, bf16[192,768]{1,0:T(8,128)(2,1)} %get-tuple-element.79.refs_4_, ...), custom_call_target="tpu_custom_call" | custom-call | flops 20000000000 | bytes 60000000 | tf_op jit(solution)/shard_map/sum_rows/pallas_call | solution.py:815
  181.3 9.2 %all-to-all-start.3 = ((bf16[32,16,768]{2,1,0:T(8,128)(2,1)}), bf16[32,16,768]{2,1,0:T(8,128)(2,1)S(1)}, u32[]{:S(2)}, u32[]{:S(2)}) async-start(bf16[32,16,768]{2,1,0:T(8,128)(2,1)} %bitcast.40), calls=%async_computation.3 | async-start | bytes 1572864 | tf_op jit(solution)/shard_map/all_to_all | solution.py:914
  190.5 2.1 collective-permute-start.21
  193.3 4.5 %collective-permute-done.21.refs_1_ = bf16[128,896]{1,0:T(8,128)(2,1)S(1)} collective-permute-done((bf16[128,896]{1,0:T(8,128)(2,1)S(1)}, bf16[128,896]{1,0:T(8,128)(2,1)S(1)}, u32[]{:S(2)}, u32[]{:S(2)}) %collective-permute-start.21) | collective-permute-done | bytes 229408 | tf_op jit(solution)/shard_map/ppermute | solution.py:34
  197.8 3.0 %collective-permute-done.22.refs_2_ = bf16[128,896]{1,0:T(8,128)(2,1)S(1)} collective-permute-done((bf16[128,896]{1,0:T(8,128)(2,1)S(1)}, bf16[128,896]{1,0:T(8,128)(2,1)S(1)}, u32[]{:S(2)}, u32[]{:S(2)}) %collective-permute-start.22) | collective-permute-done | bytes 229408 | tf_op jit(solution)/shard_map/ppermute | solution.py:34
  200.8 5.7 %collective-permute-done.23.refs_3_ = bf16[128,896]{1,0:T(8,128)(2,1)S(1)} collective-permute-done((bf16[128,896]{1,0:T(8,128)(2,1)S(1)}, bf16[128,896]{1,0:T(8,128)(2,1)S(1)}, u32[]{:S(2)}, u32[]{:S(2)}) %collective-permute-start.23) | collective-permute-done | bytes 229408 | tf_op jit(solution)/shard_map/ppermute | solution.py:34
  207.6 15.8 %backward.1 = (bf16[128,768]{1,0:T(8,128)(2,1)}, f32[128,768]{1,0:T(8,128)}, bf16[1536,896]{1,0:T(8,128)(2,1)}, bf16[1536,896]{1,0:T(8,128)(2,1)}) custom-call(s32[2]{0:T(128)} %pad_add_fusion.place_ref, bf16[128,768]{1,0:T(8,128)(2,1)} %tokens_ref.5, bf16[128,768]{1,0:T(8,128)(2,1)} %cotangent_ref.3, f32[1,768]{1,0:T(1,128)} %get-tuple-element.107.gain_ref.gain_one_ref, ...), custom_call_target="tpu_custom_call" | custom-call | tf_op jit(solution)/shard_map/backward/pallas_call | solution.py:451
  223.9 4.9 %collective-permute-done.24 = bf16[1536,896]{1,0:T(8,128)(2,1)S(1)} collective-permute-done((bf16[1536,896]{1,0:T(8,128)(2,1)}, bf16[1536,896]{1,0:T(8,128)(2,1)S(1)}, u32[]{:S(2)}, u32[]{:S(2)}) %collective-permute-start.24) | collective-permute-done | bytes 2752544 | tf_op jit(solution)/shard_map/ppermute | solution.py:42
  228.9 2.5 add_convert_fusion
  231.4 43.5 %all_to_all.61 = bf16[64,24,896]{2,1,0:T(8,128)(2,1)S(1)} all-to-all(bf16[64,24,896]{2,1,0:T(8,128)(2,1)S(1)} %bitcast.32), channel_id=1, replica_groups=mesh['y'=4,'z'=4,'c'=2,'x'=4] {'y','x','z'}, dimensions={0} | all-to-all | bytes 5505024 | tf_op jit(solution)/shard_map/all_to_all | solution.py:997
  275.3 13.1 %all_to_all.62 = bf16[16,24,896]{2,1,0:T(8,128)(2,1)S(1)} all-to-all(bf16[16,24,896]{2,1,0:T(8,128)(2,1)S(1)} %broadcast_in_dim.15), channel_id=1, replica_groups=mesh['y'=4,'z'=4,'c'=2,'x'=4] {'y','z'}, dimensions={0} | all-to-all | bytes 1376256 | tf_op jit(solution)/shard_map/all_to_all | solution.py:999
  288.5 3.5 %collective-permute-start.25 = (bf16[384,896]{1,0:T(8,128)(2,1)S(1)}, bf16[384,896]{1,0:T(8,128)(2,1)S(1)}, u32[]{:S(2)}, u32[]{:S(2)}) collective-permute-start(bf16[384,896]{1,0:T(8,128)(2,1)S(1)} %bitcast.37), channel_id=1, source_target_pairs={{0,4},{4,0},{1,5},{5,1},{2,6},{6,2},{3,7},{7,3},{8,12},{12,8},{9,1... | collective-permute-start | bytes 2064392 | tf_op jit(solution)/shard_map/ppermute | solution.py:42
  291.9 1.8 collective-permute-done.25.other_ref
  294.6 2.8 finish.1
  297.4 1.3 fusion.5
  (110 shorter events, 19.5 us)
Async XLA Ops:
  5.0 12.3 %collective-permute-start.2 = (bf16[160,768]{1,0:T(8,128)(2,1)}, bf16[160,768]{1,0:T(8,128)(2,1)S(1)}, u32[]{:S(2)}, u32[]{:S(2)}) collective-permute-start(bf16[160,768]{1,0:T(8,128)(2,1)} %line.1.refs_0_.refs_4_.refs_3_), channel_id=1, source_target_pairs={{0,3},{1,0},{2,1},{3,2},{4,7},{5,4},{6,5},{7,6},{8,11},{9,8},{10,9... | collective-permute-start | bytes 737288 | tf_op jit(solution)/shard_map/ppermute | solution.py:34
  8.4 9.0 %collective-permute-start.1 = (bf16[160,768]{1,0:T(8,128)(2,1)}, bf16[160,768]{1,0:T(8,128)(2,1)S(1)}, u32[]{:S(2)}, u32[]{:S(2)}) collective-permute-start(bf16[160,768]{1,0:T(8,128)(2,1)} %line.1.refs_0_.refs_4_.refs_3_), channel_id=1, source_target_pairs={{0,2},{1,3},{2,0},{3,1},{4,6},{5,7},{6,4},{7,5},{8,10},{9,11},{10,... | collective-permute-start | bytes 737288 | tf_op jit(solution)/shard_map/ppermute | solution.py:34
  8.9 15.7 %collective-permute-start = (bf16[160,768]{1,0:T(8,128)(2,1)}, bf16[160,768]{1,0:T(8,128)(2,1)S(1)}, u32[]{:S(2)}, u32[]{:S(2)}) collective-permute-start(bf16[160,768]{1,0:T(8,128)(2,1)} %line.1.refs_0_.refs_4_.refs_3_), channel_id=1, source_target_pairs={{0,1},{1,2},{2,3},{3,0},{4,5},{5,6},{6,7},{7,4},{8,9},{9,10},{10,1... | collective-permute-start | bytes 737288 | tf_op jit(solution)/shard_map/ppermute | solution.py:34
  11.3 31.6 %collective-permute-start.5 = (bf16[288,768]{1,0:T(8,128)(2,1)}, bf16[288,768]{1,0:T(8,128)(2,1)}, u32[]{:S(2)}, u32[]{:S(2)}) collective-permute-start(bf16[288,768]{1,0:T(8,128)(2,1)} %pack.1), channel_id=1, source_target_pairs={{0,3},{1,0},{2,1},{3,2},{4,7},{5,4},{6,5},{7,6},{8,11},{9,8},{10,9... | collective-permute-start | bytes 1327112 | tf_op jit(solution)/shard_map/ppermute | solution.py:34
  13.5 29.7 %collective-permute-start.4 = (bf16[288,768]{1,0:T(8,128)(2,1)}, bf16[288,768]{1,0:T(8,128)(2,1)}, u32[]{:S(2)}, u32[]{:S(2)}) collective-permute-start(bf16[288,768]{1,0:T(8,128)(2,1)} %pack.1), channel_id=1, source_target_pairs={{0,2},{1,3},{2,0},{3,1},{4,6},{5,7},{6,4},{7,5},{8,10},{9,11},{10,... | collective-permute-start | bytes 1327112 | tf_op jit(solution)/shard_map/ppermute | solution.py:34
  17.3 7.3 %copy-start.16 = (bf16[160,768]{1,0:T(8,128)(2,1)}, bf16[160,768]{1,0:T(8,128)(2,1)S(1)}, u32[]{:S(2)}) copy-start(bf16[160,768]{1,0:T(8,128)(2,1)S(1)} %collective-permute-done.2.refs_3_) | copy-start | bytes 737284
  17.3 26.2 %collective-permute-start.3 = (bf16[288,768]{1,0:T(8,128)(2,1)}, bf16[288,768]{1,0:T(8,128)(2,1)}, u32[]{:S(2)}, u32[]{:S(2)}) collective-permute-start(bf16[288,768]{1,0:T(8,128)(2,1)} %pack.1), channel_id=1, source_target_pairs={{0,1},{1,2},{2,3},{3,0},{4,5},{5,6},{6,7},{7,4},{8,9},{9,10},{10,1... | collective-permute-start | bytes 1327112 | tf_op jit(solution)/shard_map/ppermute | solution.py:34
  17.4 7.2 %copy-start.17 = (bf16[160,768]{1,0:T(8,128)(2,1)}, bf16[160,768]{1,0:T(8,128)(2,1)S(1)}, u32[]{:S(2)}) copy-start(bf16[160,768]{1,0:T(8,128)(2,1)S(1)} %collective-permute-done.1.refs_2_) | copy-start | bytes 737284
  31.7 22.7 %collective-permute-start.11 = (bf16[192,768]{1,0:T(8,128)(2,1)}, bf16[192,768]{1,0:T(8,128)(2,1)S(1)}, u32[]{:S(2)}, u32[]{:S(2)}) collective-permute-start(bf16[192,768]{1,0:T(8,128)(2,1)} %hold_back.1), channel_id=1, source_target_pairs={{0,3},{1,0},{2,1},{3,2},{4,7},{5,4},{6,5},{7,6},{8,11},{9,8},{10,9... | collective-permute-start | bytes 884744 | tf_op jit(solution)/shard_map/ppermute | solution.py:34
  31.7 22.7 %collective-permute-start.10 = (bf16[192,768]{1,0:T(8,128)(2,1)}, bf16[192,768]{1,0:T(8,128)(2,1)S(1)}, u32[]{:S(2)}, u32[]{:S(2)}) collective-permute-start(bf16[192,768]{1,0:T(8,128)(2,1)} %hold_back.1), channel_id=1, source_target_pairs={{0,2},{1,3},{2,0},{3,1},{4,6},{5,7},{6,4},{7,5},{8,10},{9,11},{10,... | collective-permute-start | bytes 884744 | tf_op jit(solution)/shard_map/ppermute | solution.py:34
  32.4 10.1 %copy-start.23 = (f32[12,32]{1,0:T(8,128)S(1)}, f32[12,32]{1,0:T(8,128)}, u32[]{:S(2)}) copy-start(f32[12,32]{1,0:T(8,128)} %get-tuple-element.62) | copy-start | bytes 4612
  32.4 11.8 %copy-start.24 = (f32[2,768]{1,0:T(2,128)S(1)}, f32[2,768]{1,0:T(2,128)}, u32[]{:S(2)}) copy-start(f32[2,768]{1,0:T(2,128)} %get-tuple-element.59) | copy-start | bytes 18436
  32.4 43.3 %all-to-all-start = ((bf16[32,24,1664]{2,1,0:T(8,128)(2,1)}), bf16[32,24,1664]{2,1,0:T(8,128)(2,1)S(1)}, u32[]{:S(2)}, u32[]{:S(2)}) async-start(bf16[32,24,1664]{2,1,0:T(8,128)(2,1)} %bitcast.33), calls=%async_computation | async-start | bytes 5111808 | tf_op jit(solution)/shard_map/all_to_all | solution.py:914
  42.4 3.5 %copy-start.15 = (bf16[192,768]{1,0:T(8,128)(2,1)S(1)}, bf16[192,768]{1,0:T(8,128)(2,1)}, u32[]{:S(2)}) copy-start(bf16[192,768]{1,0:T(8,128)(2,1)} %hold_back.1) | copy-start | bytes 884740
  42.9 3.0 %collective-permute-start.8 = (bf16[288,768]{1,0:T(8,128)(2,1)}, bf16[288,768]{1,0:T(8,128)(2,1)S(1)}, u32[]{:S(2)}, u32[]{:S(2)}) collective-permute-start(bf16[288,768]{1,0:T(8,128)(2,1)} %collective-permute-done.5.refs_5_.refs_10_), channel_id=1, source_target_pairs={{0,4},{4,0},{1,5},{5,1},{2,6},{6,2},{3,7},{7,3},{8,12},{12,8},{9,1... | collective-permute-start | bytes 1327112 | tf_op jit(solution)/shard_map/ppermute | solution.py:42
  43.2 3.5 %collective-permute-start.7 = (bf16[288,768]{1,0:T(8,128)(2,1)}, bf16[288,768]{1,0:T(8,128)(2,1)S(1)}, u32[]{:S(2)}, u32[]{:S(2)}) collective-permute-start(bf16[288,768]{1,0:T(8,128)(2,1)} %collective-permute-done.4.refs_4_.refs_9_), channel_id=1, source_target_pairs={{0,4},{4,0},{1,5},{5,1},{2,6},{6,2},{3,7},{7,3},{8,12},{12,8},{9,1... | collective-permute-start | bytes 1327112 | tf_op jit(solution)/shard_map/ppermute | solution.py:42
  43.5 3.2 %collective-permute-start.6 = (bf16[288,768]{1,0:T(8,128)(2,1)}, bf16[288,768]{1,0:T(8,128)(2,1)S(1)}, u32[]{:S(2)}, u32[]{:S(2)}) collective-permute-start(bf16[288,768]{1,0:T(8,128)(2,1)} %collective-permute-done.3.refs_3_.refs_8_), channel_id=1, source_target_pairs={{0,4},{4,0},{1,5},{5,1},{2,6},{6,2},{3,7},{7,3},{8,12},{12,8},{9,1... | collective-permute-start | bytes 1327112 | tf_op jit(solution)/shard_map/ppermute | solution.py:42
  45.9 9.9 %collective-permute-start.9 = (bf16[192,768]{1,0:T(8,128)(2,1)S(1)}, bf16[192,768]{1,0:T(8,128)(2,1)S(1)}, u32[]{:S(2)}, u32[]{:S(2)}) collective-permute-start(bf16[192,768]{1,0:T(8,128)(2,1)S(1)} %copy-done.15), channel_id=1, source_target_pairs={{0,1},{1,2},{2,3},{3,0},{4,5},{5,6},{6,7},{7,4},{8,9},{9,10},{10,1... | collective-permute-start | bytes 884744 | tf_op jit(solution)/shard_map/ppermute | solution.py:34
  60.0 5.9 %collective-permute-start.14 = (bf16[128,768]{1,0:T(8,128)(2,1)}, bf16[128,768]{1,0:T(8,128)(2,1)S(1)}, u32[]{:S(2)}, u32[]{:S(2)}) collective-permute-start(bf16[128,768]{1,0:T(8,128)(2,1)} %get-tuple-element.66.refs_0_.refs_4_.moe_ref), channel_id=1, source_target_pairs={{0,3},{1,0},{2,1},{3,2},{4,7},{5,4},{6,5},{7,6},{8,11},{9,8},{10,9... | collective-permute-start | bytes 589832 | tf_op jit(solution)/shard_map/ppermute | solution.py:34
  61.0 6.9 %collective-permute-start.13 = (bf16[128,768]{1,0:T(8,128)(2,1)}, bf16[128,768]{1,0:T(8,128)(2,1)S(1)}, u32[]{:S(2)}, u32[]{:S(2)}) collective-permute-start(bf16[128,768]{1,0:T(8,128)(2,1)} %get-tuple-element.66.refs_0_.refs_4_.moe_ref), channel_id=1, source_target_pairs={{0,2},{1,3},{2,0},{3,1},{4,6},{5,7},{6,4},{7,5},{8,10},{9,11},{10,... | collective-permute-start | bytes 589832 | tf_op jit(solution)/shard_map/ppermute | solution.py:34
  61.7 12.0 %collective-permute-start.12 = (bf16[128,768]{1,0:T(8,128)(2,1)}, bf16[128,768]{1,0:T(8,128)(2,1)S(1)}, u32[]{:S(2)}, u32[]{:S(2)}) collective-permute-start(bf16[128,768]{1,0:T(8,128)(2,1)} %get-tuple-element.66.refs_0_.refs_4_.moe_ref), channel_id=1, source_target_pairs={{0,1},{1,2},{2,3},{3,0},{4,5},{5,6},{6,7},{7,4},{8,9},{9,10},{10,1... | collective-permute-start | bytes 589832 | tf_op jit(solution)/shard_map/ppermute | solution.py:34
  66.0 9.7 %copy-start.8 = (bf16[128,768]{1,0:T(8,128)(2,1)}, bf16[128,768]{1,0:T(8,128)(2,1)S(1)}, u32[]{:S(2)}) copy-start(bf16[128,768]{1,0:T(8,128)(2,1)S(1)} %collective-permute-done.14.refs_3_.refs_7_) | copy-start | bytes 589828
  67.9 7.8 %copy-start.9 = (bf16[128,768]{1,0:T(8,128)(2,1)}, bf16[128,768]{1,0:T(8,128)(2,1)S(1)}, u32[]{:S(2)}) copy-start(bf16[128,768]{1,0:T(8,128)(2,1)S(1)} %collective-permute-done.13.refs_2_.refs_6_) | copy-start | bytes 589828
  73.7 1.9 copy-start.10
  75.7 1.5 copy-start
  81.1 6.8 %copy-start.22 = (f32[64,768]{1,0:T(8,128)S(1)}, f32[64,768]{1,0:T(8,128)}, u32[]{:S(2)}) copy-start(f32[64,768]{1,0:T(8,128)} %get-tuple-element.61) | copy-start | bytes 589828
  81.1 37.9 %all-to-all-start.1 = ((bf16[32,24,1536]{2,1,0:T(8,128)(2,1)}), bf16[32,24,1536]{2,1,0:T(8,128)(2,1)S(1)}, u32[]{:S(2)}, u32[]{:S(2)}) async-start(bf16[32,24,1536]{2,1,0:T(8,128)(2,1)} %bitcast.35), calls=%async_computation.1 | async-start | bytes 4718592 | tf_op jit(solution)/shard_map/all_to_all | solution.py:914
  119.0 1.5 copy-start.1
  131.5 38.2 %all-to-all-start.2 = ((bf16[32,24,1536]{2,1,0:T(8,128)(2,1)}), bf16[32,24,1536]{2,1,0:T(8,128)(2,1)S(1)}, u32[]{:S(2)}, u32[]{:S(2)}) async-start(bf16[32,24,1536]{2,1,0:T(8,128)(2,1)} %bitcast.39), calls=%async_computation.2 | async-start | bytes 4718592 | tf_op jit(solution)/shard_map/all_to_all | solution.py:914
  144.7 13.8 %collective-permute-start.18 = (bf16[192,768]{1,0:T(8,128)(2,1)}, bf16[192,768]{1,0:T(8,128)(2,1)S(1)}, u32[]{:S(2)}, u32[]{:S(2)}) collective-permute-start(bf16[192,768]{1,0:T(8,128)(2,1)} %get-tuple-element.80), channel_id=1, source_target_pairs={{0,3},{1,0},{2,1},{3,2},{4,7},{5,4},{6,5},{7,6},{8,11},{9,8},{10,9... | collective-permute-start | bytes 884744 | tf_op jit(solution)/shard_map/ppermute | solution.py:34
  145.5 31.5 %collective-permute-start.19 = (bf16[192,768]{1,0:T(8,128)(2,1)}, bf16[192,768]{1,0:T(8,128)(2,1)S(1)}, u32[]{:S(2)}, u32[]{:S(2)}) collective-permute-start(bf16[192,768]{1,0:T(8,128)(2,1)} %get-tuple-element.81), channel_id=1, source_target_pairs={{0,2},{1,3},{2,0},{3,1},{4,6},{5,7},{6,4},{7,5},{8,10},{9,11},{10,... | collective-permute-start | bytes 884744 | tf_op jit(solution)/shard_map/ppermute | solution.py:34
  145.8 31.3 %collective-permute-start.20 = (bf16[192,768]{1,0:T(8,128)(2,1)}, bf16[192,768]{1,0:T(8,128)(2,1)S(1)}, u32[]{:S(2)}, u32[]{:S(2)}) collective-permute-start(bf16[192,768]{1,0:T(8,128)(2,1)} %get-tuple-element.82), channel_id=1, source_target_pairs={{0,1},{1,2},{2,3},{3,0},{4,5},{5,6},{6,7},{7,4},{8,9},{9,10},{10,1... | collective-permute-start | bytes 884744 | tf_op jit(solution)/shard_map/ppermute | solution.py:34
  154.7 22.3 %collective-permute-start.15 = (bf16[192,768]{1,0:T(8,128)(2,1)}, bf16[192,768]{1,0:T(8,128)(2,1)S(1)}, u32[]{:S(2)}, u32[]{:S(2)}) collective-permute-start(bf16[192,768]{1,0:T(8,128)(2,1)} %get-tuple-element.76), channel_id=1, source_target_pairs={{0,3},{1,0},{2,1},{3,2},{4,7},{5,4},{6,5},{7,6},{8,11},{9,8},{10,9... | collective-permute-start | bytes 884744 | tf_op jit(solution)/shard_map/ppermute | solution.py:34
  157.1 19.9 %collective-permute-start.16 = (bf16[192,768]{1,0:T(8,128)(2,1)}, bf16[192,768]{1,0:T(8,128)(2,1)}, u32[]{:S(2)}, u32[]{:S(2)}) collective-permute-start(bf16[192,768]{1,0:T(8,128)(2,1)} %get-tuple-element.77), channel_id=1, source_target_pairs={{0,2},{1,3},{2,0},{3,1},{4,6},{5,7},{6,4},{7,5},{8,10},{9,11},{10,... | collective-permute-start | bytes 884744 | tf_op jit(solution)/shard_map/ppermute | solution.py:34
  158.5 11.2 %copy-start.25 = (bf16[192,768]{1,0:T(8,128)(2,1)}, bf16[192,768]{1,0:T(8,128)(2,1)S(1)}, u32[]{:S(2)}) copy-start(bf16[192,768]{1,0:T(8,128)(2,1)S(1)} %collective-permute-done.18.refs_5_) | copy-start | bytes 884740
  158.5 18.5 %collective-permute-start.17 = (bf16[192,768]{1,0:T(8,128)(2,1)}, bf16[192,768]{1,0:T(8,128)(2,1)}, u32[]{:S(2)}, u32[]{:S(2)}) collective-permute-start(bf16[192,768]{1,0:T(8,128)(2,1)} %get-tuple-element.78), channel_id=1, source_target_pairs={{0,1},{1,2},{2,3},{3,0},{4,5},{5,6},{6,7},{7,4},{8,9},{9,10},{10,1... | collective-permute-start | bytes 884744 | tf_op jit(solution)/shard_map/ppermute | solution.py:34
  177.9 12.5 %copy-start.31 = (bf16[128,896]{1,0:T(8,128)(2,1)S(1)}, bf16[128,896]{1,0:T(8,128)(2,1)}, u32[]{:S(2)}) copy-start(bf16[128,896]{1,0:T(8,128)(2,1)} %get-tuple-element.92) | copy-start | bytes 688132
  177.9 14.7 %copy-start.30 = (bf16[128,896]{1,0:T(8,128)(2,1)S(1)}, bf16[128,896]{1,0:T(8,128)(2,1)}, u32[]{:S(2)}) copy-start(bf16[128,896]{1,0:T(8,128)(2,1)} %get-tuple-element.93) | copy-start | bytes 688132
  177.9 14.9 %copy-start.29 = (bf16[128,896]{1,0:T(8,128)(2,1)S(1)}, bf16[128,896]{1,0:T(8,128)(2,1)}, u32[]{:S(2)}) copy-start(bf16[128,896]{1,0:T(8,128)(2,1)} %get-tuple-element.94) | copy-start | bytes 688132
  181.3 25.3 %all-to-all-start.3 = ((bf16[32,16,768]{2,1,0:T(8,128)(2,1)}), bf16[32,16,768]{2,1,0:T(8,128)(2,1)S(1)}, u32[]{:S(2)}, u32[]{:S(2)}) async-start(bf16[32,16,768]{2,1,0:T(8,128)(2,1)} %bitcast.40), calls=%async_computation.3 | async-start | bytes 1572864 | tf_op jit(solution)/shard_map/all_to_all | solution.py:914
  190.5 7.3 %collective-permute-start.21 = (bf16[128,896]{1,0:T(8,128)(2,1)S(1)}, bf16[128,896]{1,0:T(8,128)(2,1)S(1)}, u32[]{:S(2)}, u32[]{:S(2)}) collective-permute-start(bf16[128,896]{1,0:T(8,128)(2,1)S(1)} %copy-done.31), channel_id=1, source_target_pairs={{0,3},{1,0},{2,1},{3,2},{4,7},{5,4},{6,5},{7,6},{8,11},{9,8},{10,9... | collective-permute-start | bytes 688136 | tf_op jit(solution)/shard_map/ppermute | solution.py:34
  192.6 8.2 %collective-permute-start.22 = (bf16[128,896]{1,0:T(8,128)(2,1)S(1)}, bf16[128,896]{1,0:T(8,128)(2,1)S(1)}, u32[]{:S(2)}, u32[]{:S(2)}) collective-permute-start(bf16[128,896]{1,0:T(8,128)(2,1)S(1)} %copy-done.30), channel_id=1, source_target_pairs={{0,2},{1,3},{2,0},{3,1},{4,6},{5,7},{6,4},{7,5},{8,10},{9,11},{10,... | collective-permute-start | bytes 688136 | tf_op jit(solution)/shard_map/ppermute | solution.py:34
  192.8 13.7 %collective-permute-start.23 = (bf16[128,896]{1,0:T(8,128)(2,1)S(1)}, bf16[128,896]{1,0:T(8,128)(2,1)S(1)}, u32[]{:S(2)}, u32[]{:S(2)}) collective-permute-start(bf16[128,896]{1,0:T(8,128)(2,1)S(1)} %copy-done.29), channel_id=1, source_target_pairs={{0,1},{1,2},{2,3},{3,0},{4,5},{5,6},{6,7},{7,4},{8,9},{9,10},{10,1... | collective-permute-start | bytes 688136 | tf_op jit(solution)/shard_map/ppermute | solution.py:34
  197.8 8.8 %copy-start.19 = (bf16[128,896]{1,0:T(8,128)(2,1)}, bf16[128,896]{1,0:T(8,128)(2,1)S(1)}, u32[]{:S(2)}) copy-start(bf16[128,896]{1,0:T(8,128)(2,1)S(1)} %collective-permute-done.21.refs_1_) | copy-start | bytes 688132
  200.8 5.8 %copy-start.20 = (bf16[128,896]{1,0:T(8,128)(2,1)}, bf16[128,896]{1,0:T(8,128)(2,1)S(1)}, u32[]{:S(2)}) copy-start(bf16[128,896]{1,0:T(8,128)(2,1)S(1)} %collective-permute-done.22.refs_2_) | copy-start | bytes 688132
  223.4 5.5 %collective-permute-start.24 = (bf16[1536,896]{1,0:T(8,128)(2,1)}, bf16[1536,896]{1,0:T(8,128)(2,1)S(1)}, u32[]{:S(2)}, u32[]{:S(2)}) collective-permute-start(bf16[1536,896]{1,0:T(8,128)(2,1)} %get-tuple-element.98), channel_id=1, source_target_pairs={{0,4},{4,0},{1,5},{5,1},{2,6},{6,2},{3,7},{7,3},{8,12},{12,8},{9,1... | collective-permute-start | bytes 8257544 | tf_op jit(solution)/shard_map/ppermute | solution.py:42
  288.5 5.2 %copy-start.4 = (bf16[16,24,896]{2,1,0:T(8,128)(2,1)}, bf16[16,24,896]{2,1,0:T(8,128)(2,1)S(1)}, u32[]{:S(2)}) copy-start(bf16[16,24,896]{2,1,0:T(8,128)(2,1)S(1)} %all_to_all.62) | copy-start | bytes 2064388
  288.5 5.2 %collective-permute-start.25 = (bf16[384,896]{1,0:T(8,128)(2,1)S(1)}, bf16[384,896]{1,0:T(8,128)(2,1)S(1)}, u32[]{:S(2)}, u32[]{:S(2)}) collective-permute-start(bf16[384,896]{1,0:T(8,128)(2,1)S(1)} %bitcast.37), channel_id=1, source_target_pairs={{0,4},{4,0},{1,5},{5,1},{2,6},{6,2},{3,7},{7,3},{8,12},{12,8},{9,1... | collective-permute-start | bytes 2064392 | tf_op jit(solution)/shard_map/ppermute | solution.py:42
  (14 other events, 13.0 us)

commit v5 on v3

--- a/solution.py
+++ b/solution.py
@@ -157,8 +157,7 @@
     f32, bf16 = jnp.float32, jnp.bfloat16
     mats, near, far = refs[:3], refs[3:6], refs[6:9]
     hidden_ref, q_ref, k_ref, v_ref, probs_ref, attended_ref = refs[9:15]
-    held, sems = refs[15:]
-    weights = [held.at[n] for n in range(3)]
+    weights, sems = refs[15:18], refs[18]
     copies = start_copies(
         block_copies(place_ref[0], place_ref[1], mats, near, far, weights), sems
     )
@@ -223,15 +222,10 @@
     *refs,
 ):
     f32, bf16 = jnp.float32, jnp.bfloat16
-    homes, mats, near, far, near_out = refs[:4], refs[4:8], refs[8:11], refs[11:14], refs[14:17]
-    result_ref, tokens_out, kept_ref, given_ref = refs[17:21]
-    held, grads_ref, small_ref, sems = refs[21:]
-    weights = [held.at[n] for n in range(4)]
-    copies = start_copies(
-        block_copies(place_ref[0], place_ref[1], mats[:3], near, far, weights[:3])
-        + whole_copies(place_ref[0], mats[3], near_out, weights[3]),
-        sems,
-    )
+    homes, mats = refs[:4], refs[4:8]
+    result_ref, tokens_out, kept_ref, given_ref = refs[8:12]
+    held, grads_ref, small_ref, sems = refs[12:]
+    copies = start_copies([(m, held.at[n]) for n, m in enumerate(mats)], sems)
     features = tokens_ref.shape[1]
     core = place_ref[1]
     width = features // 4
@@ -293,8 +287,7 @@
     )
     branch = grad_middle.astype(bf16)
     leave(3, attended_ref[...], branch)
-    for c in copies[21:]:
-        c.wait()
+    copies[3].wait()
     grad_attended = lax.dot_general(branch, held[3], LAST, preferred_element_type=f32).astype(bf16)
     grad_q, grad_k, grad_v, diagonals = [], [], [], []
     for pair in range(probs_ref.shape[0] // 2):
@@ -338,8 +331,7 @@
     for n, parts in enumerate((grad_q, grad_k, grad_v)):
         grad = jnp.concatenate(parts, axis=1)
         leave(n, hidden, grad)
-        for c in copies[7 * n : 7 * n + 7]:
-            c.wait()
+        copies[n].wait()
         grad_hidden = grad_hidden + lax.dot_general(
             grad, held[n], LAST, preferred_element_type=f32
         )
@@ -358,9 +350,11 @@
 
 
 ANYWHERE = pl.BlockSpec(memory_space=pl.ANY)
+UNREAD = pl.BlockSpec(memory_space=pltpu.HBM)
 SCALARS = pl.BlockSpec(memory_space=pltpu.SMEM)
 WHOLE = pl.BlockSpec(memory_space=pltpu.VMEM)
-ROOM = pltpu.CompilerParams(vmem_limit_bytes=56 * 1024 * 1024)
+ROOM = pltpu.CompilerParams(vmem_limit_bytes=38 * 1024 * 1024)
+SOME = pltpu.CompilerParams(vmem_limit_bytes=20 * 1024 * 1024)
 
 
 def make_line(routes, gains, bias, router, cotangent):
@@ -371,7 +365,7 @@
         in_specs=[WHOLE] * 4 + [ANYWHERE],
         out_specs=WHOLE,
         scratch_shapes=[pltpu.VMEM((32, cols), jnp.float32), pltpu.SemaphoreType.DMA],
-        compiler_params=ROOM,
+        compiler_params=SOME,
         name="line",
     )(routes, gains, bias, router, cotangent)
 
@@ -385,7 +379,7 @@
         in_specs=[SCALARS] + [ANYWHERE] * (count + 1),
         out_specs=WHOLE,
         scratch_shapes=[pltpu.SemaphoreType.DMA((count,))],
-        compiler_params=ROOM,
+        compiler_params=SOME,
         name="pack",
     )(core[None], *mats, after)
 
@@ -407,16 +401,16 @@
 def attend(where, tokens, gain, bias, mats, near, far):
     rows, cols = mats[0].shape
     state = jax.ShapeDtypeStruct(tokens.shape, jnp.bfloat16)
+    full = jax.ShapeDtypeStruct((4 * rows, cols), jnp.bfloat16)
     return pl.pallas_call(
         attend_kernel,
-        out_shape=[state] * 4 + [jax.ShapeDtypeStruct(bias.shape, jnp.float32), state],
+        out_shape=[state] * 4
+        + [jax.ShapeDtypeStruct(bias.shape, jnp.float32), state]
+        + [full] * 3,
         in_specs=[SCALARS] + [WHOLE] * 3 + [ANYWHERE] * 9,
-        out_specs=[WHOLE] * 6,
-        scratch_shapes=[
-            pltpu.VMEM((3, 4 * rows, cols), jnp.bfloat16),
-            pltpu.SemaphoreType.DMA((21,)),
-        ],
-        compiler_params=ROOM,
+        out_specs=[WHOLE] * 9,
+        scratch_shapes=[pltpu.SemaphoreType.DMA((21,))],
+        compiler_params=SOME,
         cost_estimate=pl.CostEstimate(
             flops=80000000000, bytes_accessed=300000000, transcendentals=0
         ),
@@ -431,14 +425,12 @@
         out_shape=[
             jax.ShapeDtypeStruct(tokens.shape, jnp.float32),
             jax.ShapeDtypeStruct(tokens.shape, jnp.bfloat16),
+            jax.ShapeDtypeStruct((4 * rows, cols), jnp.bfloat16),
         ],
         in_specs=[SCALARS] + [WHOLE] * 3 + [ANYWHERE] * 4,
-        out_specs=[WHOLE] * 2,
-        scratch_shapes=[
-            pltpu.VMEM((4 * rows, cols), jnp.bfloat16),
-            pltpu.SemaphoreType.DMA((4,)),
-        ],
-        compiler_params=ROOM,
+        out_specs=[WHOLE] * 3,
+        scratch_shapes=[pltpu.SemaphoreType.DMA((4,))],
+        compiler_params=SOME,
         name="middle",
     )(where, tokens, gain, attended, mat, *near)
 
@@ -456,13 +448,13 @@
             shape((2 * features, features + 128), bf16),
             shape((2 * features, features + 128), bf16),
         ],
-        in_specs=[SCALARS] + [WHOLE] * 20 + [ANYWHERE] * 13,
+        in_specs=[SCALARS] + [WHOLE] * 20 + [ANYWHERE] * 4,
         out_specs=[WHOLE] * 4,
         scratch_shapes=[
             pltpu.VMEM((4, features, features), bf16),
             pltpu.VMEM((features, features), bf16),
             pltpu.VMEM((2 * features, 128), f32),
-            pltpu.SemaphoreType.DMA((25,)),
+            pltpu.SemaphoreType.DMA((4,)),
         ],
         compiler_params=ROOM,
         name="backward",
@@ -502,7 +494,7 @@
         + [shape(experts_all, shard_rows), shape(2, shard_rows), shape(*bias_shape)],
         in_specs=[SCALARS] + [WHOLE] * 2,
         out_specs=[WHOLE] * 7,
-        compiler_params=ROOM,
+        compiler_params=SOME,
         name="finish",
     )(core, own, other)
 
@@ -586,7 +578,7 @@
         ],
         in_specs=[SCALARS] + [WHOLE] * 4 + [ANYWHERE],
         out_specs=[WHOLE] * 7,
-        compiler_params=ROOM,
+        compiler_params=SOME,
         cost_estimate=pl.CostEstimate(
             flops=30000000000, bytes_accessed=100000000, transcendentals=0
         ),
@@ -609,9 +601,9 @@
     return pl.pallas_call(
         dispatch_kernel,
         out_shape=jax.ShapeDtypeStruct((rows, 2 * pieces[0].shape[1]), jnp.bfloat16),
-        in_specs=[WHOLE] * 5 + [ANYWHERE],
+        in_specs=[WHOLE] * 5 + [UNREAD],
         out_specs=WHOLE,
-        compiler_params=ROOM,
+        compiler_params=SOME,
         name="dispatch",
     )(places, *pieces, after)
 
@@ -803,7 +795,7 @@
         out_shape=jax.ShapeDtypeStruct((rows // (2 * capacity) * 16, features), jnp.bfloat16),
         in_specs=[WHOLE] * 4 + [ANYWHERE] * len(after),
         out_specs=WHOLE,
-        compiler_params=ROOM,
+        compiler_params=SOME,
         cost_estimate=pl.CostEstimate(
             flops=20000000000, bytes_accessed=60000000, transcendentals=0
         ),
@@ -854,7 +846,7 @@
         out_shape=[jax.ShapeDtypeStruct((tokens, features + 128), jnp.bfloat16)] * 4,
         in_specs=[WHOLE] * 12 + [ANYWHERE],
         out_specs=[WHOLE] * 4,
-        compiler_params=ROOM,
+        compiler_params=SOME,
         name="combine",
     )(places, ids, router_w, returned, *grads, *moes, after)
 
@@ -921,7 +913,7 @@
     position_bias = jnp.einsum("ijb,hb->hij", onehot, bias_table, preferred_element_type=f32)
     masked_bias = jnp.where(allowed[None], position_bias, -1000000000.0)
     far = [swap_core(piece) for piece in near]
-    hidden_one, queries, key_rows, value_rows, probs, attended = attend(
+    hidden_one, queries, key_rows, value_rows, probs, attended, *full_qkv = attend(
         where,
         tokens,
         gain_one,
@@ -930,7 +922,7 @@
         near,
         far,
     )
-    middle, moe_in = to_middle(
+    middle, moe_in, full_out = to_middle(
         where, tokens, gain_two, attended, w_output, near_out
     )
 
@@ -965,13 +957,8 @@
         spots,
         back_rows,
         *homes,
-        w_query,
-        w_key,
-        w_value,
-        w_output,
-        *near,
-        *far,
-        *near_out,
+        *full_qkv,
+        full_out,
     )
     piece = shard_rows // 8
     wide = features + 128

time: 298 us -> 305 us (1.023)
  local copies, waits for them, and re-layouts: 10.4 us -> 49.2 us
  Pallas kernels: 87.2 us -> 61.7 us
  waiting for transfers between devices: 52.6 us -> 47.9 us
  other arithmetic: 7.85 us -> 3.51 us
    unnamed x58 -> x156, local copies, waits for them, and re-layouts: 7.07 us -> 47.2 us
    ppermute x18, waiting for transfers between devices: 39 us -> 33.3 us  [shift(): lax.ppermute(block, axis, [(i, (i + step) % ranks) for i in range(ranks)])]
    pallas_call x1, Pallas kernels: 15.8 us -> 11 us  [backward(): pl.pallas_call(backward_kernel, out_shape=[shape((count, features), bf16)...]
    pallas_call x1, Pallas kernels: 10 us -> 6.3 us  [weight_grads(): pl.pallas_call(weight_grads_kernel, grid=(2, cuts), out_shape=[jax.ShapeD...]
    pallas_call x1, Pallas kernels: 11 us -> 7.6 us  [experts(): pl.pallas_call(expert_kernel, grid=(2, rows // STEP), out_shape=[jax.Shap...]
  transfers between devices with their start and end apart: 26 -> 26, of which waited for: 13 -> 13; matrix products, arithmetic and copies ran while one was open for 2% -> 1% of each run, Pallas kernels for 16% -> 12%
where the time goes in v5:
time: 305 us; the launch traced here: 303 us
  blocking collectives  97.2 us (32%)
  Pallas kernels  61.7 us (20%)
  local copies, waits for them, and re-layouts  49.2 us (16%)
  waiting for transfers between devices  47.9 us (16%)
  starting transfers between devices  42.2 us (14%)
  other arithmetic  3.51 us (1%)
    unnamed x156, local copies, waits for them, and re-layouts  47.2 us
    all_to_all x1, blocking collectives, layer(): spread = lax.all_to_all(paired, ('y', 'x', 'z'), 0, 0, tiled=True)  44.4 us
    all_to_all x1, blocking collectives, to_owners(): return lax.all_to_all(outgoing, ('y', 'z', 'c'), 0, 0, tiled=True)  39.6 us
    ppermute x18, waiting for transfers between devices, shift(): lax.ppermute(block, axis, [(i, (i + step) % ranks) for i in range(ranks)])  33.3 us
    all_to_all x3, starting transfers between devices, to_owners(): return lax.all_to_all(outgoing, ('y', 'z', 'c'), 0, 0, tiled=True)  22 us
    ppermute x18, starting transfers between devices, shift(): lax.ppermute(block, axis, [(i, (i + step) % ranks) for i in range(ranks)])  14.8 us
    all_to_all x1, blocking collectives, layer(): lax.all_to_all(jnp.broadcast_to(mine[None], (16, piece, wide)).reshape(16...  13.1 us
    pallas_call x1, Pallas kernels, experts_back(): pl.pallas_call(functools.partial(expert_back_kernel, capacity), grid=(2,)...  12.4 us
  transfers between devices with their start and end apart: 26, of which 13 were waited for; matrix products, arithmetic and copies ran while one was open for 1% of the time, Pallas kernels for 12%

profile of v5, /device:TPU:1, one launch (start us, length us, event | category | flops | bytes accessed | tf_op | source)
XLA Modules:
  0.0 303.2 jit_solution(2234582272586610602)
XLA Ops:
  5.3 3.4 %collective-permute-start.2 = (bf16[160,768]{1,0:T(8,128)(2,1)S(1)}, bf16[160,768]{1,0:T(8,128)(2,1)S(1)}, u32[]{:S(2)}, u32[]{:S(2)}) collective-permute-start(bf16[160,768]{1,0:T(8,128)(2,1)S(1)} %line.1.refs_0_.refs_4_.refs_3_), channel_id=1, source_target_pairs={{0,3},{1,0},{2,1},{3,2},{4,7},{5,4},{6,5},{7,6},{8,11},{9,8},{10,9... | collective-permute-start | bytes 737288 | tf_op jit(solution)/shard_map/ppermute | solution.py:34
  13.3 2.1 collective-permute-start.5
  15.4 1.2 collective-permute-start.4
  18.8 5.8 %collective-permute-done.refs_1_ = bf16[160,768]{1,0:T(8,128)(2,1)S(1)} collective-permute-done((bf16[160,768]{1,0:T(8,128)(2,1)S(1)}, bf16[160,768]{1,0:T(8,128)(2,1)S(1)}, u32[]{:S(2)}, u32[]{:S(2)}) %collective-permute-start) | collective-permute-done | bytes 245792 | tf_op jit(solution)/shard_map/ppermute | solution.py:34
  24.7 2.5 dispatch_grads.1
  27.2 1.5 copy-done.1
  29.4 1.7 hold_back.1
  31.7 9.5 %all-to-all-start = ((bf16[32,24,1664]{2,1,0:T(8,128)(2,1)}), bf16[32,24,1664]{2,1,0:T(8,128)(2,1)S(1)}, u32[]{:S(2)}, u32[]{:S(2)}) async-start(bf16[32,24,1664]{2,1,0:T(8,128)(2,1)} %bitcast.29), calls=%async_computation | async-start | bytes 5111808 | tf_op jit(solution)/shard_map/all_to_all | solution.py:892
  42.3 1.2 collective-permute-done.3.refs_3_
  44.7 1.2 collective-permute-done.6.refs_6_
  46.0 6.1 %attend.1 = (bf16[128,768]{1,0:T(8,128)(2,1)S(1)}, bf16[128,768]{1,0:T(8,128)(2,1)S(1)}, bf16[128,768]{1,0:T(8,128)(2,1)S(1)}, bf16[128,768]{1,0:T(8,128)(2,1)S(...) custom-call(s32[2]{0:T(128)S(1)} %pad_add_fusion.place_ref, ...), custom_call_target="tpu_custom_call" | custom-call | flops 80000000000 | bytes 300000000 | tf_op jit(solution)/shard_map/attend/pallas_call | solution.py:405
  56.0 2.2 middle.1
  60.0 2.3 collective-permute-start.14
  63.1 3.9 %collective-permute-done.14.refs_3_.refs_7_ = bf16[128,768]{1,0:T(8,128)(2,1)S(1)} collective-permute-done((bf16[128,768]{1,0:T(8,128)(2,1)S(1)}, bf16[128,768]{1,0:T(8,128)(2,1)S(1)}, u32[]{:S(2)}, u32[]{:S(2)}) %collective-permute-start.14) | collective-permute-done | bytes 196640 | tf_op jit(solution)/shard_map/ppermute | solution.py:34
  67.0 2.8 collective-permute-done.13.refs_2_.refs_6_
  69.8 4.4 %collective-permute-done.12.refs_1_.refs_5_ = bf16[128,768]{1,0:T(8,128)(2,1)S(1)} collective-permute-done((bf16[128,768]{1,0:T(8,128)(2,1)S(1)}, bf16[128,768]{1,0:T(8,128)(2,1)S(1)}, u32[]{:S(2)}, u32[]{:S(2)}) %collective-permute-start.12) | collective-permute-done | bytes 196640 | tf_op jit(solution)/shard_map/ppermute | solution.py:34
  74.9 1.1 copy-done.21
  76.0 1.4 dispatch.1
  77.4 39.6 %all_to_all.61 = bf16[32,24,1536]{2,1,0:T(8,128)(2,1)S(1)} all-to-all(bf16[32,24,1536]{2,1,0:T(8,128)(2,1)S(1)} %bitcast.30), channel_id=1, replica_groups=mesh['y'=4,'z'=4,'c'=2,'x'=4] {'y','z','c'}, dimensions={0} | all-to-all | bytes 4718592 | tf_op jit(solution)/shard_map/all_to_all | solution.py:892
  117.1 7.6 %experts.1 = (bf16[768,1536]{1,0:T(8,128)(2,1)S(1)}, bf16[2,768,768]{2,1,0:T(8,128)(2,1)S(1)}, f32[2,768,768]{2,1,0:T(8,128)S(1)}) custom-call(bf16[768,1536]{1,0:T(8,128)(2,1)S(1)} %bitcast.26, bf16[2,768,768]{2,1,0:T(8,128)(2,1)S(1)} %copy-done.2, bf16[2,768,768]{2,1,0:T(8,128)(2,1)S(1)} %copy-done.4), custom_call_target="tpu_custom_call" | custom-call | tf_op jit(solution)/shard_map/experts/pallas_call | solution.py:654
  124.7 2.2 copy-done.6
  126.9 1.4 copy-done.8
  128.3 1.5 copy-done.68
  129.8 4.7 %all-to-all-start.2 = ((bf16[32,24,1536]{2,1,0:T(8,128)(2,1)}), bf16[32,24,1536]{2,1,0:T(8,128)(2,1)}, u32[]{:S(2)}, u32[]{:S(2)}) async-start(bf16[32,24,1536]{2,1,0:T(8,128)(2,1)} %bitcast.34), calls=%async_computation.2 | async-start | bytes 4718592 | tf_op jit(solution)/shard_map/all_to_all | solution.py:892
  134.6 1.7 copy-done.3
  136.2 1.7 copy-done.5
  137.9 12.4 %experts_back.1 = (bf16[2,768,768]{2,1,0:T(8,128)(2,1)S(1)}, bf16[2,768,768]{2,1,0:T(8,128)(2,1)S(1)}, bf16[384,768]{1,0:T(8,128)(2,1)S(1)}, bf16[384,768]{1,0:T...) custom-call(s32[1]{0:T(128)} %bitcast.7.own_ref, bf16[768,1536]{1,0:T(8,128)(2,1)S(1)} %bitcast.27, ...), custom_call_target="tpu_custom_call" | custom-call | tf_op jit(solution)/shard_map/experts_back/pallas_call | solution.py:717
  152.6 6.3 %weight_grads.1 = (f32[2,768,768]{2,1,0:T(8,128)}, f32[2,768,768]{2,1,0:T(8,128)}) custom-call(bf16[768,1536]{1,0:T(8,128)(2,1)S(1)} %bitcast.28, bf16[2,768,768]{2,1,0:T(8,128)(2,1)S(1)} %get-tuple-element.77.pre_ref, bf16[2,768,768]{2,1,0:T(8,128)(2,1)S(1)} %copy-done.69, bf16[2,768,768]{2,1,0:T(8,128)(2,1)S(1)} %get-tuple-element.79.arr_ref), custom_call_target="tpu_custom_call" | custom-call | flops 3623878656 | bytes 20000000 | tf_op jit(solution)/shard_map/weight_grads/pallas_call | solution.py:752
  158.9 6.9 %all-to-all-done.2 = bf16[32,24,1536]{2,1,0:T(8,128)(2,1)} async-done(((bf16[32,24,1536]{2,1,0:T(8,128)(2,1)}), bf16[32,24,1536]{2,1,0:T(8,128)(2,1)}, u32[]{:S(2)}, u32[]{:S(2)}) %all-to-all-start.2) | async-done | bytes 2359328 | tf_op jit(solution)/shard_map/all_to_all | solution.py:892
  165.8 2.3 copy-done.7
  170.9 4.9 %combine.1 = (bf16[128,896]{1,0:T(8,128)(2,1)S(1)}, bf16[128,896]{1,0:T(8,128)(2,1)S(1)}, bf16[128,896]{1,0:T(8,128)(2,1)S(1)}, bf16[128,896]{1,0:T(8,128)(2,1)S(1)}) custom-call(s32[2,512]{1,0:T(2,128)S(1)} %get-tuple-element.71.places_ref, s32[2,512]{1,0:T(2,128)S(1)} %get-tuple-element.58.ids_ref, bf16[64,768]{1,0:T(8,128)(2,1)S(1)} %convert_element_type.24.router_ref, ...), custom_call_target="tpu_custom_call" | custom-call | tf_op jit(solution)/shard_map/combine/pallas_call | solution.py:844
  177.9 3.5 %collective-permute-done.17.refs_3_ = bf16[384,768]{1,0:T(8,128)(2,1)} collective-permute-done((bf16[384,768]{1,0:T(8,128)(2,1)}, bf16[384,768]{1,0:T(8,128)(2,1)}, u32[]{:S(2)}, u32[]{:S(2)}) %collective-permute-start.17) | collective-permute-done | bytes 589856 | tf_op jit(solution)/shard_map/ppermute | solution.py:34
  181.5 3.2 %sum_rows.1 = bf16[512,768]{1,0:T(8,128)(2,1)} custom-call(bf16[384,768]{1,0:T(8,128)(2,1)S(1)} %copy-done.71, bf16[384,768]{1,0:T(8,128)(2,1)} %collective-permute-done.15.refs_1_, bf16[384,768]{1,0:T(8,128)(2,1)} %collective-permute-done.16.refs_2_, bf16[384,768]{1,0:T(8,128)(2,1)} %collective-permute-done.17.refs_3_, f32[2,768,768]{2,1,0:T(8,128)S(1)} %copy-done.76, ...), custom_call_target="tpu_custom_call" | custom-call | flops 20000000000 | bytes 60000000 | tf_op jit(solution)/shard_map/sum_rows/pallas_call | solution.py:793
  185.4 7.7 %all-to-all-start.3 = ((bf16[32,16,768]{2,1,0:T(8,128)(2,1)}), bf16[32,16,768]{2,1,0:T(8,128)(2,1)S(1)}, u32[]{:S(2)}, u32[]{:S(2)}) async-start(bf16[32,16,768]{2,1,0:T(8,128)(2,1)} %bitcast.14), calls=%async_computation.3 | async-start | bytes 1572864 | tf_op jit(solution)/shard_map/all_to_all | solution.py:892
  193.5 1.1 collective-permute-start.20
  194.7 5.7 %collective-permute-done.18.refs_1_ = bf16[128,896]{1,0:T(8,128)(2,1)S(1)} collective-permute-done((bf16[128,896]{1,0:T(8,128)(2,1)}, bf16[128,896]{1,0:T(8,128)(2,1)S(1)}, u32[]{:S(2)}, u32[]{:S(2)}) %collective-permute-start.18) | collective-permute-done | bytes 229408 | tf_op jit(solution)/shard_map/ppermute | solution.py:34
  202.6 5.1 %collective-permute-done.20.refs_3_ = bf16[128,896]{1,0:T(8,128)(2,1)S(1)} collective-permute-done((bf16[128,896]{1,0:T(8,128)(2,1)S(1)}, bf16[128,896]{1,0:T(8,128)(2,1)S(1)}, u32[]{:S(2)}, u32[]{:S(2)}) %collective-permute-start.20) | collective-permute-done | bytes 229408 | tf_op jit(solution)/shard_map/ppermute | solution.py:34
  208.4 1.3 copy-done.12
  209.7 1.3 copy-done.14
  211.0 1.3 copy-done.16
  212.2 1.1 copy-done.19
  220.8 11.0 %backward.1 = (bf16[128,768]{1,0:T(8,128)(2,1)}, f32[128,768]{1,0:T(8,128)}, bf16[1536,896]{1,0:T(8,128)(2,1)S(1)}, bf16[1536,896]{1,0:T(8,128)(2,1)S(1)}) custom-call(s32[2]{0:T(128)S(1)} %copy-done.63, bf16[128,768]{1,0:T(8,128)(2,1)S(1)} %copy-done.24, bf16[128,768]{1,0:T(8,128)(2,1)S(1)} %copy-done.28, ...), custom_call_target="tpu_custom_call" | custom-call | tf_op jit(solution)/shard_map/backward/pallas_call | solution.py:443
  232.5 4.7 %collective-permute-done.21 = bf16[1536,896]{1,0:T(8,128)(2,1)S(1)} collective-permute-done((bf16[1536,896]{1,0:T(8,128)(2,1)S(1)}, bf16[1536,896]{1,0:T(8,128)(2,1)S(1)}, u32[]{:S(2)}, u32[]{:S(2)}) %collective-permute-start.21) | collective-permute-done | bytes 2752544 | tf_op jit(solution)/shard_map/ppermute | solution.py:42
  238.0 44.4 %all_to_all.62 = bf16[64,24,896]{2,1,0:T(8,128)(2,1)S(1)} all-to-all(bf16[64,24,896]{2,1,0:T(8,128)(2,1)S(1)} %bitcast.37), channel_id=1, replica_groups=mesh['y'=4,'z'=4,'c'=2,'x'=4] {'y','x','z'}, dimensions={0} | all-to-all | bytes 5505024 | tf_op jit(solution)/shard_map/all_to_all | solution.py:966
  282.8 13.1 %all_to_all.63 = bf16[16,24,896]{2,1,0:T(8,128)(2,1)S(1)} all-to-all(bf16[16,24,896]{2,1,0:T(8,128)(2,1)S(1)} %broadcast_in_dim.15), channel_id=1, replica_groups=mesh['y'=4,'z'=4,'c'=2,'x'=4] {'y','z'}, dimensions={0} | all-to-all | bytes 1376256 | tf_op jit(solution)/shard_map/all_to_all | solution.py:968
  295.9 3.5 %collective-permute-start.22 = (bf16[384,896]{1,0:T(8,128)(2,1)S(1)}, bf16[384,896]{1,0:T(8,128)(2,1)S(1)}, u32[]{:S(2)}, u32[]{:S(2)}) collective-permute-start(bf16[384,896]{1,0:T(8,128)(2,1)S(1)} %bitcast.32), channel_id=1, source_target_pairs={{0,4},{4,0},{1,5},{5,1},{2,6},{6,2},{3,7},{7,3},{8,12},{12,8},{9,1... | collective-permute-start | bytes 2064392 | tf_op jit(solution)/shard_map/ppermute | solution.py:42
  299.4 1.8 collective-permute-done.22.other_ref
  301.2 1.5 finish.1
  (194 shorter events, 43.2 us)
Async XLA Ops:
  5.3 13.4 %collective-permute-start.2 = (bf16[160,768]{1,0:T(8,128)(2,1)S(1)}, bf16[160,768]{1,0:T(8,128)(2,1)S(1)}, u32[]{:S(2)}, u32[]{:S(2)}) collective-permute-start(bf16[160,768]{1,0:T(8,128)(2,1)S(1)} %line.1.refs_0_.refs_4_.refs_3_), channel_id=1, source_target_pairs={{0,3},{1,0},{2,1},{3,2},{4,7},{5,4},{6,5},{7,6},{8,11},{9,8},{10,9... | collective-permute-start | bytes 737288 | tf_op jit(solution)/shard_map/ppermute | solution.py:34
  8.7 10.1 %collective-permute-start.1 = (bf16[160,768]{1,0:T(8,128)(2,1)S(1)}, bf16[160,768]{1,0:T(8,128)(2,1)S(1)}, u32[]{:S(2)}, u32[]{:S(2)}) collective-permute-start(bf16[160,768]{1,0:T(8,128)(2,1)S(1)} %line.1.refs_0_.refs_4_.refs_3_), channel_id=1, source_target_pairs={{0,2},{1,3},{2,0},{3,1},{4,6},{5,7},{6,4},{7,5},{8,10},{9,11},{10,... | collective-permute-start | bytes 737288 | tf_op jit(solution)/shard_map/ppermute | solution.py:34
  9.2 15.4 %collective-permute-start = (bf16[160,768]{1,0:T(8,128)(2,1)S(1)}, bf16[160,768]{1,0:T(8,128)(2,1)S(1)}, u32[]{:S(2)}, u32[]{:S(2)}) collective-permute-start(bf16[160,768]{1,0:T(8,128)(2,1)S(1)} %line.1.refs_0_.refs_4_.refs_3_), channel_id=1, source_target_pairs={{0,1},{1,2},{2,3},{3,0},{4,5},{5,6},{6,7},{7,4},{8,9},{9,10},{10,1... | collective-permute-start | bytes 737288 | tf_op jit(solution)/shard_map/ppermute | solution.py:34
  13.3 28.4 %collective-permute-start.5 = (bf16[288,768]{1,0:T(8,128)(2,1)S(1)}, bf16[288,768]{1,0:T(8,128)(2,1)}, u32[]{:S(2)}, u32[]{:S(2)}) collective-permute-start(bf16[288,768]{1,0:T(8,128)(2,1)S(1)} %pack.1), channel_id=1, source_target_pairs={{0,3},{1,0},{2,1},{3,2},{4,7},{5,4},{6,5},{7,6},{8,11},{9,8},{10,9... | collective-permute-start | bytes 1327112 | tf_op jit(solution)/shard_map/ppermute | solution.py:34
  15.4 26.6 %collective-permute-start.4 = (bf16[288,768]{1,0:T(8,128)(2,1)S(1)}, bf16[288,768]{1,0:T(8,128)(2,1)}, u32[]{:S(2)}, u32[]{:S(2)}) collective-permute-start(bf16[288,768]{1,0:T(8,128)(2,1)S(1)} %pack.1), channel_id=1, source_target_pairs={{0,2},{1,3},{2,0},{3,1},{4,6},{5,7},{6,4},{7,5},{8,10},{9,11},{10,... | collective-permute-start | bytes 1327112 | tf_op jit(solution)/shard_map/ppermute | solution.py:34
  18.6 37.3 %copy-start.62 = (s32[2]{0:T(128)}, s32[2]{0:T(128)S(1)}, u32[]{:S(2)}) copy-start(s32[2]{0:T(128)S(1)} %pad_add_fusion.place_ref) | copy-start | bytes 28
  18.7 8.5 %copy-start.37 = (bf16[160,768]{1,0:T(8,128)(2,1)}, bf16[160,768]{1,0:T(8,128)(2,1)S(1)}, u32[]{:S(2)}) copy-start(bf16[160,768]{1,0:T(8,128)(2,1)S(1)} %collective-permute-done.2.refs_3_) | copy-start | bytes 737284
  18.7 24.8 %collective-permute-start.3 = (bf16[288,768]{1,0:T(8,128)(2,1)S(1)}, bf16[288,768]{1,0:T(8,128)(2,1)}, u32[]{:S(2)}, u32[]{:S(2)}) collective-permute-start(bf16[288,768]{1,0:T(8,128)(2,1)S(1)} %pack.1), channel_id=1, source_target_pairs={{0,1},{1,2},{2,3},{3,0},{4,5},{5,6},{6,7},{7,4},{8,9},{9,10},{10,1... | collective-permute-start | bytes 1327112 | tf_op jit(solution)/shard_map/ppermute | solution.py:34
  31.1 24.8 %collective-permute-start.11 = (bf16[192,768]{1,0:T(8,128)(2,1)}, bf16[192,768]{1,0:T(8,128)(2,1)}, u32[]{:S(2)}, u32[]{:S(2)}) collective-permute-start(bf16[192,768]{1,0:T(8,128)(2,1)} %hold_back.1), channel_id=1, source_target_pairs={{0,3},{1,0},{2,1},{3,2},{4,7},{5,4},{6,5},{7,6},{8,11},{9,8},{10,9... | collective-permute-start | bytes 884744 | tf_op jit(solution)/shard_map/ppermute | solution.py:34
  31.1 24.8 %collective-permute-start.10 = (bf16[192,768]{1,0:T(8,128)(2,1)}, bf16[192,768]{1,0:T(8,128)(2,1)}, u32[]{:S(2)}, u32[]{:S(2)}) collective-permute-start(bf16[192,768]{1,0:T(8,128)(2,1)} %hold_back.1), channel_id=1, source_target_pairs={{0,2},{1,3},{2,0},{3,1},{4,6},{5,7},{6,4},{7,5},{8,10},{9,11},{10,... | collective-permute-start | bytes 884744 | tf_op jit(solution)/shard_map/ppermute | solution.py:34
  31.7 43.2 %all-to-all-start = ((bf16[32,24,1664]{2,1,0:T(8,128)(2,1)}), bf16[32,24,1664]{2,1,0:T(8,128)(2,1)S(1)}, u32[]{:S(2)}, u32[]{:S(2)}) async-start(bf16[32,24,1664]{2,1,0:T(8,128)(2,1)} %bitcast.29), calls=%async_computation | async-start | bytes 5111808 | tf_op jit(solution)/shard_map/all_to_all | solution.py:892
  41.7 2.9 collective-permute-start.8
  42.0 2.7 collective-permute-start.7
  43.5 2.4 collective-permute-start.6
  44.6 11.3 %collective-permute-start.9 = (bf16[192,768]{1,0:T(8,128)(2,1)S(1)}, bf16[192,768]{1,0:T(8,128)(2,1)S(1)}, u32[]{:S(2)}, u32[]{:S(2)}) collective-permute-start(bf16[192,768]{1,0:T(8,128)(2,1)S(1)} %copy-done.77), channel_id=1, source_target_pairs={{0,1},{1,2},{2,3},{3,0},{4,5},{5,6},{6,7},{7,4},{8,9},{9,10},{10,1... | collective-permute-start | bytes 884744 | tf_op jit(solution)/shard_map/ppermute | solution.py:34
  45.9 10.0 %copy-start.17 = (bf16[192,768]{1,0:T(8,128)(2,1)S(1)}, bf16[192,768]{1,0:T(8,128)(2,1)}, u32[]{:S(2)}) copy-start(bf16[192,768]{1,0:T(8,128)(2,1)} %refs_0_.5) | copy-start | bytes 884740
  55.9 13.9 %copy-start.18 = (f32[12,128,128]{2,1,0:T(8,128)}, f32[12,128,128]{2,1,0:T(8,128)S(1)}, u32[]{:S(2)}) copy-start(f32[12,128,128]{2,1,0:T(8,128)S(1)} %get-tuple-element.69.probs_ref) | copy-start | bytes 2359300
  55.9 13.9 %copy-start.25 = (bf16[128,768]{1,0:T(8,128)(2,1)}, bf16[128,768]{1,0:T(8,128)(2,1)S(1)}, u32[]{:S(2)}) copy-start(bf16[128,768]{1,0:T(8,128)(2,1)S(1)} %get-tuple-element.61.attended_ref) | copy-start | bytes 589828
  55.9 13.9 %copy-start.53 = (bf16[128,768]{1,0:T(8,128)(2,1)}, bf16[128,768]{1,0:T(8,128)(2,1)S(1)}, u32[]{:S(2)}) copy-start(bf16[128,768]{1,0:T(8,128)(2,1)S(1)} %get-tuple-element.65.hidden_ref) | copy-start | bytes 589828
  55.9 13.9 %copy-start.55 = (bf16[128,768]{1,0:T(8,128)(2,1)}, bf16[128,768]{1,0:T(8,128)(2,1)S(1)}, u32[]{:S(2)}) copy-start(bf16[128,768]{1,0:T(8,128)(2,1)S(1)} %get-tuple-element.66.q_ref) | copy-start | bytes 589828
  55.9 13.9 %copy-start.57 = (bf16[128,768]{1,0:T(8,128)(2,1)}, bf16[128,768]{1,0:T(8,128)(2,1)S(1)}, u32[]{:S(2)}) copy-start(bf16[128,768]{1,0:T(8,128)(2,1)S(1)} %get-tuple-element.67.k_ref) | copy-start | bytes 589828
  60.0 7.0 %collective-permute-start.14 = (bf16[128,768]{1,0:T(8,128)(2,1)S(1)}, bf16[128,768]{1,0:T(8,128)(2,1)S(1)}, u32[]{:S(2)}, u32[]{:S(2)}) collective-permute-start(bf16[128,768]{1,0:T(8,128)(2,1)S(1)} %get-tuple-element.64.refs_0_.refs_4_.moe_ref), channel_id=1, source_target_pairs={{0,3},{1,0},{2,1},{3,2},{4,7},{5,4},{6,5},{7,6},{8,11},{9,8},{10,9... | collective-permute-start | bytes 589832 | tf_op jit(solution)/shard_map/ppermute | solution.py:34
  62.3 7.5 %collective-permute-start.13 = (bf16[128,768]{1,0:T(8,128)(2,1)S(1)}, bf16[128,768]{1,0:T(8,128)(2,1)S(1)}, u32[]{:S(2)}, u32[]{:S(2)}) collective-permute-start(bf16[128,768]{1,0:T(8,128)(2,1)S(1)} %get-tuple-element.64.refs_0_.refs_4_.moe_ref), channel_id=1, source_target_pairs={{0,2},{1,3},{2,0},{3,1},{4,6},{5,7},{6,4},{7,5},{8,10},{9,11},{10,... | collective-permute-start | bytes 589832 | tf_op jit(solution)/shard_map/ppermute | solution.py:34
  62.3 11.9 %collective-permute-start.12 = (bf16[128,768]{1,0:T(8,128)(2,1)S(1)}, bf16[128,768]{1,0:T(8,128)(2,1)S(1)}, u32[]{:S(2)}, u32[]{:S(2)}) collective-permute-start(bf16[128,768]{1,0:T(8,128)(2,1)S(1)} %get-tuple-element.64.refs_0_.refs_4_.moe_ref), channel_id=1, source_target_pairs={{0,1},{1,2},{2,3},{3,0},{4,5},{5,6},{6,7},{7,4},{8,9},{9,10},{10,1... | collective-permute-start | bytes 589832 | tf_op jit(solution)/shard_map/ppermute | solution.py:34
  77.4 39.7 %copy-start.2 = (bf16[2,768,768]{2,1,0:T(8,128)(2,1)S(1)}, bf16[2,768,768]{2,1,0:T(8,128)(2,1)}, u32[]{:S(2)}) copy-start(bf16[2,768,768]{2,1,0:T(8,128)(2,1)} %in_ref.3) | copy-start | bytes 7077892
  77.4 39.6 %copy-start.4 = (bf16[2,768,768]{2,1,0:T(8,128)(2,1)S(1)}, bf16[2,768,768]{2,1,0:T(8,128)(2,1)}, u32[]{:S(2)}) copy-start(bf16[2,768,768]{2,1,0:T(8,128)(2,1)} %out_ref.3) | copy-start | bytes 7077892
  129.8 36.0 %all-to-all-start.2 = ((bf16[32,24,1536]{2,1,0:T(8,128)(2,1)}), bf16[32,24,1536]{2,1,0:T(8,128)(2,1)}, u32[]{:S(2)}, u32[]{:S(2)}) async-start(bf16[32,24,1536]{2,1,0:T(8,128)(2,1)} %bitcast.34), calls=%async_computation.2 | async-start | bytes 4718592 | tf_op jit(solution)/shard_map/all_to_all | solution.py:892
  137.9 14.7 %copy-start.69 = (bf16[2,768,768]{2,1,0:T(8,128)(2,1)S(1)}, bf16[2,768,768]{2,1,0:T(8,128)(2,1)}, u32[]{:S(2)}) copy-start(bf16[2,768,768]{2,1,0:T(8,128)(2,1)} %copy-done.68) | copy-start | bytes 7077892
  151.1 26.8 %collective-permute-start.15 = (bf16[384,768]{1,0:T(8,128)(2,1)}, bf16[384,768]{1,0:T(8,128)(2,1)}, u32[]{:S(2)}, u32[]{:S(2)}) collective-permute-start(bf16[384,768]{1,0:T(8,128)(2,1)} %get-tuple-element.74), channel_id=1, source_target_pairs={{0,3},{1,0},{2,1},{3,2},{4,7},{5,4},{6,5},{7,6},{8,11},{9,8},{10,9... | collective-permute-start | bytes 1769480 | tf_op jit(solution)/shard_map/ppermute | solution.py:34
  151.7 26.2 %collective-permute-start.16 = (bf16[384,768]{1,0:T(8,128)(2,1)}, bf16[384,768]{1,0:T(8,128)(2,1)}, u32[]{:S(2)}, u32[]{:S(2)}) collective-permute-start(bf16[384,768]{1,0:T(8,128)(2,1)} %get-tuple-element.75), channel_id=1, source_target_pairs={{0,2},{1,3},{2,0},{3,1},{4,6},{5,7},{6,4},{7,5},{8,10},{9,11},{10,... | collective-permute-start | bytes 1769480 | tf_op jit(solution)/shard_map/ppermute | solution.py:34
  151.7 29.7 %collective-permute-start.17 = (bf16[384,768]{1,0:T(8,128)(2,1)}, bf16[384,768]{1,0:T(8,128)(2,1)}, u32[]{:S(2)}, u32[]{:S(2)}) collective-permute-start(bf16[384,768]{1,0:T(8,128)(2,1)} %get-tuple-element.76), channel_id=1, source_target_pairs={{0,1},{1,2},{2,3},{3,0},{4,5},{5,6},{6,7},{7,4},{8,9},{9,10},{10,1... | collective-permute-start | bytes 1769480 | tf_op jit(solution)/shard_map/ppermute | solution.py:34
  152.6 13.2 %copy-start.38 = (bf16[160,768]{1,0:T(8,128)(2,1)S(1)}, bf16[160,768]{1,0:T(8,128)(2,1)}, u32[]{:S(2)}) copy-start(bf16[160,768]{1,0:T(8,128)(2,1)} %copy-done.37) | copy-start | bytes 737284
  170.9 10.5 %copy-start.71 = (bf16[384,768]{1,0:T(8,128)(2,1)S(1)}, bf16[384,768]{1,0:T(8,128)(2,1)}, u32[]{:S(2)}) copy-start(bf16[384,768]{1,0:T(8,128)(2,1)} %copy-done.70) | copy-start | bytes 1769476
  170.9 10.5 %copy-start.76 = (f32[2,768,768]{2,1,0:T(8,128)S(1)}, f32[2,768,768]{2,1,0:T(8,128)}, u32[]{:S(2)}) copy-start(f32[2,768,768]{2,1,0:T(8,128)} %get-tuple-element.56.refs_4_) | copy-start | bytes 14155780
  181.4 12.1 %copy-start.73 = (bf16[128,896]{1,0:T(8,128)(2,1)S(1)}, bf16[128,896]{1,0:T(8,128)(2,1)}, u32[]{:S(2)}) copy-start(bf16[128,896]{1,0:T(8,128)(2,1)} %copy-done.72) | copy-start | bytes 688132
  181.4 26.9 %copy-start.24 = (bf16[128,768]{1,0:T(8,128)(2,1)S(1)}, bf16[128,768]{1,0:T(8,128)(2,1)}, u32[]{:S(2)}) copy-start(bf16[128,768]{1,0:T(8,128)(2,1)} %tokens_ref.5) | copy-start | bytes 589828
  181.4 26.9 %copy-start.26 = (bf16[128,768]{1,0:T(8,128)(2,1)S(1)}, bf16[128,768]{1,0:T(8,128)(2,1)}, u32[]{:S(2)}) copy-start(bf16[128,768]{1,0:T(8,128)(2,1)} %copy-done.25) | copy-start | bytes 589828
  181.5 26.9 %copy-start.28 = (bf16[128,768]{1,0:T(8,128)(2,1)S(1)}, bf16[128,768]{1,0:T(8,128)(2,1)}, u32[]{:S(2)}) copy-start(bf16[128,768]{1,0:T(8,128)(2,1)} %cotangent_ref.3) | copy-start | bytes 589828
  181.5 26.9 %copy-start.30 = (f32[128,768]{1,0:T(8,128)S(1)}, f32[128,768]{1,0:T(8,128)}, u32[]{:S(2)}) copy-start(f32[128,768]{1,0:T(8,128)} %copy-done.29) | copy-start | bytes 1179652
  181.5 26.9 %copy-start.63 = (s32[2]{0:T(128)S(1)}, s32[2]{0:T(128)}, u32[]{:S(2)}) copy-start(s32[2]{0:T(128)} %copy-done.62) | copy-start | bytes 28
  181.5 26.9 %copy-start.67 = (s32[2,128]{1,0:T(2,128)S(1)}, s32[2,128]{1,0:T(2,128)}, u32[]{:S(2)}) copy-start(s32[2,128]{1,0:T(2,128)} %copy-done.66) | copy-start | bytes 3076
  185.4 23.1 %copy-start.10 = (bf16[768,768]{1,0:T(8,128)(2,1)S(1)}, bf16[768,768]{1,0:T(8,128)(2,1)}, u32[]{:S(2)}) copy-start(bf16[768,768]{1,0:T(8,128)(2,1)} %copy-done.9) | copy-start | bytes 3538948
  185.4 23.0 %all-to-all-start.3 = ((bf16[32,16,768]{2,1,0:T(8,128)(2,1)}), bf16[32,16,768]{2,1,0:T(8,128)(2,1)S(1)}, u32[]{:S(2)}, u32[]{:S(2)}) async-start(bf16[32,16,768]{2,1,0:T(8,128)(2,1)} %bitcast.14), calls=%async_computation.3 | async-start | bytes 1572864 | tf_op jit(solution)/shard_map/all_to_all | solution.py:892
  193.1 7.3 %collective-permute-start.18 = (bf16[128,896]{1,0:T(8,128)(2,1)}, bf16[128,896]{1,0:T(8,128)(2,1)S(1)}, u32[]{:S(2)}, u32[]{:S(2)}) collective-permute-start(bf16[128,896]{1,0:T(8,128)(2,1)} %copy-done.75), channel_id=1, source_target_pairs={{0,3},{1,0},{2,1},{3,2},{4,7},{5,4},{6,5},{7,6},{8,11},{9,8},{10,9... | collective-permute-start | bytes 688136 | tf_op jit(solution)/shard_map/ppermute | solution.py:34
  193.5 8.4 %collective-permute-start.19 = (bf16[128,896]{1,0:T(8,128)(2,1)}, bf16[128,896]{1,0:T(8,128)(2,1)S(1)}, u32[]{:S(2)}, u32[]{:S(2)}) collective-permute-start(bf16[128,896]{1,0:T(8,128)(2,1)} %copy-done.74), channel_id=1, source_target_pairs={{0,2},{1,3},{2,0},{3,1},{4,6},{5,7},{6,4},{7,5},{8,10},{9,11},{10,... | collective-permute-start | bytes 688136 | tf_op jit(solution)/shard_map/ppermute | solution.py:34
  193.5 14.2 %collective-permute-start.20 = (bf16[128,896]{1,0:T(8,128)(2,1)S(1)}, bf16[128,896]{1,0:T(8,128)(2,1)S(1)}, u32[]{:S(2)}, u32[]{:S(2)}) collective-permute-start(bf16[128,896]{1,0:T(8,128)(2,1)S(1)} %copy-done.73), channel_id=1, source_target_pairs={{0,1},{1,2},{2,3},{3,0},{4,5},{5,6},{6,7},{7,4},{8,9},{9,10},{10,1... | collective-permute-start | bytes 688136 | tf_op jit(solution)/shard_map/ppermute | solution.py:34
  231.9 5.3 %collective-permute-start.21 = (bf16[1536,896]{1,0:T(8,128)(2,1)S(1)}, bf16[1536,896]{1,0:T(8,128)(2,1)S(1)}, u32[]{:S(2)}, u32[]{:S(2)}) collective-permute-start(bf16[1536,896]{1,0:T(8,128)(2,1)S(1)} %get-tuple-element.94), channel_id=1, source_target_pairs={{0,4},{4,0},{1,5},{5,1},{2,6},{6,2},{3,7},{7,3},{8,12},{12,8},{9,1... | collective-permute-start | bytes 8257544 | tf_op jit(solution)/shard_map/ppermute | solution.py:42
  295.9 5.2 %collective-permute-start.22 = (bf16[384,896]{1,0:T(8,128)(2,1)S(1)}, bf16[384,896]{1,0:T(8,128)(2,1)S(1)}, u32[]{:S(2)}, u32[]{:S(2)}) collective-permute-start(bf16[384,896]{1,0:T(8,128)(2,1)S(1)} %bitcast.32), channel_id=1, source_target_pairs={{0,4},{4,0},{1,5},{5,1},{2,6},{6,2},{3,7},{7,3},{8,12},{12,8},{9,1... | collective-permute-start | bytes 2064392 | tf_op jit(solution)/shard_map/ppermute | solution.py:42
  (56 other events, 89.8 us)
